TPU v7x, 32 devices: a whole 2x2x4 slice. The times are simulated.
32 devices in a mesh: gx: 2 (over x), gy: 16 (over z, y, core).
Axes of the slice: x: 2, y: 2, z: 4, core: 2. Of those that a mesh axis runs over, the one named last changes fastest.
Arguments:
- vectors: bfloat16 [8192, 32, 128], P(('gx', 'gy')), may hold values from -6 to 6
- coupling_table: bfloat16 [5, 16, 128, 128], replicated, may hold values from -0.375 to 0.375
- factor_index: int32 [8192, 5, 2], P(('gx', 'gy')), may hold values from 0 to 15
- level_order: int32 [5], replicated, may hold values from 0 to 4, each once
Outputs:
- applied: bfloat16 [8192, 32, 128], P(('gx', 'gy'))
Inputs may be any that keep to these rules, and one draw needn't show every extreme that they name: `factor_index`: table entries of the coupling matrices. `level_order`: each level slot appears once.
All inputs are finite; a program needn't handle non-finite values.
Results may differ from a plain program's by a relative error of at most 0.0086.
Values may be sent and summed in bfloat16 or wider, within the bound.
No kernel may reach another device: no remote copies, remote signals or barrier semaphores. Data moves between devices by JAX's collectives and lax.ppermute only.
A program may use at most 64 MiB of HBM per device.

v0:
```python
import math

import jax
import jax.numpy as jnp
from jax import lax
from jax.sharding import PartitionSpec as P


def partner_2(array, axis, distance):
    return lax.ppermute(array, axis, [(i, i ^ 1 << distance) for i in range(lax.axis_size(axis))])


def body(vectors, coupling_table, factor_index, level_order):
    middle_bits = lax.axis_size("gy").bit_length() - 1
    high_bits = lax.axis_size("gx").bit_length() - 1

    def apply_level(field, partner, indices, position):
        level_slot = level_order[position]
        level_table = lax.dynamic_index_in_dim(coupling_table, level_slot, 0, keepdims=False)
        chosen = lax.dynamic_index_in_dim(indices, level_slot, 1, keepdims=False)
        block_total = field.shape[0]
        group_size = math.gcd(block_total, 64)
        group_total = block_total // group_size

        def one_group(operands):
            own_blocks, other_blocks, selected = operands
            first = jnp.take(level_table, selected[:, 0], axis=0)
            second = jnp.take(level_table, selected[:, 1], axis=0)
            local_part = jnp.einsum(
                "bnj,bij->bni", own_blocks, first, preferred_element_type=jnp.float32
            )
            remote_part = jnp.einsum(
                "bnj,bij->bni", other_blocks, second, preferred_element_type=jnp.float32
            )
            return (local_part + remote_part).astype(jnp.bfloat16)

        result = lax.map(
            one_group,
            (
                field.reshape((group_total, group_size) + field.shape[1:]),
                partner.reshape((group_total, group_size) + partner.shape[1:]),
                chosen.reshape(group_total, group_size, 2),
            ),
        )
        return result.reshape(field.shape)

    field = vectors
    for offset in range(middle_bits):
        partner = partner_2(field, "gy", offset)
        field = apply_level(field, partner, factor_index, offset)
    for offset in range(high_bits):
        partner = partner_2(field, "gx", offset)
        field = apply_level(field, partner, factor_index, middle_bits + offset)
    return field


def solution(mesh):
    placed = (P(("gx", "gy"), None, None), P(), P(("gx", "gy"), None, None), P())
    return jax.shard_map(
        body, mesh=mesh, in_specs=placed, out_specs=P(("gx", "gy"), None, None), check_vma=False
    )
```

profile of v0, /device:TPU:0, one launch (start us, length us, event | category | flops | bytes accessed | tf_op | source)
XLA Modules:
  0.0 468.4 jit_solution(13250754589427925499)
XLA Ops:
  15.9 49.5 %while.50 = (s32[]{:T(128)}, bf16[4,64,32,128]{3,2,1,0:T(8,128)(2,1)}, bf16[4,64,32,128]{3,2,1,0:T(8,128)(2,1)}, s32[4,64,2]{1,0,2:T(4,128)S(1)}, bf16[16,128,12...) while((s32[]{:T(128)}, bf16[4,64,32,128]{3,2,1,0:T(8,128)(2,1)}, ...), condition=%wide.region_1.3_spmd, body=%wide.region_0.2_spmd.sunk | while | flops 136841984 | bytes 16266065 | solution.py:37
  18.0 4.0 fusion.175
  24.2 4.1 fusion.176
  30.4 4.0 fusion.175
  36.5 4.1 fusion.176
  42.8 4.0 fusion.175
  48.9 4.1 fusion.176
  55.2 4.0 fusion.175
  61.3 4.1 fusion.176
  65.4 2.5 collective-permute-start.1
  68.0 46.5 %collective-permute-done.1 = bf16[256,32,128]{2,1,0:T(8,128)(2,1)} collective-permute-done((bf16[256,32,128]{2,1,0:T(8,128)(2,1)}, bf16[256,32,128]{2,1,0:T(8,128)(2,1)}, u32[]{:S(2)}, u32[]{:S(2)}) %collective-permute-start.1) | collective-permute-done | bytes 2097184 | tf_op jit(solution)/shard_map/ppermute | solution.py:10
  116.2 45.0 %while.51 = (s32[]{:T(128)}, bf16[4,64,32,128]{3,2,1,0:T(8,128)(2,1)}, bf16[4,64,32,128]{3,2,1,0:T(8,128)(2,1)}, s32[4,64,2]{1,0,2:T(4,128)S(1)}, bf16[16,128,12...) while((s32[]{:T(128)}, bf16[4,64,32,128]{3,2,1,0:T(8,128)(2,1)}, ...), condition=%wide.region_3.5_spmd, body=%wide.region_2.4_spmd.sunk | while | flops 136841984 | bytes 16266065 | solution.py:37
  116.2 2.2 gather_fusion.2
  118.3 3.0 fusion.181
  121.4 2.2 gather_fusion.3
  123.6 3.8 fusion.182
  127.4 2.2 gather_fusion.2
  129.6 3.0 fusion.181
  132.6 2.2 gather_fusion.3
  134.8 3.8 fusion.182
  138.7 2.2 gather_fusion.2
  140.8 3.0 fusion.181
  143.9 2.2 gather_fusion.3
  146.0 3.8 fusion.182
  149.9 2.2 gather_fusion.2
  152.1 3.0 fusion.181
  155.1 2.2 gather_fusion.3
  157.3 3.8 fusion.182
  163.0 45.9 %collective-permute-done.2 = bf16[256,32,128]{2,1,0:T(8,128)(2,1)} collective-permute-done((bf16[256,32,128]{2,1,0:T(8,128)(2,1)}, bf16[256,32,128]{2,1,0:T(8,128)(2,1)}, u32[]{:S(2)}, u32[]{:S(2)}) %collective-permute-start.2) | collective-permute-done | bytes 2097184 | tf_op jit(solution)/shard_map/ppermute | solution.py:10
  210.5 45.0 %while.52 = (s32[]{:T(128)}, bf16[4,64,32,128]{3,2,1,0:T(8,128)(2,1)}, bf16[4,64,32,128]{3,2,1,0:T(8,128)(2,1)}, s32[4,64,2]{1,0,2:T(4,128)S(1)}, bf16[16,128,12...) while((s32[]{:T(128)}, bf16[4,64,32,128]{3,2,1,0:T(8,128)(2,1)}, ...), condition=%wide.region_5.7_spmd, body=%wide.region_4.6_spmd.sunk | while | flops 136841984 | bytes 16266065 | solution.py:37
  210.6 2.2 gather_fusion.4
  212.7 3.0 fusion.187
  215.8 2.2 gather_fusion.5
  217.9 3.8 fusion.188
  224.0 3.0 fusion.187
  227.0 2.2 gather_fusion.5
  229.2 3.8 fusion.188
  235.2 3.0 fusion.187
  238.2 2.2 gather_fusion.5
  240.4 3.8 fusion.188
  246.5 3.0 fusion.187
  249.5 2.2 gather_fusion.5
  251.7 3.8 fusion.188
  255.5 2.6 collective-permute-start.3
  258.2 90.1 %collective-permute-done.3 = bf16[256,32,128]{2,1,0:T(8,128)(2,1)} collective-permute-done((bf16[256,32,128]{2,1,0:T(8,128)(2,1)}, bf16[256,32,128]{2,1,0:T(8,128)(2,1)}, u32[]{:S(2)}, u32[]{:S(2)}) %collective-permute-start.3) | collective-permute-done | bytes 2097184 | tf_op jit(solution)/shard_map/ppermute | solution.py:10
  349.9 34.9 %while.53 = (s32[]{:T(128)}, bf16[4,64,32,128]{3,2,1,0:T(8,128)(2,1)}, bf16[4,64,32,128]{3,2,1,0:T(8,128)(2,1)}, s32[4,64,2]{1,0,2:T(4,128)S(1)}, bf16[16,128,12...) while((s32[]{:T(128)}, bf16[4,64,32,128]{3,2,1,0:T(8,128)(2,1)}, ...), condition=%wide.region_7.9_spmd, body=%wide.region_6.8_spmd.sunk | while | flops 136841984 | bytes 16266065 | solution.py:37
  350.9 3.3 fusion.193
  355.1 3.5 fusion.194
  359.6 3.3 fusion.193
  363.9 3.5 fusion.194
  368.3 3.3 fusion.193
  372.6 3.5 fusion.194
  377.1 3.3 fusion.193
  381.3 3.5 fusion.194
  386.2 45.6 %collective-permute-done.4 = bf16[256,32,128]{2,1,0:T(8,128)(2,1)} collective-permute-done((bf16[256,32,128]{2,1,0:T(8,128)(2,1)}, bf16[256,32,128]{2,1,0:T(8,128)(2,1)}, u32[]{:S(2)}, u32[]{:S(2)}) %collective-permute-start.4) | collective-permute-done | bytes 2097184 | tf_op jit(solution)/shard_map/ppermute | solution.py:10
  433.5 34.9 %while.54 = (s32[]{:T(128)}, bf16[4,64,32,128]{3,2,1,0:T(8,128)(2,1)}, bf16[4,64,32,128]{3,2,1,0:T(8,128)(2,1)}, s32[4,64,2]{1,0,2:T(4,128)S(1)}, bf16[16,128,12...) while((s32[]{:T(128)}, bf16[4,64,32,128]{3,2,1,0:T(8,128)(2,1)}, ...), condition=%wide.region_9.11_spmd, body=%wide.region_8.10_spmd.sunk | while | flops 136841984 | bytes 16266065 | solution.py:37
  434.4 3.3 fusion.199
  438.7 3.5 fusion.200
  443.2 3.3 fusion.199
  447.5 3.5 fusion.200
  451.9 3.3 fusion.199
  456.2 3.5 fusion.200
  460.7 3.3 fusion.199
  464.9 3.5 fusion.200
  (104 shorter events, 55.3 us)
Async XLA Ops:
  0.0 14.2 %collective-permute-start = (bf16[256,32,128]{2,1,0:T(8,128)(2,1)}, bf16[256,32,128]{2,1,0:T(8,128)(2,1)}, u32[]{:S(2)}, u32[]{:S(2)}) collective-permute-start(bf16[256,32,128]{2,1,0:T(8,128)(2,1)} %param.16), channel_id=1, source_target_pairs={{0,1},{1,0},{2,3},{3,2},{4,5},{5,4},{6,7},{7,6},{8,9},{9,8},{10,11... | collective-permute-start | bytes 6291464 | tf_op jit(solution)/shard_map/ppermute | solution.py:10
  65.4 49.1 %collective-permute-start.1 = (bf16[256,32,128]{2,1,0:T(8,128)(2,1)}, bf16[256,32,128]{2,1,0:T(8,128)(2,1)}, u32[]{:S(2)}, u32[]{:S(2)}) collective-permute-start(bf16[256,32,128]{2,1,0:T(8,128)(2,1)} %bitcast.171), channel_id=1, source_target_pairs={{0,2},{1,3},{2,0},{3,1},{4,6},{5,7},{6,4},{7,5},{8,10},{9,11},{10,... | collective-permute-start | bytes 6291464 | tf_op jit(solution)/shard_map/ppermute | solution.py:10
  161.1 47.8 %collective-permute-start.2 = (bf16[256,32,128]{2,1,0:T(8,128)(2,1)}, bf16[256,32,128]{2,1,0:T(8,128)(2,1)}, u32[]{:S(2)}, u32[]{:S(2)}) collective-permute-start(bf16[256,32,128]{2,1,0:T(8,128)(2,1)} %bitcast.172), channel_id=1, source_target_pairs={{0,4},{1,5},{2,6},{3,7},{4,0},{5,1},{6,2},{7,3},{8,12},{9,13},{10,... | collective-permute-start | bytes 6291464 | tf_op jit(solution)/shard_map/ppermute | solution.py:10
  255.5 92.8 %collective-permute-start.3 = (bf16[256,32,128]{2,1,0:T(8,128)(2,1)}, bf16[256,32,128]{2,1,0:T(8,128)(2,1)}, u32[]{:S(2)}, u32[]{:S(2)}) collective-permute-start(bf16[256,32,128]{2,1,0:T(8,128)(2,1)} %bitcast.173), channel_id=1, source_target_pairs={{0,8},{1,9},{2,10},{3,11},{4,12},{5,13},{6,14},{7,15},{8,0},{9,1},... | collective-permute-start | bytes 6291464 | tf_op jit(solution)/shard_map/ppermute | solution.py:10
  384.8 47.0 %collective-permute-start.4 = (bf16[256,32,128]{2,1,0:T(8,128)(2,1)}, bf16[256,32,128]{2,1,0:T(8,128)(2,1)}, u32[]{:S(2)}, u32[]{:S(2)}) collective-permute-start(bf16[256,32,128]{2,1,0:T(8,128)(2,1)} %bitcast.174), channel_id=1, source_target_pairs={{0,16},{16,0},{1,17},{17,1},{2,18},{18,2},{3,19},{19,3},{4,20},{20... | collective-permute-start | bytes 6291464 | tf_op jit(solution)/shard_map/ppermute | solution.py:10
where the time goes:
time: 470 us; the launch traced here: 468 us
  waiting for transfers between devices  228 us (49%)
  matrix products  142 us (30%)
  local copies, waits for them, and re-layouts  79.7 us (17%)
  between operations  9.53 us (2%)
  starting transfers between devices  8.66 us (2%)
    ppermute x5, waiting for transfers between devices, partner_2(): lax.ppermute(array, axis, [(i, i ^ 1 << distance) for i in range(lax.axis...  228 us
    dot_general x20, matrix products, one_group(): jnp.einsum('bnj,bij->bni', own_blocks, first, preferred_element_type=jnp....  74.8 us
    dot_general x20, matrix products, one_group(): jnp.einsum('bnj,bij->bni', other_blocks, second, preferred_element_type=j...  66.9 us
    gather x20, local copies, waits for them, and re-layouts, one_group(): first = jnp.take(level_table, selected[:, 0], axis=0)  33.4 us
    gather x20, local copies, waits for them, and re-layouts, one_group(): second = jnp.take(level_table, selected[:, 1], axis=0)  33.4 us
  transfers between devices with their start and end apart: 5, of which 4 were waited for; matrix products, arithmetic and copies ran while one was open for 1% of the time, Pallas kernels for 0%

commit v1 on v0

v1 whole, which is shorter than its diff:
```python
import functools
import math

import jax
import jax.numpy as jnp
from jax import lax
from jax.experimental import pallas as pl
from jax.experimental.pallas import tpu as pltpu
from jax.sharding import PartitionSpec as P

AXES = ("gx", "gy")
LOAD_FACTOR = 7
PACK_PARAMS = pltpu.CompilerParams(vmem_limit_bytes=58 * 1024 * 1024)
PARAMS = pltpu.CompilerParams(vmem_limit_bytes=24 * 1024 * 1024)


def all_levels_kernel(offset, rhs, order_ref, index_ref, field_ref, table_ref, out_ref, even, odd, in_sems, out_sem):
    devices, rows, rank = out_ref.shape
    share = rows // rhs
    levels = order_ref.shape[0]
    pairs = devices // 2
    group = min(pairs, 1 << (48 // share).bit_length() - 1)
    part = min(group, 8)

    def arrival(p):
        some = pl.ds(p * 2 * part, 2 * part)
        return pltpu.make_async_copy(
            field_ref.at[some, pl.ds(rhs * offset, rows)], even.at[some], in_sems.at[p]
        )

    for p in range(pairs // part):
        arrival(p).start()

    for level in range(levels):
        source, target = ((even, odd), (odd, even))[level % 2]
        slot = order_ref[level]

        def entries(d, j):
            at = ((offset + j) * levels + slot) * 2
            return table_ref[slot, index_ref[d, at]], table_ref[slot, index_ref[d, at + 1]]

        def one_group(step, carry):
            for k in range(group):
                if level == 0 and k % part == 0:
                    arrival(step * (group // part) + k // part).wait()
                pair = step * group + k
                low = ((pair >> level) << (level + 1)) | (pair & ((1 << level) - 1))
                high = low + (1 << level)
                for j in range(share):
                    block = pl.ds(rhs * j, rhs)
                    both = jnp.concatenate([source[low, block], source[high, block]], axis=1)
                    low_own, low_other = entries(low, j)
                    high_own, high_other = entries(high, j)
                    coupling = jnp.concatenate(
                        [jnp.concatenate([low_own, low_other], axis=0), jnp.concatenate([high_other, high_own], axis=0)],
                        axis=1,
                    )
                    product = jnp.dot(both, coupling, preferred_element_type=jnp.float32).astype(jnp.bfloat16)
                    target[low, block] = product[:, :rank]
                    target[high, block] = product[:, rank:]
                if level == levels - 1 and k % part == part - 1:
                    for first in (pair - part + 1, pairs + pair - part + 1):
                        done = pl.ds(first, part)
                        pltpu.make_async_copy(target.at[done], out_ref.at[done], out_sem).start()
            return carry

        lax.fori_loop(0, pairs // group, one_group, 0)
    last = (even, odd)[levels % 2]
    pltpu.make_async_copy(last, out_ref, out_sem).wait()


def apply_all_levels(payload, offset, share, rhs, table, index, order):
    devices, _, rank = payload.shape
    levels = table.shape[0]
    shape = (devices, share * rhs, rank)
    blocks = devices * share
    return pl.pallas_call(
        functools.partial(all_levels_kernel, offset, rhs),
        grid_spec=pltpu.PrefetchScalarGridSpec(
            num_scalar_prefetch=2,
            grid=(),
            in_specs=[pl.BlockSpec(memory_space=pltpu.HBM), pl.BlockSpec(memory_space=pltpu.VMEM)],
            out_specs=pl.BlockSpec(memory_space=pltpu.HBM),
            scratch_shapes=[pltpu.VMEM(shape, jnp.bfloat16)] * 2
            + [pltpu.SemaphoreType.DMA((devices // 2,)), pltpu.SemaphoreType.DMA],
        ),
        out_shape=jax.ShapeDtypeStruct(shape, jnp.bfloat16),
        compiler_params=PARAMS,
        cost_estimate=pl.CostEstimate(
            flops=LOAD_FACTOR * levels * blocks * 4 * rhs * rank * rank,
            bytes_accessed=2 * (2 * blocks * rhs * rank + table.size),
            transcendentals=0,
        ),
    )(order, index, payload, table)


def pack_kernel(units, vectors_ref, index_ref, out_ref, held, in_sems, out_sems):
    devices, rows, rank = out_ref.shape
    rhs = vectors_ref.shape[1]
    levels, _, blocks = index_ref.shape
    used = units * rhs
    parts = in_sems.shape[0]
    size = devices // parts
    source = vectors_ref.at[pl.ds(0, devices * units)].reshape(devices, used, rank)
    inward = [
        pltpu.make_async_copy(
            source.at[pl.ds(p * size, size)], held.at[pl.ds(p * size, size), pl.ds(0, used)], in_sems.at[p]
        )
        for p in range(parts)
    ]
    for copy in inward:
        copy.start()

    def pick(shape, condition):
        first, second = (lax.broadcasted_iota(jnp.int32, shape, dim) for dim in (0, 1))
        return condition(first, second).astype(jnp.float32).astype(jnp.bfloat16)

    def product(left, right, contract):
        return lax.dot_general(left, right, ((contract[:1], contract[1:]), ((), ())), preferred_element_type=jnp.float32)

    width = -(-2 * levels // 16) * 16
    entries = jnp.zeros((width, blocks), jnp.float32)
    for slot in range(levels):
        spot = pick((width, 2), lambda r, t: r == 2 * slot + t)
        entries += product(spot, index_ref[slot].astype(jnp.float32).astype(jnp.bfloat16), (1, 0))
    entries = entries.astype(jnp.bfloat16)
    lanes = jnp.zeros((devices, rank), jnp.float32)
    for unit in range(units):
        chosen = product(pick((devices, blocks), lambda d, b: b == d * units + unit), entries, (1, 1))
        spot = pick((width, rank), lambda r, lane: (lane == unit * 2 * levels + r) & (r < 2 * levels))
        lanes += product(chosen.astype(jnp.bfloat16), spot, (1, 0))
    for d in range(devices):
        held[d, pl.ds(used, rows - used)] = jnp.broadcast_to(lanes[d : d + 1], (rows - used, rank)).astype(jnp.bfloat16)

    outward = [
        pltpu.make_async_copy(held.at[pl.ds(p * size, size)], out_ref.at[pl.ds(p * size, size)], out_sems.at[p])
        for p in range(parts)
    ]
    for arrival, departure in zip(inward, outward):
        arrival.wait()
        departure.start()
    for copy in outward:
        copy.wait()


def pack(vectors, factor_index, devices, units):
    blocks, rhs, rank = vectors.shape
    levels = factor_index.shape[1]
    assert units * levels * 2 <= rank
    shape = (devices, units * rhs + 8, rank)
    parts = 8
    return pl.pallas_call(
        functools.partial(pack_kernel, units),
        in_specs=[pl.BlockSpec(memory_space=pltpu.HBM), pl.BlockSpec(memory_space=pltpu.VMEM)],
        out_specs=pl.BlockSpec(memory_space=pltpu.HBM),
        out_shape=jax.ShapeDtypeStruct(shape, jnp.bfloat16),
        scratch_shapes=[pltpu.VMEM(shape, jnp.bfloat16)] + [pltpu.SemaphoreType.DMA((parts,))] * 2,
        compiler_params=PACK_PARAMS,
        cost_estimate=pl.CostEstimate(flops=0, bytes_accessed=4 * vectors.size, transcendentals=0),
    )(vectors, jnp.transpose(factor_index, (1, 2, 0)))


def one_level_kernel(level, order_ref, index_ref, own_ref, other_ref, table_ref, out_ref):
    levels = order_ref.shape[0]
    slot = order_ref[level]

    def one_block(b, carry):
        at = (b * levels + slot) * 2
        both = jnp.concatenate([own_ref[b], other_ref[b]], axis=1)
        coupling = jnp.concatenate([table_ref[slot, index_ref[at]], table_ref[slot, index_ref[at + 1]]], axis=0)
        out_ref[b] = jnp.dot(both, coupling, preferred_element_type=jnp.float32).astype(jnp.bfloat16)
        return carry

    lax.fori_loop(0, own_ref.shape[0], one_block, 0, unroll=16)


def apply_level(own, other, table, index, order, level):
    blocks, rhs, rank = own.shape
    return pl.pallas_call(
        functools.partial(one_level_kernel, level),
        grid_spec=pltpu.PrefetchScalarGridSpec(
            num_scalar_prefetch=2,
            grid=(),
            in_specs=[pl.BlockSpec(memory_space=pltpu.VMEM)] * 3,
            out_specs=pl.BlockSpec(memory_space=pltpu.VMEM),
        ),
        out_shape=jax.ShapeDtypeStruct(own.shape, jnp.bfloat16),
        compiler_params=PARAMS,
        cost_estimate=pl.CostEstimate(
            flops=LOAD_FACTOR * blocks * 4 * rhs * rank * rank,
            bytes_accessed=2 * (3 * own.size + table.size),
            transcendentals=0,
        ),
    )(order, index, own, other, table)


def place_kernel(shares, starts, aliased, *refs):
    count = len(shares)
    pieces = refs[aliased : aliased + count]
    out_ref = refs[aliased + count]
    held = refs[aliased + count + 1 : aliased + 2 * count + 1]
    in_sems, out_sems = refs[aliased + 2 * count + 1 :]
    moves = []
    for c, (piece, share, (first, units)) in enumerate(zip(pieces, shares, starts)):
        groups = piece.shape[0]
        target = out_ref.at[pl.ds(first[0], groups * units)].reshape((groups, units) + out_ref.shape[1:])
        parts = 4 if groups % 4 == 0 else 1
        for p in range(parts):
            some = pl.ds(p * (groups // parts), groups // parts)
            at = len(moves)
            moves.append((
                pltpu.make_async_copy(piece.at[some], held[c].at[some], in_sems.at[at]),
                pltpu.make_async_copy(
                    held[c].at[some], target.at[some, pl.ds(first[1], share)], out_sems.at[at]
                ),
            ))
    for inward, _ in moves:
        inward.start()
    for inward, outward in moves:
        inward.wait()
        outward.start()
    for _, outward in moves:
        outward.wait()


def place(result, shape, pieces, starts):
    aliased = int(result is not None)
    operands = ([result] if aliased else []) + pieces
    return pl.pallas_call(
        functools.partial(place_kernel, [p.shape[1] for p in pieces], starts, aliased),
        in_specs=[pl.BlockSpec(memory_space=pltpu.HBM)] * len(operands),
        out_specs=pl.BlockSpec(memory_space=pltpu.HBM),
        out_shape=jax.ShapeDtypeStruct(shape, jnp.bfloat16),
        scratch_shapes=[pltpu.VMEM(p.shape, jnp.bfloat16) for p in pieces]
        + [pltpu.SemaphoreType.DMA((4 * len(pieces),))] * 2,
        input_output_aliases={0: 0} if aliased else {},
        compiler_params=PARAMS,
        cost_estimate=pl.CostEstimate(
            flops=0, bytes_accessed=4 * sum(p.size for p in pieces), transcendentals=0
        ),
    )(*operands)


def body(vectors, coupling_table, factor_index, level_order):
    devices = lax.axis_size("gx") * lax.axis_size("gy")
    middle_bits = lax.axis_size("gy").bit_length() - 1
    levels = coupling_table.shape[0]
    blocks, rhs, rank = vectors.shape
    units = blocks // devices
    far_units = units - units // 8
    first = (far_units + 1) // 4
    shares = [first, far_units - first] if first else [far_units]
    starts = [sum(shares[:c]) for c in range(len(shares) + 1)]
    spread = devices * far_units

    def exchange(array):
        return lax.all_to_all(array, AXES, split_axis=0, concat_axis=0, tiled=True)

    def partner(array, level):
        axis, bit = ("gy", level) if level < middle_bits else ("gx", level - middle_bits)
        return lax.ppermute(array, axis, [(i, i ^ 1 << bit) for i in range(lax.axis_size(axis))])

    def near_level(near, level):
        return apply_level(near, partner(near, level), table, near_index, level_order, level)

    arrived = exchange(pack(vectors, factor_index, devices, far_units))
    table = jnp.swapaxes(coupling_table, 2, 3)

    near = vectors[spread:]
    near_index = factor_index[spread:].reshape(-1)
    if units > far_units:
        for level in range(middle_bits - 1):
            near = near_level(near, level)
        arrived, near = lax.optimization_barrier((arrived, near))
    index = arrived[:, far_units * rhs].astype(jnp.int32)

    done = []
    other = None
    for c, share in enumerate(shares):
        if c == 1:
            other = partner(near, middle_bits - 1)
            arrived, other = lax.optimization_barrier((arrived, other))
        far = apply_all_levels(arrived, starts[c], share, rhs, table, index, level_order)
        done.append(exchange(far).reshape(devices, share, rhs, rank))
    if units == far_units:
        return jnp.concatenate(done, axis=1).reshape(vectors.shape)
    if other is None:
        other = partner(near, middle_bits - 1)
    near = apply_level(near, other, table, near_index, level_order, middle_bits - 1)
    for level in range(middle_bits, levels):
        near = near_level(near, level)
    at = [((0, start), far_units) for start in starts]
    near_at = ((spread, 0), blocks - spread)
    result = place(None, vectors.shape, done[:-1] + [near[None]], at[: len(done) - 1] + [near_at])
    return place(result, vectors.shape, done[-1:], at[len(done) - 1 : len(done)])


def solution(mesh):
    placed = (P(AXES, None, None), P(), P(AXES, None, None), P())
    return jax.shard_map(
        body, mesh=mesh, in_specs=placed, out_specs=P(AXES, None, None), check_vma=False
    )
```

time: 470 us -> 123 us (0.26)
  waiting for transfers between devices: 228 us -> 64.2 us
  matrix products: 142 us -> 0 us
  local copies, waits for them, and re-layouts: 79.7 us -> 6.42 us
  Pallas kernels: 0 us -> 31.3 us
  starting transfers between devices: 8.66 us -> 19.6 us
  between operations: 9.53 us -> 0.18 us
    ppermute x5, waiting for transfers between devices: 228 us -> 44.5 us  [partner(): lax.ppermute(array, axis, [(i, i ^ 1 << bit) for i in range(lax.axis_size...]
    dot_general x40 -> x0, matrix products: 142 us -> none  [the longest x20 74.8 us: one_group(): jnp.einsum('bnj,bij->bni', own_blocks, first, preferred_element_type=jnp....]
    gather x40 -> x0, local copies, waits for them, and re-layouts: 66.8 us -> none  [the longest x20 33.4 us: one_group(): first = jnp.take(level_table, selected[:, 0], axis=0)]
    pallas_call x0 -> x10, Pallas kernels: none -> 31.3 us  [the longest x2 17.8 us: apply_all_levels(): pl.pallas_call(functools.partial(all_levels_kernel, offset, rhs), grid_sp...]
    all_to_all x0 -> x3, waiting for transfers between devices: none -> 19.7 us  [exchange(): return lax.all_to_all(array, AXES, split_axis=0, concat_axis=0, tiled=True)]
    all_to_all x0 -> x3, starting transfers between devices: none -> 14.7 us  [exchange(): return lax.all_to_all(array, AXES, split_axis=0, concat_axis=0, tiled=True)]
    another operation x5 -> x0, local copies, waits for them, and re-layouts: 8.17 us -> none
    unnamed x0 -> x9, local copies, waits for them, and re-layouts: none -> 5.1 us
  transfers between devices with their start and end apart: 5 -> 8, of which waited for: 4 -> 7; matrix products, arithmetic and copies ran while one was open for 1% -> 4% of each run, Pallas kernels for 0% -> 21%
where the time goes in v1:
time: 123 us
  waiting for transfers between devices  64.2 us (52%)
  Pallas kernels  31.3 us (25%)
  starting transfers between devices  19.6 us (16%)
  local copies, waits for them, and re-layouts  6.42 us (5%)
    ppermute x5, waiting for transfers between devices, partner(): lax.ppermute(array, axis, [(i, i ^ 1 << bit) for i in range(lax.axis_size...  44.5 us
    all_to_all x3, waiting for transfers between devices, exchange(): return lax.all_to_all(array, AXES, split_axis=0, concat_axis=0, tiled=True)  19.7 us
    pallas_call x2, Pallas kernels, apply_all_levels(): pl.pallas_call(functools.partial(all_levels_kernel, offset, rhs), grid_sp...  17.8 us
    all_to_all x3, starting transfers between devices, exchange(): return lax.all_to_all(array, AXES, split_axis=0, concat_axis=0, tiled=True)  14.7 us
    pallas_call x5, Pallas kernels, apply_level(): pl.pallas_call(functools.partial(one_level_kernel, level), grid_spec=pltp...  6.55 us
    unnamed x9, local copies, waits for them, and re-layouts  5.1 us
    ppermute x5, starting transfers between devices, partner(): lax.ppermute(array, axis, [(i, i ^ 1 << bit) for i in range(lax.axis_size...  4.91 us
    pallas_call x2, Pallas kernels, place(): pl.pallas_call(functools.partial(place_kernel, [p.shape[1] for p in piece...  3.8 us
  transfers between devices with their start and end apart: 8, of which 7 were waited for; matrix products, arithmetic and copies ran while one was open for 4% of the time, Pallas kernels for 21%

profile of v1, /device:TPU:0, one launch (start us, length us, event | category | flops | bytes accessed | tf_op | source)
XLA Modules:
  0.0 122.5 jit_solution(11799255039591763548)
XLA Ops:
  0.0 3.1 %shard_map.46 = bf16[32,232,128]{2,1,0:T(8,128)(2,1)} custom-call(bf16[256,32,128]{2,1,0:T(8,128)(2,1)} %vectors_ref.1, s32[5,2,256]{2,1,0:T(2,128)} %bitcast.17), custom_call_target="tpu_custom_call" | custom-call | bytes 4194304 | tf_op jit(solution)/shard_map/pallas_call | solution.py:152
  3.1 0.0 copy-start.3
  3.1 7.4 %all-to-all-start = ((bf16[32,232,128]{2,1,0:T(8,128)(2,1)}), bf16[32,232,128]{2,1,0:T(8,128)(2,1)}, u32[]{:S(2)}, u32[]{:S(2)}) async-start(bf16[32,232,128]{2,1,0:T(8,128)(2,1)} %shard_map.46), calls=%async_computation | async-start | bytes 3801088 | tf_op jit(solution)/shard_map/all_to_all | solution.py:257
  10.6 1.0 slice.10.own_ref
  11.5 0.3 collective-permute-start
  11.8 0.0 copy-done.3
  11.8 0.1 slice.9
  11.9 0.1 copy.7
  12.0 0.1 reshape.11.index_ref
  12.2 0.0 copy-start.2
  12.2 3.2 %copy.8 = bf16[5,16,128,128]{2,3,1,0:T(8,128)(2,1)S(1)} copy(bf16[5,16,128,128]{3,2,1,0:T(8,128)(2,1)} %param.5) | data formatting | bytes 5242880 | tf_op args[1]
  15.4 0.0 collective-permute-done.other_ref
  15.4 0.0 copy-done.2
  15.4 1.1 shard_map.47.own_ref
  16.6 1.7 %collective-permute-start.1 = (bf16[32,32,128]{2,1,0:T(8,128)(2,1)S(1)}, bf16[32,32,128]{2,1,0:T(8,128)(2,1)S(1)}, u32[]{:S(2)}, u32[]{:S(2)}) collective-permute-start(bf16[32,32,128]{2,1,0:T(8,128)(2,1)S(1)} %shard_map.47.own_ref), channel_id=1, source_target_pairs={{0,2},{1,3},{2,0},{3,1},{4,6},{5,7},{6,4},{7,5},{8,10},{9,11},{10,... | collective-permute-start | bytes 786440 | tf_op jit(solution)/shard_map/ppermute | solution.py:261
  18.3 14.6 %collective-permute-done.1.other_ref = bf16[32,32,128]{2,1,0:T(8,128)(2,1)S(1)} collective-permute-done((bf16[32,32,128]{2,1,0:T(8,128)(2,1)S(1)}, bf16[32,32,128]{2,1,0:T(8,128)(2,1)S(1)}, u32[]{:S(2)}, u32[]{:S(2)}) %collective-permute-start.1) | collective-permute-done | bytes 262176 | tf_op jit(solution)/shard_map/ppermute | solution.py:261
  32.9 1.1 shard_map.48.own_ref
  34.1 1.2 collective-permute-start.2
  35.3 13.0 %collective-permute-done.2.other_ref = bf16[32,32,128]{2,1,0:T(8,128)(2,1)S(1)} collective-permute-done((bf16[32,32,128]{2,1,0:T(8,128)(2,1)S(1)}, bf16[32,32,128]{2,1,0:T(8,128)(2,1)S(1)}, u32[]{:S(2)}, u32[]{:S(2)}) %collective-permute-start.2) | collective-permute-done | bytes 262176 | tf_op jit(solution)/shard_map/ppermute | solution.py:261
  48.3 1.1 shard_map.49.own_ref
  49.4 7.0 %all-to-all-done.field_ref = bf16[32,232,128]{2,1,0:T(8,128)(2,1)} async-done(((bf16[32,232,128]{2,1,0:T(8,128)(2,1)}), bf16[32,232,128]{2,1,0:T(8,128)(2,1)}, u32[]{:S(2)}, u32[]{:S(2)}) %all-to-all-start) | async-done | bytes 1900576 | tf_op jit(solution)/shard_map/all_to_all | solution.py:257
  56.4 0.9 slice_convert_fusion
  57.2 0.1 collective-permute-start.3
  57.3 6.4 %shard_map.50 = bf16[32,64,128]{2,1,0:T(8,128)(2,1)S(1)} custom-call(s32[5]{0:T(128)S(1)} %copy-done.2, s32[32,128]{1,0:T(8,128)S(1)} %bitcast.15, bf16[32,232,128]{2,1,0:T(8,128)(2,1)} %all-to-all-done.field_ref, bf16[5,16,128,128]{3,2,1,0:T(8,128)(2,1)S(1)} %bitcast.9), custom_call_target="tpu_custom_call" | custom-call | flops 4697620480 | bytes 3670016 | tf_op jit(solution)/shard_map/pallas_call | solution.py:77
  63.7 0.0 copy-start.1
  63.7 0.8 copy-done.1
  64.5 3.9 %all-to-all-start.1 = ((bf16[32,64,128]{2,1,0:T(8,128)(2,1)}), bf16[32,64,128]{2,1,0:T(8,128)(2,1)S(1)}, u32[]{:S(2)}, u32[]{:S(2)}) async-start(bf16[32,64,128]{2,1,0:T(8,128)(2,1)} %copy-done.1), calls=%async_computation.1 | async-start | bytes 1048576 | tf_op jit(solution)/shard_map/all_to_all | solution.py:257
  68.4 1.8 %collective-permute-done.3.other_ref = bf16[32,32,128]{2,1,0:T(8,128)(2,1)} collective-permute-done((bf16[32,32,128]{2,1,0:T(8,128)(2,1)S(1)}, bf16[32,32,128]{2,1,0:T(8,128)(2,1)}, u32[]{:S(2)}, u32[]{:S(2)}) %collective-permute-start.3) | collective-permute-done | bytes 262176 | tf_op jit(solution)/shard_map/ppermute | solution.py:261
  70.2 11.4 %shard_map.54 = bf16[32,160,128]{2,1,0:T(8,128)(2,1)S(1)} custom-call(s32[5]{0:T(128)S(1)} %copy-done.2, s32[32,128]{1,0:T(8,128)S(1)} %bitcast.16, bf16[32,232,128]{2,1,0:T(8,128)(2,1)} %all-to-all-done.field_ref, bf16[5,16,128,128]{3,2,1,0:T(8,128)(2,1)S(1)} %bitcast.10), custom_call_target="tpu_custom_call" | custom-call | flops 11744051200 | bytes 5242880 | tf_op jit(solution)/shard_map/pallas_call | solution.py:77
  81.6 0.0 copy-start
  81.6 1.0 copy-done
  82.7 1.6 %all-to-all-done.1 = bf16[32,64,128]{2,1,0:T(8,128)(2,1)S(1)} async-done(((bf16[32,64,128]{2,1,0:T(8,128)(2,1)}), bf16[32,64,128]{2,1,0:T(8,128)(2,1)S(1)}, u32[]{:S(2)}, u32[]{:S(2)}) %all-to-all-start.1) | async-done | bytes 524320 | tf_op jit(solution)/shard_map/all_to_all | solution.py:257
  84.3 3.4 %all-to-all-start.2 = ((bf16[32,160,128]{2,1,0:T(8,128)(2,1)}), bf16[32,160,128]{2,1,0:T(8,128)(2,1)}, u32[]{:S(2)}, u32[]{:S(2)}) async-start(bf16[32,160,128]{2,1,0:T(8,128)(2,1)} %copy-done), calls=%async_computation.2 | async-start | bytes 2621440 | tf_op jit(solution)/shard_map/all_to_all | solution.py:257
  87.7 2.1 %shard_map.51.own_ref = bf16[32,32,128]{2,1,0:T(8,128)(2,1)S(1)} custom-call(s32[5]{0:T(128)S(1)} %copy-done.2, s32[320]{0:T(512)S(1)} %reshape.11.index_ref, bf16[32,32,128]{2,1,0:T(8,128)(2,1)S(1)} %shard_map.49.own_ref, bf16[32,32,128]{2,1,0:T(8,128)(2,1)} %collective-permute-done.3.other_ref, bf16[5,16,128,128]{3,2,1,0:T(8,128)(2,1)S(1)} %bitcast.11), custom_call_target="tpu_custom_call" | custom-call | flops 469762048 | bytes 3407872 | tf_op jit(solution)/shard_map/pallas_call | solution.py:179
  89.7 1.6 %collective-permute-start.4 = (bf16[32,32,128]{2,1,0:T(8,128)(2,1)S(1)}, bf16[32,32,128]{2,1,0:T(8,128)(2,1)S(1)}, u32[]{:S(2)}, u32[]{:S(2)}) collective-permute-start(bf16[32,32,128]{2,1,0:T(8,128)(2,1)S(1)} %shard_map.51.own_ref), channel_id=1, source_target_pairs={{0,16},{16,0},{1,17},{17,1},{2,18},{18,2},{3,19},{19,3},{4,20},{20... | collective-permute-start | bytes 786440 | tf_op jit(solution)/shard_map/ppermute | solution.py:261
  91.4 15.1 %collective-permute-done.4.other_ref = bf16[32,32,128]{2,1,0:T(8,128)(2,1)S(1)} collective-permute-done((bf16[32,32,128]{2,1,0:T(8,128)(2,1)S(1)}, bf16[32,32,128]{2,1,0:T(8,128)(2,1)S(1)}, u32[]{:S(2)}, u32[]{:S(2)}) %collective-permute-start.4) | collective-permute-done | bytes 262176 | tf_op jit(solution)/shard_map/ppermute | solution.py:261
  106.4 1.1 shard_map.52
  107.6 1.7 %shard_map.53.refs_0_ = bf16[256,32,128]{2,1,0:T(8,128)(2,1)} custom-call(bf16[32,2,32,128]{3,2,1,0:T(8,128)(2,1)S(1)} %bitcast.13, bf16[1,32,32,128]{3,2,1,0:T(8,128)(2,1)S(1)} %bitcast.14), custom_call_target="tpu_custom_call" | custom-call | bytes 1572864 | tf_op jit(solution)/shard_map/pallas_call | solution.py:229
  109.3 11.1 %all-to-all-done.2 = bf16[32,160,128]{2,1,0:T(8,128)(2,1)} async-done(((bf16[32,160,128]{2,1,0:T(8,128)(2,1)}), bf16[32,160,128]{2,1,0:T(8,128)(2,1)}, u32[]{:S(2)}, u32[]{:S(2)}) %all-to-all-start.2) | async-done | bytes 1310752 | tf_op jit(solution)/shard_map/all_to_all | solution.py:257
  120.4 2.1 %shard_map.55 = bf16[256,32,128]{2,1,0:T(8,128)(2,1)} custom-call(bf16[256,32,128]{2,1,0:T(8,128)(2,1)} %shard_map.53.refs_0_, bf16[32,5,32,128]{3,2,1,0:T(8,128)(2,1)} %bitcast.5.refs_1_), custom_call_target="tpu_custom_call", output_to_operand_aliasing={{}: (0, {})} | custom-call | bytes 2621440 | tf_op jit(solution)/shard_map/pallas_call | solution.py:229
Async XLA Ops:
  3.1 8.7 %copy-start.3 = (s32[256,5,2]{0,2,1:T(2,128)S(1)}, s32[256,5,2]{0,2,1:T(2,128)}, u32[]{:S(2)}) copy-start(s32[256,5,2]{0,2,1:T(2,128)} %param.6) | copy-start | bytes 30724
  3.1 53.2 %all-to-all-start = ((bf16[32,232,128]{2,1,0:T(8,128)(2,1)}), bf16[32,232,128]{2,1,0:T(8,128)(2,1)}, u32[]{:S(2)}, u32[]{:S(2)}) async-start(bf16[32,232,128]{2,1,0:T(8,128)(2,1)} %shard_map.46), calls=%async_computation | async-start | bytes 3801088 | tf_op jit(solution)/shard_map/all_to_all | solution.py:257
  11.5 3.9 %collective-permute-start = (bf16[32,32,128]{2,1,0:T(8,128)(2,1)S(1)}, bf16[32,32,128]{2,1,0:T(8,128)(2,1)S(1)}, u32[]{:S(2)}, u32[]{:S(2)}) collective-permute-start(bf16[32,32,128]{2,1,0:T(8,128)(2,1)S(1)} %slice.10.own_ref), channel_id=1, source_target_pairs={{0,1},{1,0},{2,3},{3,2},{4,5},{5,4},{6,7},{7,6},{8,9},{9,8},{10,11... | collective-permute-start | bytes 786440 | tf_op jit(solution)/shard_map/ppermute | solution.py:261
  12.2 3.3 %copy-start.2 = (s32[5]{0:T(128)S(1)}, s32[5]{0:T(128)}, u32[]{:S(2)}) copy-start(s32[5]{0:T(128)} %order_ref.13) | copy-start | bytes 64
  16.6 16.4 %collective-permute-start.1 = (bf16[32,32,128]{2,1,0:T(8,128)(2,1)S(1)}, bf16[32,32,128]{2,1,0:T(8,128)(2,1)S(1)}, u32[]{:S(2)}, u32[]{:S(2)}) collective-permute-start(bf16[32,32,128]{2,1,0:T(8,128)(2,1)S(1)} %shard_map.47.own_ref), channel_id=1, source_target_pairs={{0,2},{1,3},{2,0},{3,1},{4,6},{5,7},{6,4},{7,5},{8,10},{9,11},{10,... | collective-permute-start | bytes 786440 | tf_op jit(solution)/shard_map/ppermute | solution.py:261
  34.1 14.2 %collective-permute-start.2 = (bf16[32,32,128]{2,1,0:T(8,128)(2,1)S(1)}, bf16[32,32,128]{2,1,0:T(8,128)(2,1)S(1)}, u32[]{:S(2)}, u32[]{:S(2)}) collective-permute-start(bf16[32,32,128]{2,1,0:T(8,128)(2,1)S(1)} %shard_map.48.own_ref), channel_id=1, source_target_pairs={{0,4},{1,5},{2,6},{3,7},{4,0},{5,1},{6,2},{7,3},{8,12},{9,13},{10,... | collective-permute-start | bytes 786440 | tf_op jit(solution)/shard_map/ppermute | solution.py:261
  57.2 12.9 %collective-permute-start.3 = (bf16[32,32,128]{2,1,0:T(8,128)(2,1)S(1)}, bf16[32,32,128]{2,1,0:T(8,128)(2,1)}, u32[]{:S(2)}, u32[]{:S(2)}) collective-permute-start(bf16[32,32,128]{2,1,0:T(8,128)(2,1)S(1)} %shard_map.49.own_ref), channel_id=1, source_target_pairs={{0,8},{1,9},{2,10},{3,11},{4,12},{5,13},{6,14},{7,15},{8,0},{9,1},... | collective-permute-start | bytes 786440 | tf_op jit(solution)/shard_map/ppermute | solution.py:261
  63.7 0.8 copy-start.1
  64.5 19.8 %all-to-all-start.1 = ((bf16[32,64,128]{2,1,0:T(8,128)(2,1)}), bf16[32,64,128]{2,1,0:T(8,128)(2,1)S(1)}, u32[]{:S(2)}, u32[]{:S(2)}) async-start(bf16[32,64,128]{2,1,0:T(8,128)(2,1)} %copy-done.1), calls=%async_computation.1 | async-start | bytes 1048576 | tf_op jit(solution)/shard_map/all_to_all | solution.py:257
  81.6 1.1 copy-start
  84.3 36.2 %all-to-all-start.2 = ((bf16[32,160,128]{2,1,0:T(8,128)(2,1)}), bf16[32,160,128]{2,1,0:T(8,128)(2,1)}, u32[]{:S(2)}, u32[]{:S(2)}) async-start(bf16[32,160,128]{2,1,0:T(8,128)(2,1)} %copy-done), calls=%async_computation.2 | async-start | bytes 2621440 | tf_op jit(solution)/shard_map/all_to_all | solution.py:257
  89.7 16.7 %collective-permute-start.4 = (bf16[32,32,128]{2,1,0:T(8,128)(2,1)S(1)}, bf16[32,32,128]{2,1,0:T(8,128)(2,1)S(1)}, u32[]{:S(2)}, u32[]{:S(2)}) collective-permute-start(bf16[32,32,128]{2,1,0:T(8,128)(2,1)S(1)} %shard_map.51.own_ref), channel_id=1, source_target_pairs={{0,16},{16,0},{1,17},{17,1},{2,18},{18,2},{3,19},{19,3},{4,20},{20... | collective-permute-start | bytes 786440 | tf_op jit(solution)/shard_map/ppermute | solution.py:261

commit v2 on v1

v2 whole, which is shorter than its diff:
```python
import functools
import math

import jax
import jax.numpy as jnp
from jax import lax
from jax.experimental import pallas as pl
from jax.experimental.pallas import tpu as pltpu
from jax.sharding import PartitionSpec as P

AXES = ("gx", "gy")
LOAD_FACTOR = 7
HEAVY = 50
PACK_PARAMS = pltpu.CompilerParams(vmem_limit_bytes=58 * 1024 * 1024)
PARAMS = pltpu.CompilerParams(vmem_limit_bytes=24 * 1024 * 1024)


def all_levels_kernel(order_ref, index_ref, field_ref, table_ref, out_ref, even, odd):
    devices, share, rhs, rank = out_ref.shape
    levels = order_ref.shape[0]
    for level in range(levels):
        target = out_ref if level == levels - 1 else (even, odd)[(level + 1) % 2]
        slot = order_ref[level]

        def load(d, j):
            if level == 0:
                return field_ref[d, pl.ds(rhs * j, rhs), :]
            return (even, odd)[level % 2][d, j]

        def entries(d, j):
            at = (j * levels + slot) * 2
            return table_ref[slot, index_ref[d, at]], table_ref[slot, index_ref[d, at + 1]]

        def one_pair(pair, carry):
            low = ((pair >> level) << (level + 1)) | (pair & ((1 << level) - 1))
            high = low + (1 << level)
            for j in range(share):
                both = jnp.concatenate([load(low, j), load(high, j)], axis=1)
                low_own, low_other = entries(low, j)
                high_own, high_other = entries(high, j)
                coupling = jnp.concatenate(
                    [jnp.concatenate([low_own, low_other], axis=0), jnp.concatenate([high_other, high_own], axis=0)],
                    axis=1,
                )
                product = jnp.dot(both, coupling, preferred_element_type=jnp.float32).astype(jnp.bfloat16)
                target[low, j] = product[:, :rank]
                target[high, j] = product[:, rank:]
            return carry

        lax.fori_loop(0, devices // 2, one_pair, 0, unroll=8)


def apply_all_levels(payload, share, rhs, table, index, order):
    devices, _, rank = payload.shape
    levels = table.shape[0]
    shape = (devices, share, rhs, rank)
    blocks = devices * share
    return pl.pallas_call(
        all_levels_kernel,
        grid_spec=pltpu.PrefetchScalarGridSpec(
            num_scalar_prefetch=2,
            grid=(),
            in_specs=[pl.BlockSpec(memory_space=pltpu.VMEM)] * 2,
            out_specs=pl.BlockSpec(memory_space=pltpu.VMEM),
            scratch_shapes=[pltpu.VMEM(shape, jnp.bfloat16)] * 2,
        ),
        out_shape=jax.ShapeDtypeStruct(shape, jnp.bfloat16),
        compiler_params=PARAMS,
        cost_estimate=pl.CostEstimate(
            flops=levels * blocks * 4 * rhs * rank * rank,
            bytes_accessed=2 * (2 * blocks * rhs * rank + table.size),
            transcendentals=0,
        ),
    )(order, index, payload, table)


def pack_kernel(units, vectors_ref, index_ref, out_ref, held, in_sems, out_sems):
    devices, rows, rank = out_ref.shape
    rhs = vectors_ref.shape[1]
    levels, _, blocks = index_ref.shape
    used = units * rhs
    parts = in_sems.shape[0]
    size = devices // parts
    source = vectors_ref.at[pl.ds(0, devices * units)].reshape(devices, used, rank)
    inward = [
        pltpu.make_async_copy(
            source.at[pl.ds(p * size, size)], held.at[pl.ds(p * size, size), pl.ds(0, used)], in_sems.at[p]
        )
        for p in range(parts)
    ]
    for copy in inward:
        copy.start()

    def pick(shape, condition):
        first, second = (lax.broadcasted_iota(jnp.int32, shape, dim) for dim in (0, 1))
        return condition(first, second).astype(jnp.float32).astype(jnp.bfloat16)

    def product(left, right, contract):
        return lax.dot_general(left, right, ((contract[:1], contract[1:]), ((), ())), preferred_element_type=jnp.float32)

    width = -(-2 * levels // 16) * 16
    entries = jnp.zeros((width, blocks), jnp.float32)
    for slot in range(levels):
        spot = pick((width, 2), lambda r, t: r == 2 * slot + t)
        entries += product(spot, index_ref[slot].astype(jnp.float32).astype(jnp.bfloat16), (1, 0))
    entries = entries.astype(jnp.bfloat16)
    lanes = jnp.zeros((devices, rank), jnp.float32)
    for unit in range(units):
        chosen = product(pick((devices, blocks), lambda d, b: b == d * units + unit), entries, (1, 1))
        spot = pick((width, rank), lambda r, lane: (lane == unit * 2 * levels + r) & (r < 2 * levels))
        lanes += product(chosen.astype(jnp.bfloat16), spot, (1, 0))
    for d in range(devices):
        held[d, pl.ds(used, rows - used)] = jnp.broadcast_to(lanes[d : d + 1], (rows - used, rank)).astype(jnp.bfloat16)

    outward = [
        pltpu.make_async_copy(held.at[pl.ds(p * size, size)], out_ref.at[pl.ds(p * size, size)], out_sems.at[p])
        for p in range(parts)
    ]
    for arrival, departure in zip(inward, outward):
        arrival.wait()
        departure.start()
    for copy in outward:
        copy.wait()


def pack(vectors, factor_index, devices, units):
    blocks, rhs, rank = vectors.shape
    levels = factor_index.shape[1]
    assert units * levels * 2 <= rank
    shape = (devices, units * rhs + 8, rank)
    parts = 8
    return pl.pallas_call(
        functools.partial(pack_kernel, units),
        in_specs=[pl.BlockSpec(memory_space=pltpu.HBM), pl.BlockSpec(memory_space=pltpu.VMEM)],
        out_specs=pl.BlockSpec(memory_space=pltpu.HBM),
        out_shape=jax.ShapeDtypeStruct(shape, jnp.bfloat16),
        scratch_shapes=[pltpu.VMEM(shape, jnp.bfloat16)] + [pltpu.SemaphoreType.DMA((parts,))] * 2,
        compiler_params=PACK_PARAMS,
        cost_estimate=pl.CostEstimate(flops=0, bytes_accessed=4 * vectors.size, transcendentals=0),
    )(vectors, jnp.transpose(factor_index, (1, 2, 0)))


def one_level_kernel(level, offset, order_ref, index_ref, own_ref, other_ref, table_ref, out_ref):
    levels = order_ref.shape[0]
    slot = order_ref[level]

    def one_block(b, carry):
        at = ((offset + b) * levels + slot) * 2
        both = jnp.concatenate([own_ref[b], other_ref[b]], axis=1)
        coupling = jnp.concatenate([table_ref[slot, index_ref[at]], table_ref[slot, index_ref[at + 1]]], axis=0)
        out_ref[b] = jnp.dot(both, coupling, preferred_element_type=jnp.float32).astype(jnp.bfloat16)
        return carry

    lax.fori_loop(0, own_ref.shape[0], one_block, 0, unroll=16)


def apply_level(own, other, table, index, order, level, offset=0, weight=1):
    blocks, rhs, rank = own.shape
    return pl.pallas_call(
        functools.partial(one_level_kernel, level, offset),
        grid_spec=pltpu.PrefetchScalarGridSpec(
            num_scalar_prefetch=2,
            grid=(),
            in_specs=[pl.BlockSpec(memory_space=pltpu.VMEM)] * 3,
            out_specs=pl.BlockSpec(memory_space=pltpu.VMEM),
        ),
        out_shape=jax.ShapeDtypeStruct(own.shape, jnp.bfloat16),
        compiler_params=PARAMS,
        cost_estimate=pl.CostEstimate(
            flops=weight * LOAD_FACTOR * blocks * 4 * rhs * rank * rank,
            bytes_accessed=2 * (3 * own.size + table.size),
            transcendentals=0,
        ),
    )(order, index, own, other, table)


def place_kernel(offsets, aliased, *refs):
    count = len(offsets)
    pieces = refs[aliased : aliased + count]
    out_ref = refs[aliased + count]
    held, in_sems, out_sem = refs[aliased + count + 1 :]
    total = held.shape[0]
    step = math.gcd(32, *(piece.shape[0] for piece in pieces))
    moves = []
    for piece, offset in zip(pieces, offsets):
        for first in range(0, piece.shape[0], step):
            at = len(moves) * step
            slot = held.at[pl.ds(at, step)]
            moves.append((
                pltpu.make_async_copy(piece.at[pl.ds(first, step)], slot, in_sems.at[len(moves)]),
                pltpu.make_async_copy(slot, out_ref.at[pl.ds(offset + first, step)], out_sem),
            ))
    for inward, _ in moves:
        inward.start()
    for inward, outward in moves:
        inward.wait()
        outward.start()
    pltpu.make_async_copy(held, out_ref.at[pl.ds(0, total)], out_sem).wait()


def place(result, shape, pieces, offsets):
    aliased = int(result is not None)
    operands = ([result] if aliased else []) + pieces
    total = sum(p.shape[0] for p in pieces)
    return pl.pallas_call(
        functools.partial(place_kernel, offsets, aliased),
        in_specs=[pl.BlockSpec(memory_space=pltpu.HBM)] * len(operands),
        out_specs=pl.BlockSpec(memory_space=pltpu.HBM),
        out_shape=jax.ShapeDtypeStruct(shape, jnp.bfloat16),
        scratch_shapes=[
            pltpu.VMEM((total,) + shape[1:], jnp.bfloat16),
            pltpu.SemaphoreType.DMA((total // math.gcd(32, *(p.shape[0] for p in pieces)),)),
            pltpu.SemaphoreType.DMA,
        ],
        input_output_aliases={0: 0} if aliased else {},
        compiler_params=PARAMS,
        cost_estimate=pl.CostEstimate(
            flops=0, bytes_accessed=4 * sum(p.size for p in pieces), transcendentals=0
        ),
    )(*operands)


def body(vectors, coupling_table, factor_index, level_order):
    devices = lax.axis_size("gx") * lax.axis_size("gy")
    middle_bits = lax.axis_size("gy").bit_length() - 1
    levels = coupling_table.shape[0]
    blocks, rhs, rank = vectors.shape
    units = blocks // devices
    far_units = units - units // 4
    spread = devices * far_units

    def exchange(array):
        return lax.all_to_all(array, AXES, split_axis=0, concat_axis=0, tiled=True)

    def partner(array, level):
        axis, bit = ("gy", level) if level < middle_bits else ("gx", level - middle_bits)
        return lax.ppermute(array, axis, [(i, i ^ 1 << bit) for i in range(lax.axis_size(axis))])

    def near_level(near, level, other=None, **more):
        other = partner(near, level) if other is None else other
        return apply_level(near, other, table, near_index, level_order, level, **more)

    arrived = exchange(pack(vectors, factor_index, devices, far_units))
    table = jnp.swapaxes(coupling_table, 2, 3)
    half = (blocks - spread) // 2
    last_middle = middle_bits - 1
    if units > far_units:
        near_index = factor_index[spread:].reshape(-1)
        near = near_level(vectors[spread:], 0)
        first, second = near[:half], near[half:]
        for level in range(1, last_middle):
            first = near_level(first, level)
        for level in range(1, last_middle - 1):
            second = near_level(second, level, offset=half)
        first_other = partner(first, last_middle)
        second_other = partner(second, last_middle - 1)
    index = arrived[:, far_units * rhs].astype(jnp.int32)
    far = apply_all_levels(arrived, far_units, rhs, table, index, level_order)
    if units == far_units:
        return exchange(far).reshape(vectors.shape)
    far, first_other, near_index = lax.optimization_barrier((far, first_other, near_index))
    second = near_level(second, last_middle - 1, second_other, offset=half)
    second_other = partner(second, last_middle)
    far = exchange(far).reshape(spread, rhs, rank)
    near = near_level(
        jnp.concatenate([first, second]),
        last_middle,
        jnp.concatenate([first_other, second_other]),
        weight=HEAVY,
    )
    for level in range(middle_bits, levels):
        near = near_level(near, level)
    result = place(None, vectors.shape, [near], [spread])
    return place(result, vectors.shape, [far], [0])


def solution(mesh):
    placed = (P(AXES, None, None), P(), P(AXES, None, None), P())
    return jax.shard_map(
        body, mesh=mesh, in_specs=placed, out_specs=P(AXES, None, None), check_vma=False
    )
```

time: 123 us -> 118 us (0.959)
  waiting for transfers between devices: 64.2 us -> 55.4 us
  starting transfers between devices: 19.6 us -> 24.4 us
  Pallas kernels: 31.3 us -> 28.8 us
    all_to_all x3 -> x2, waiting for transfers between devices: 19.7 us -> 8.03 us  [exchange(): return lax.all_to_all(array, AXES, split_axis=0, concat_axis=0, tiled=True)]
    ppermute x5 -> x8, starting transfers between devices: 4.91 us -> 11.4 us  [partner(): lax.ppermute(array, axis, [(i, i ^ 1 << bit) for i in range(lax.axis_size...]
    ppermute x5 -> x8, waiting for transfers between devices: 44.5 us -> 47.4 us  [partner(): lax.ppermute(array, axis, [(i, i ^ 1 << bit) for i in range(lax.axis_size...]
    pallas_call x9 -> x10, Pallas kernels: 28.1 us -> 25.8 us  [the longest x1 12.1 us: apply_all_levels(): pl.pallas_call(all_levels_kernel, grid_spec=pltpu.PrefetchScalarGridSpec(...]
    all_to_all x3 -> x2, starting transfers between devices: 14.7 us -> 13 us  [exchange(): return lax.all_to_all(array, AXES, split_axis=0, concat_axis=0, tiled=True)]
    unnamed x9 -> x11, local copies, waits for them, and re-layouts: 5.1 us -> 5 us
  transfers between devices with their start and end apart: 8 -> 10, of which waited for: 7 -> 6; matrix products, arithmetic and copies ran while one was open for 4% -> 6% of each run, Pallas kernels for 21% -> 19%
where the time goes in v2:
time: 118 us; the launch traced here: 117 us
  waiting for transfers between devices  55.4 us (47%)
  Pallas kernels  28.8 us (24%)
  starting transfers between devices  24.4 us (21%)
  local copies, waits for them, and re-layouts  6.49 us (6%)
  other arithmetic  1.9 us (2%)
    ppermute x8, waiting for transfers between devices, partner(): lax.ppermute(array, axis, [(i, i ^ 1 << bit) for i in range(lax.axis_size...  47.4 us
    all_to_all x2, starting transfers between devices, exchange(): return lax.all_to_all(array, AXES, split_axis=0, concat_axis=0, tiled=True)  13 us
    pallas_call x1, Pallas kernels, apply_all_levels(): pl.pallas_call(all_levels_kernel, grid_spec=pltpu.PrefetchScalarGridSpec(...  12.1 us
    ppermute x8, starting transfers between devices, partner(): lax.ppermute(array, axis, [(i, i ^ 1 << bit) for i in range(lax.axis_size...  11.4 us
    pallas_call x7, Pallas kernels, apply_level(): pl.pallas_call(functools.partial(one_level_kernel, level, offset), grid_s...  10.7 us
    all_to_all x2, waiting for transfers between devices, exchange(): return lax.all_to_all(array, AXES, split_axis=0, concat_axis=0, tiled=True)  8.03 us
    unnamed x11, local copies, waits for them, and re-layouts  5 us
    pallas_call x1, Pallas kernels, pack(): pl.pallas_call(functools.partial(pack_kernel, units), in_specs=[pl.BlockS...  3.01 us
  transfers between devices with their start and end apart: 10, of which 6 were waited for; matrix products, arithmetic and copies ran while one was open for 6% of the time, Pallas kernels for 19%

profile of v2, /device:TPU:0, one launch (start us, length us, event | category | flops | bytes accessed | tf_op | source)
XLA Modules:
  0.0 117.2 jit_solution(4264304806819743246)
XLA Ops:
  0.0 3.0 %shard_map.46 = bf16[32,200,128]{2,1,0:T(8,128)(2,1)} custom-call(bf16[256,32,128]{2,1,0:T(8,128)(2,1)} %vectors_ref.1, s32[5,2,256]{2,1,0:T(2,128)} %bitcast.13), custom_call_target="tpu_custom_call" | custom-call | bytes 4194304 | tf_op jit(solution)/shard_map/pallas_call | solution.py:132
  3.0 0.0 copy-start.4
  3.0 7.4 %all-to-all-start = ((bf16[32,200,128]{2,1,0:T(8,128)(2,1)}), bf16[32,200,128]{2,1,0:T(8,128)(2,1)}, u32[]{:S(2)}, u32[]{:S(2)}) async-start(bf16[32,200,128]{2,1,0:T(8,128)(2,1)} %shard_map.46), calls=%async_computation | async-start | bytes 3276800 | tf_op jit(solution)/shard_map/all_to_all | solution.py:233
  10.5 1.1 slice.17.own_ref
  11.5 0.3 collective-permute-start
  11.8 0.0 copy-done.4
  11.8 0.1 slice.16
  11.9 0.0 copy-start.3
  11.9 3.3 %copy.7 = bf16[5,16,128,128]{2,3,1,0:T(8,128)(2,1)S(1)} copy(bf16[5,16,128,128]{3,2,1,0:T(8,128)(2,1)} %param.5) | data formatting | bytes 5242880 | tf_op args[1]
  15.1 0.2 copy.8
  15.3 0.1 reshape.8.index_ref
  15.4 0.0 collective-permute-done.other_ref
  15.5 0.0 copy-done.3
  15.5 2.7 %shard_map.48 = bf16[64,32,128]{2,1,0:T(8,128)(2,1)S(1)} custom-call(s32[5]{0:T(128)S(1)} %copy-done.3, s32[640]{0:T(1024)S(1)} %reshape.8.index_ref, bf16[64,32,128]{2,1,0:T(8,128)(2,1)S(1)} %slice.17.own_ref, bf16[64,32,128]{2,1,0:T(8,128)(2,1)} %collective-permute-done.other_ref, bf16[5,16,128,128]{3,2,1,0:T(8,128)(2,1)S(1)} %bitcast.4), custom_call_target="tpu_custom_call" | custom-call | flops 939524096 | bytes 4194304 | tf_op jit(solution)/shard_map/pallas_call | solution.py:159
  18.3 1.7 %collective-permute-start.1 = (bf16[32,32,128]{2,1,0:T(8,128)(2,1)S(1)}, bf16[32,32,128]{2,1,0:T(8,128)(2,1)S(1)}, u32[]{:S(2)}, u32[]{:S(2)}) collective-permute-start(bf16[32,32,128]{2,1,0:T(8,128)(2,1)S(1)} %get-tuple-element.12.own_ref), channel_id=1, source_target_pairs={{0,2},{1,3},{2,0},{3,1},{4,6},{5,7},{6,4},{7,5},{8,10},{9,11},{10,... | collective-permute-start | bytes 786440 | tf_op jit(solution)/shard_map/ppermute | solution.py:237
  20.0 0.3 collective-permute-start.4
  20.4 11.3 %collective-permute-done.1.other_ref = bf16[32,32,128]{2,1,0:T(8,128)(2,1)S(1)} collective-permute-done((bf16[32,32,128]{2,1,0:T(8,128)(2,1)S(1)}, bf16[32,32,128]{2,1,0:T(8,128)(2,1)S(1)}, u32[]{:S(2)}, u32[]{:S(2)}) %collective-permute-start.1) | collective-permute-done | bytes 262176 | tf_op jit(solution)/shard_map/ppermute | solution.py:237
  31.7 1.1 shard_map.49.own_ref
  32.9 1.9 %collective-permute-start.2 = (bf16[32,32,128]{2,1,0:T(8,128)(2,1)S(1)}, bf16[32,32,128]{2,1,0:T(8,128)(2,1)S(1)}, u32[]{:S(2)}, u32[]{:S(2)}) collective-permute-start(bf16[32,32,128]{2,1,0:T(8,128)(2,1)S(1)} %shard_map.49.own_ref), channel_id=1, source_target_pairs={{0,4},{1,5},{2,6},{3,7},{4,0},{5,1},{6,2},{7,3},{8,12},{9,13},{10,... | collective-permute-start | bytes 786440 | tf_op jit(solution)/shard_map/ppermute | solution.py:237
  34.7 5.3 %collective-permute-done.4.other_ref = bf16[32,32,128]{2,1,0:T(8,128)(2,1)S(1)} collective-permute-done((bf16[32,32,128]{2,1,0:T(8,128)(2,1)S(1)}, bf16[32,32,128]{2,1,0:T(8,128)(2,1)S(1)}, u32[]{:S(2)}, u32[]{:S(2)}) %collective-permute-start.4) | collective-permute-done | bytes 262176 | tf_op jit(solution)/shard_map/ppermute | solution.py:237
  40.0 1.1 shard_map.51.own_ref
  41.2 2.4 %collective-permute-start.5 = (bf16[32,32,128]{2,1,0:T(8,128)(2,1)S(1)}, bf16[32,32,128]{2,1,0:T(8,128)(2,1)S(1)}, u32[]{:S(2)}, u32[]{:S(2)}) collective-permute-start(bf16[32,32,128]{2,1,0:T(8,128)(2,1)S(1)} %shard_map.51.own_ref), channel_id=1, source_target_pairs={{0,4},{1,5},{2,6},{3,7},{4,0},{5,1},{6,2},{7,3},{8,12},{9,13},{10,... | collective-permute-start | bytes 786440 | tf_op jit(solution)/shard_map/ppermute | solution.py:237
  43.6 3.7 %collective-permute-done.2.other_ref = bf16[32,32,128]{2,1,0:T(8,128)(2,1)S(1)} collective-permute-done((bf16[32,32,128]{2,1,0:T(8,128)(2,1)S(1)}, bf16[32,32,128]{2,1,0:T(8,128)(2,1)S(1)}, u32[]{:S(2)}, u32[]{:S(2)}) %collective-permute-start.2) | collective-permute-done | bytes 262176 | tf_op jit(solution)/shard_map/ppermute | solution.py:237
  47.3 1.1 shard_map.50
  48.5 2.2 %collective-permute-start.3 = (bf16[32,32,128]{2,1,0:T(8,128)(2,1)S(1)}, bf16[32,32,128]{2,1,0:T(8,128)(2,1)}, u32[]{:S(2)}, u32[]{:S(2)}) collective-permute-start(bf16[32,32,128]{2,1,0:T(8,128)(2,1)S(1)} %shard_map.50), channel_id=1, source_target_pairs={{0,8},{1,9},{2,10},{3,11},{4,12},{5,13},{6,14},{7,15},{8,0},{9,1},... | collective-permute-start | bytes 786440 | tf_op jit(solution)/shard_map/ppermute | solution.py:237
  50.7 0.0 all-to-all-done.field_ref
  50.7 0.9 slice_convert_fusion
  51.5 12.1 %shard_map.47 = bf16[32,6,32,128]{3,2,1,0:T(8,128)(2,1)S(1)} custom-call(s32[5]{0:T(128)S(1)} %copy-done.3, s32[32,128]{1,0:T(8,128)S(1)} %bitcast.12, bf16[32,200,128]{2,1,0:T(8,128)(2,1)} %all-to-all-done.field_ref, bf16[5,16,128,128]{3,2,1,0:T(8,128)(2,1)S(1)} %bitcast.8), custom_call_target="tpu_custom_call" | custom-call | flops 2013265920 | bytes 5767168 | tf_op jit(solution)/shard_map/pallas_call | solution.py:58
  63.6 0.0 copy-start
  63.6 0.0 collective-permute-done.3
  63.6 0.0 collective-permute-done.5.other_ref
  63.7 0.0 copy-start.1
  63.7 0.8 copy-done.1
  64.4 0.0 copy-start.2
  64.4 0.9 copy-done.2
  65.4 1.1 shard_map.52
  66.5 0.0 copy-done
  66.5 0.9 collective-permute-start.6
  67.4 5.5 %all-to-all-start.1 = ((bf16[32,6,32,128]{3,2,1,0:T(8,128)(2,1)}), bf16[32,6,32,128]{3,2,1,0:T(8,128)(2,1)}, u32[]{:S(2)}, u32[]{:S(2)}) async-start(bf16[32,6,32,128]{3,2,1,0:T(8,128)(2,1)} %copy-done), calls=%async_computation.1 | async-start | bytes 3145728 | tf_op jit(solution)/shard_map/all_to_all | solution.py:233
  73.0 16.3 %collective-permute-done.6 = bf16[32,32,128]{2,1,0:T(8,128)(2,1)S(1)} collective-permute-done((bf16[32,32,128]{2,1,0:T(8,128)(2,1)S(1)}, bf16[32,32,128]{2,1,0:T(8,128)(2,1)S(1)}, u32[]{:S(2)}, u32[]{:S(2)}) %collective-permute-start.6) | collective-permute-done | bytes 262176 | tf_op jit(solution)/shard_map/ppermute | solution.py:237
  89.3 1.0 pad_maximum_fusion.1.other_ref
  90.3 1.7 %shard_map.53.own_ref = bf16[64,32,128]{2,1,0:T(8,128)(2,1)S(1)} custom-call(s32[5]{0:T(128)S(1)} %copy-done.3, s32[640]{0:T(1024)S(1)} %reshape.8.index_ref, bf16[64,32,128]{2,1,0:T(8,128)(2,1)S(1)} %pad_maximum_fusion.own_ref, bf16[64,32,128]{2,1,0:T(8,128)(2,1)S(1)} %pad_maximum_fusion.1.other_ref, bf16[5,16,128,128]{3,2,1,0:T(8,128)(2,1)S(1)} %bitcast.10), custom_call_target="tpu_custom_call" | custom-call | flops 46976204800 | bytes 4194304 | tf_op jit(solution)/shard_map/pallas_call | solution.py:159
  92.1 1.7 %collective-permute-start.7 = (bf16[64,32,128]{2,1,0:T(8,128)(2,1)S(1)}, bf16[64,32,128]{2,1,0:T(8,128)(2,1)S(1)}, u32[]{:S(2)}, u32[]{:S(2)}) collective-permute-start(bf16[64,32,128]{2,1,0:T(8,128)(2,1)S(1)} %shard_map.53.own_ref), channel_id=1, source_target_pairs={{0,16},{16,0},{1,17},{17,1},{2,18},{18,2},{3,19},{19,3},{4,20},{20... | collective-permute-start | bytes 1572872 | tf_op jit(solution)/shard_map/ppermute | solution.py:237
  93.8 10.7 %collective-permute-done.7.other_ref = bf16[64,32,128]{2,1,0:T(8,128)(2,1)S(1)} collective-permute-done((bf16[64,32,128]{2,1,0:T(8,128)(2,1)S(1)}, bf16[64,32,128]{2,1,0:T(8,128)(2,1)S(1)}, u32[]{:S(2)}, u32[]{:S(2)}) %collective-permute-start.7) | collective-permute-done | bytes 524320 | tf_op jit(solution)/shard_map/ppermute | solution.py:237
  104.4 1.7 %shard_map.54.refs_0_ = bf16[64,32,128]{2,1,0:T(8,128)(2,1)S(1)} custom-call(s32[5]{0:T(128)S(1)} %copy-done.3, s32[640]{0:T(1024)S(1)} %reshape.8.index_ref, bf16[64,32,128]{2,1,0:T(8,128)(2,1)S(1)} %shard_map.53.own_ref, bf16[64,32,128]{2,1,0:T(8,128)(2,1)S(1)} %collective-permute-done.7.other_ref, bf16[5,16,128,128]{3,2,1,0:T(8,128)(2,1)S(1)} %bitcast.11), custom_call_target="tpu_custom_call" | custom-call | flops 939524096 | bytes 4194304 | tf_op jit(solution)/shard_map/pallas_call | solution.py:159
  106.2 0.9 shard_map.55.refs_0_
  107.0 8.0 %all-to-all-done.1 = bf16[32,6,32,128]{3,2,1,0:T(8,128)(2,1)} async-done(((bf16[32,6,32,128]{3,2,1,0:T(8,128)(2,1)}), bf16[32,6,32,128]{3,2,1,0:T(8,128)(2,1)}, u32[]{:S(2)}, u32[]{:S(2)}) %all-to-all-start.1) | async-done | bytes 1572896 | tf_op jit(solution)/shard_map/all_to_all | solution.py:233
  115.1 2.1 %shard_map.56 = bf16[256,32,128]{2,1,0:T(8,128)(2,1)} custom-call(bf16[256,32,128]{2,1,0:T(8,128)(2,1)} %shard_map.55.refs_0_, bf16[192,32,128]{2,1,0:T(8,128)(2,1)} %bitcast.3.refs_1_), custom_call_target="tpu_custom_call", output_to_operand_aliasing={{}: (0, {})} | custom-call | bytes 3145728 | tf_op jit(solution)/shard_map/pallas_call | solution.py:205
  (2 shorter events, 0.1 us)
Async XLA Ops:
  3.0 8.8 %copy-start.4 = (s32[256,5,2]{0,2,1:T(2,128)S(1)}, s32[256,5,2]{0,2,1:T(2,128)}, u32[]{:S(2)}) copy-start(s32[256,5,2]{0,2,1:T(2,128)} %param.6) | copy-start | bytes 30724
  3.0 47.6 %all-to-all-start = ((bf16[32,200,128]{2,1,0:T(8,128)(2,1)}), bf16[32,200,128]{2,1,0:T(8,128)(2,1)}, u32[]{:S(2)}, u32[]{:S(2)}) async-start(bf16[32,200,128]{2,1,0:T(8,128)(2,1)} %shard_map.46), calls=%async_computation | async-start | bytes 3276800 | tf_op jit(solution)/shard_map/all_to_all | solution.py:233
  11.5 3.9 %collective-permute-start = (bf16[64,32,128]{2,1,0:T(8,128)(2,1)S(1)}, bf16[64,32,128]{2,1,0:T(8,128)(2,1)}, u32[]{:S(2)}, u32[]{:S(2)}) collective-permute-start(bf16[64,32,128]{2,1,0:T(8,128)(2,1)S(1)} %slice.17.own_ref), channel_id=1, source_target_pairs={{0,1},{1,0},{2,3},{3,2},{4,5},{5,4},{6,7},{7,6},{8,9},{9,8},{10,11... | collective-permute-start | bytes 1572872 | tf_op jit(solution)/shard_map/ppermute | solution.py:237
  11.9 3.6 %copy-start.3 = (s32[5]{0:T(128)S(1)}, s32[5]{0:T(128)}, u32[]{:S(2)}) copy-start(s32[5]{0:T(128)} %order_ref.15) | copy-start | bytes 64
  18.3 13.4 %collective-permute-start.1 = (bf16[32,32,128]{2,1,0:T(8,128)(2,1)S(1)}, bf16[32,32,128]{2,1,0:T(8,128)(2,1)S(1)}, u32[]{:S(2)}, u32[]{:S(2)}) collective-permute-start(bf16[32,32,128]{2,1,0:T(8,128)(2,1)S(1)} %get-tuple-element.12.own_ref), channel_id=1, source_target_pairs={{0,2},{1,3},{2,0},{3,1},{4,6},{5,7},{6,4},{7,5},{8,10},{9,11},{10,... | collective-permute-start | bytes 786440 | tf_op jit(solution)/shard_map/ppermute | solution.py:237
  20.0 20.0 %collective-permute-start.4 = (bf16[32,32,128]{2,1,0:T(8,128)(2,1)S(1)}, bf16[32,32,128]{2,1,0:T(8,128)(2,1)S(1)}, u32[]{:S(2)}, u32[]{:S(2)}) collective-permute-start(bf16[32,32,128]{2,1,0:T(8,128)(2,1)S(1)} %get-tuple-element.11.own_ref), channel_id=1, source_target_pairs={{0,2},{1,3},{2,0},{3,1},{4,6},{5,7},{6,4},{7,5},{8,10},{9,11},{10,... | collective-permute-start | bytes 786440 | tf_op jit(solution)/shard_map/ppermute | solution.py:237
  32.9 14.5 %collective-permute-start.2 = (bf16[32,32,128]{2,1,0:T(8,128)(2,1)S(1)}, bf16[32,32,128]{2,1,0:T(8,128)(2,1)S(1)}, u32[]{:S(2)}, u32[]{:S(2)}) collective-permute-start(bf16[32,32,128]{2,1,0:T(8,128)(2,1)S(1)} %shard_map.49.own_ref), channel_id=1, source_target_pairs={{0,4},{1,5},{2,6},{3,7},{4,0},{5,1},{6,2},{7,3},{8,12},{9,13},{10,... | collective-permute-start | bytes 786440 | tf_op jit(solution)/shard_map/ppermute | solution.py:237
  41.2 22.5 %collective-permute-start.5 = (bf16[32,32,128]{2,1,0:T(8,128)(2,1)S(1)}, bf16[32,32,128]{2,1,0:T(8,128)(2,1)S(1)}, u32[]{:S(2)}, u32[]{:S(2)}) collective-permute-start(bf16[32,32,128]{2,1,0:T(8,128)(2,1)S(1)} %shard_map.51.own_ref), channel_id=1, source_target_pairs={{0,4},{1,5},{2,6},{3,7},{4,0},{5,1},{6,2},{7,3},{8,12},{9,13},{10,... | collective-permute-start | bytes 786440 | tf_op jit(solution)/shard_map/ppermute | solution.py:237
  48.5 15.1 %collective-permute-start.3 = (bf16[32,32,128]{2,1,0:T(8,128)(2,1)S(1)}, bf16[32,32,128]{2,1,0:T(8,128)(2,1)}, u32[]{:S(2)}, u32[]{:S(2)}) collective-permute-start(bf16[32,32,128]{2,1,0:T(8,128)(2,1)S(1)} %shard_map.50), channel_id=1, source_target_pairs={{0,8},{1,9},{2,10},{3,11},{4,12},{5,13},{6,14},{7,15},{8,0},{9,1},... | collective-permute-start | bytes 786440 | tf_op jit(solution)/shard_map/ppermute | solution.py:237
  63.6 2.9 %copy-start = (bf16[32,6,32,128]{3,2,1,0:T(8,128)(2,1)}, bf16[32,6,32,128]{3,2,1,0:T(8,128)(2,1)S(1)}, u32[]{:S(2)}) copy-start(bf16[32,6,32,128]{3,2,1,0:T(8,128)(2,1)S(1)} %shard_map.47) | copy-start | bytes 4718596
  63.7 0.8 copy-start.1
  64.4 0.9 copy-start.2
  66.5 22.8 %collective-permute-start.6 = (bf16[32,32,128]{2,1,0:T(8,128)(2,1)S(1)}, bf16[32,32,128]{2,1,0:T(8,128)(2,1)S(1)}, u32[]{:S(2)}, u32[]{:S(2)}) collective-permute-start(bf16[32,32,128]{2,1,0:T(8,128)(2,1)S(1)} %shard_map.52), channel_id=1, source_target_pairs={{0,8},{1,9},{2,10},{3,11},{4,12},{5,13},{6,14},{7,15},{8,0},{9,1},... | collective-permute-start | bytes 786440 | tf_op jit(solution)/shard_map/ppermute | solution.py:237
  67.4 47.6 %all-to-all-start.1 = ((bf16[32,6,32,128]{3,2,1,0:T(8,128)(2,1)}), bf16[32,6,32,128]{3,2,1,0:T(8,128)(2,1)}, u32[]{:S(2)}, u32[]{:S(2)}) async-start(bf16[32,6,32,128]{3,2,1,0:T(8,128)(2,1)} %copy-done), calls=%async_computation.1 | async-start | bytes 3145728 | tf_op jit(solution)/shard_map/all_to_all | solution.py:233
  92.1 12.4 %collective-permute-start.7 = (bf16[64,32,128]{2,1,0:T(8,128)(2,1)S(1)}, bf16[64,32,128]{2,1,0:T(8,128)(2,1)S(1)}, u32[]{:S(2)}, u32[]{:S(2)}) collective-permute-start(bf16[64,32,128]{2,1,0:T(8,128)(2,1)S(1)} %shard_map.53.own_ref), channel_id=1, source_target_pairs={{0,16},{16,0},{1,17},{17,1},{2,18},{18,2},{3,19},{19,3},{4,20},{20... | collective-permute-start | bytes 1572872 | tf_op jit(solution)/shard_map/ppermute | solution.py:237

commit v3 on v2

--- a/solution.py
+++ b/solution.py
@@ -15,16 +15,18 @@
 PARAMS = pltpu.CompilerParams(vmem_limit_bytes=24 * 1024 * 1024)
 
 
-def all_levels_kernel(order_ref, index_ref, field_ref, table_ref, out_ref, even, odd):
+def levels_kernel(some, order_ref, index_ref, field_ref, table_ref, out_ref, even, odd):
     devices, share, rhs, rank = out_ref.shape
     levels = order_ref.shape[0]
-    for level in range(levels):
-        target = out_ref if level == levels - 1 else (even, odd)[(level + 1) % 2]
+    for level in some:
+        target = out_ref if level == some[-1] else (even, odd)[(level + 1) % 2]
         slot = order_ref[level]
 
         def load(d, j):
             if level == 0:
                 return field_ref[d, pl.ds(rhs * j, rhs), :]
+            if level == some[0]:
+                return field_ref[d, j]
             return (even, odd)[level % 2][d, j]
 
         def entries(d, j):
@@ -50,13 +52,13 @@
         lax.fori_loop(0, devices // 2, one_pair, 0, unroll=8)
 
 
-def apply_all_levels(payload, share, rhs, table, index, order):
-    devices, _, rank = payload.shape
-    levels = table.shape[0]
+def apply_levels(some, payload, share, rhs, table, index, order):
+    devices, rank = payload.shape[0], payload.shape[-1]
+    levels = len(some)
     shape = (devices, share, rhs, rank)
     blocks = devices * share
     return pl.pallas_call(
-        all_levels_kernel,
+        functools.partial(levels_kernel, some),
         grid_spec=pltpu.PrefetchScalarGridSpec(
             num_scalar_prefetch=2,
             grid=(),
@@ -255,12 +257,16 @@
         first_other = partner(first, last_middle)
         second_other = partner(second, last_middle - 1)
     index = arrived[:, far_units * rhs].astype(jnp.int32)
-    far = apply_all_levels(arrived, far_units, rhs, table, index, level_order)
     if units == far_units:
+        far = apply_levels(range(levels), arrived, far_units, rhs, table, index, level_order)
         return exchange(far).reshape(vectors.shape)
-    far, first_other, near_index = lax.optimization_barrier((far, first_other, near_index))
+    far = apply_levels(range(2), arrived, far_units, rhs, table, index, level_order)
+    far, near_index = lax.optimization_barrier((far, near_index))
     second = near_level(second, last_middle - 1, second_other, offset=half)
+    far, second = lax.optimization_barrier((far, second))
     second_other = partner(second, last_middle)
+    far = apply_levels(range(2, levels), far, far_units, rhs, table, index, level_order)
+    far, first_other = lax.optimization_barrier((far, first_other))
     far = exchange(far).reshape(spread, rhs, rank)
     near = near_level(
         jnp.concatenate([first, second]),

time: 118 us -> 116 us (0.983)
  waiting for transfers between devices: 55.4 us -> 52 us
  local copies, waits for them, and re-layouts: 6.49 us -> 8.39 us
    ppermute x8, waiting for transfers between devices: 47.4 us -> 43.6 us  [partner(): lax.ppermute(array, axis, [(i, i ^ 1 << bit) for i in range(lax.axis_size...]
    pallas_call x1 -> x2, Pallas kernels: 12.1 us -> 12.9 us  [apply_levels(): pl.pallas_call(functools.partial(levels_kernel, some), grid_spec=pltpu.Pr...]
  transfers between devices with their start and end apart: 10 -> 10, of which waited for: 6 -> 5; matrix products, arithmetic and copies ran while one was open for 6% -> 6% of each run, Pallas kernels for 19% -> 21%
where the time goes in v3:
time: 116 us
  waiting for transfers between devices  52 us (45%)
  Pallas kernels  29.6 us (26%)
  starting transfers between devices  24.4 us (21%)
  local copies, waits for them, and re-layouts  8.39 us (7%)
    ppermute x8, waiting for transfers between devices, partner(): lax.ppermute(array, axis, [(i, i ^ 1 << bit) for i in range(lax.axis_size...  43.6 us
    all_to_all x2, starting transfers between devices, exchange(): return lax.all_to_all(array, AXES, split_axis=0, concat_axis=0, tiled=True)  13 us
    pallas_call x2, Pallas kernels, apply_levels(): pl.pallas_call(functools.partial(levels_kernel, some), grid_spec=pltpu.Pr...  12.9 us
    ppermute x8, starting transfers between devices, partner(): lax.ppermute(array, axis, [(i, i ^ 1 << bit) for i in range(lax.axis_size...  11.5 us
    pallas_call x7, Pallas kernels, apply_level(): pl.pallas_call(functools.partial(one_level_kernel, level, offset), grid_s...  10.7 us
    all_to_all x2, waiting for transfers between devices, exchange(): return lax.all_to_all(array, AXES, split_axis=0, concat_axis=0, tiled=True)  8.39 us
    unnamed x11, local copies, waits for them, and re-layouts  6.04 us
    pallas_call x1, Pallas kernels, pack(): pl.pallas_call(functools.partial(pack_kernel, units), in_specs=[pl.BlockS...  3.01 us
  transfers between devices with their start and end apart: 10, of which 5 were waited for; matrix products, arithmetic and copies ran while one was open for 6% of the time, Pallas kernels for 21%

profile of v3, /device:TPU:0, one launch (start us, length us, event | category | flops | bytes accessed | tf_op | source)
XLA Modules:
  0.0 115.7 jit_solution(9663182887430968998)
XLA Ops:
  0.0 3.0 %shard_map.46 = bf16[32,200,128]{2,1,0:T(8,128)(2,1)} custom-call(bf16[256,32,128]{2,1,0:T(8,128)(2,1)} %vectors_ref.1, s32[5,2,256]{2,1,0:T(2,128)} %bitcast.17), custom_call_target="tpu_custom_call" | custom-call | bytes 4194304 | tf_op jit(solution)/shard_map/pallas_call | solution.py:134
  3.0 0.0 copy-start.4
  3.0 7.4 %all-to-all-start = ((bf16[32,200,128]{2,1,0:T(8,128)(2,1)}), bf16[32,200,128]{2,1,0:T(8,128)(2,1)}, u32[]{:S(2)}, u32[]{:S(2)}) async-start(bf16[32,200,128]{2,1,0:T(8,128)(2,1)} %shard_map.46), calls=%async_computation | async-start | bytes 3276800 | tf_op jit(solution)/shard_map/all_to_all | solution.py:235
  10.5 1.1 slice.17.own_ref
  11.5 0.3 collective-permute-start
  11.8 0.0 copy-done.4
  11.8 0.1 slice.16
  11.9 0.2 copy.15
  12.0 0.1 reshape.8.index_ref
  12.2 0.0 copy-start.3
  12.2 3.2 %copy.14 = bf16[5,16,128,128]{2,3,1,0:T(8,128)(2,1)S(1)} copy(bf16[5,16,128,128]{3,2,1,0:T(8,128)(2,1)} %param.5) | data formatting | bytes 5242880 | tf_op args[1]
  15.5 0.0 collective-permute-done.other_ref
  15.5 0.0 copy-done.3
  15.5 2.7 %shard_map.48 = bf16[64,32,128]{2,1,0:T(8,128)(2,1)S(1)} custom-call(s32[5]{0:T(128)S(1)} %copy-done.3, s32[640]{0:T(1024)S(1)} %reshape.8.index_ref, bf16[64,32,128]{2,1,0:T(8,128)(2,1)S(1)} %slice.17.own_ref, bf16[64,32,128]{2,1,0:T(8,128)(2,1)} %collective-permute-done.other_ref, bf16[5,16,128,128]{3,2,1,0:T(8,128)(2,1)S(1)} %bitcast.8), custom_call_target="tpu_custom_call" | custom-call | flops 939524096 | bytes 4194304 | tf_op jit(solution)/shard_map/pallas_call | solution.py:161
  18.3 1.7 %collective-permute-start.1 = (bf16[32,32,128]{2,1,0:T(8,128)(2,1)S(1)}, bf16[32,32,128]{2,1,0:T(8,128)(2,1)S(1)}, u32[]{:S(2)}, u32[]{:S(2)}) collective-permute-start(bf16[32,32,128]{2,1,0:T(8,128)(2,1)S(1)} %get-tuple-element.17.own_ref), channel_id=1, source_target_pairs={{0,2},{1,3},{2,0},{3,1},{4,6},{5,7},{6,4},{7,5},{8,10},{9,11},{10,... | collective-permute-start | bytes 786440 | tf_op jit(solution)/shard_map/ppermute | solution.py:239
  20.0 0.3 collective-permute-start.3
  20.4 11.3 %collective-permute-done.1.other_ref = bf16[32,32,128]{2,1,0:T(8,128)(2,1)S(1)} collective-permute-done((bf16[32,32,128]{2,1,0:T(8,128)(2,1)S(1)}, bf16[32,32,128]{2,1,0:T(8,128)(2,1)S(1)}, u32[]{:S(2)}, u32[]{:S(2)}) %collective-permute-start.1) | collective-permute-done | bytes 262176 | tf_op jit(solution)/shard_map/ppermute | solution.py:239
  31.7 1.1 shard_map.49.own_ref
  32.8 1.9 %collective-permute-start.2 = (bf16[32,32,128]{2,1,0:T(8,128)(2,1)S(1)}, bf16[32,32,128]{2,1,0:T(8,128)(2,1)S(1)}, u32[]{:S(2)}, u32[]{:S(2)}) collective-permute-start(bf16[32,32,128]{2,1,0:T(8,128)(2,1)S(1)} %shard_map.49.own_ref), channel_id=1, source_target_pairs={{0,4},{1,5},{2,6},{3,7},{4,0},{5,1},{6,2},{7,3},{8,12},{9,13},{10,... | collective-permute-start | bytes 786440 | tf_op jit(solution)/shard_map/ppermute | solution.py:239
  34.7 5.3 %collective-permute-done.3.other_ref = bf16[32,32,128]{2,1,0:T(8,128)(2,1)S(1)} collective-permute-done((bf16[32,32,128]{2,1,0:T(8,128)(2,1)S(1)}, bf16[32,32,128]{2,1,0:T(8,128)(2,1)S(1)}, u32[]{:S(2)}, u32[]{:S(2)}) %collective-permute-start.3) | collective-permute-done | bytes 262176 | tf_op jit(solution)/shard_map/ppermute | solution.py:239
  40.0 1.1 shard_map.51.own_ref
  41.2 2.4 %collective-permute-start.4 = (bf16[32,32,128]{2,1,0:T(8,128)(2,1)S(1)}, bf16[32,32,128]{2,1,0:T(8,128)(2,1)S(1)}, u32[]{:S(2)}, u32[]{:S(2)}) collective-permute-start(bf16[32,32,128]{2,1,0:T(8,128)(2,1)S(1)} %shard_map.51.own_ref), channel_id=1, source_target_pairs={{0,4},{1,5},{2,6},{3,7},{4,0},{5,1},{6,2},{7,3},{8,12},{9,13},{10,... | collective-permute-start | bytes 786440 | tf_op jit(solution)/shard_map/ppermute | solution.py:239
  43.6 3.7 %collective-permute-done.2.other_ref = bf16[32,32,128]{2,1,0:T(8,128)(2,1)S(1)} collective-permute-done((bf16[32,32,128]{2,1,0:T(8,128)(2,1)S(1)}, bf16[32,32,128]{2,1,0:T(8,128)(2,1)S(1)}, u32[]{:S(2)}, u32[]{:S(2)}) %collective-permute-start.2) | collective-permute-done | bytes 262176 | tf_op jit(solution)/shard_map/ppermute | solution.py:239
  47.3 1.1 shard_map.50
  48.5 2.2 %collective-permute-start.5 = (bf16[32,32,128]{2,1,0:T(8,128)(2,1)S(1)}, bf16[32,32,128]{2,1,0:T(8,128)(2,1)}, u32[]{:S(2)}, u32[]{:S(2)}) collective-permute-start(bf16[32,32,128]{2,1,0:T(8,128)(2,1)S(1)} %shard_map.50), channel_id=1, source_target_pairs={{0,8},{1,9},{2,10},{3,11},{4,12},{5,13},{6,14},{7,15},{8,0},{9,1},... | collective-permute-start | bytes 786440 | tf_op jit(solution)/shard_map/ppermute | solution.py:239
  50.7 0.0 all-to-all-done.field_ref
  50.7 0.9 slice.20
  51.5 6.2 %shard_map.47.field_ref = bf16[32,6,32,128]{3,2,1,0:T(8,128)(2,1)S(1)} custom-call(s32[5]{0:T(128)S(1)} %copy-done.3, s32[32,128]{1,0:T(8,128)S(1)} %fusion.index_ref, bf16[32,200,128]{2,1,0:T(8,128)(2,1)} %all-to-all-done.field_ref, bf16[5,16,128,128]{3,2,1,0:T(8,128)(2,1)S(1)} %bitcast.12), custom_call_target="tpu_custom_call" | custom-call | flops 805306368 | bytes 5767168 | tf_op jit(solution)/shard_map/pallas_call | solution.py:60
  57.8 0.0 collective-permute-done.4.other_ref
  57.8 0.0 copy-start.1
  57.8 0.7 copy-done.1
  58.5 0.0 copy-start.2
  58.5 0.9 copy-done.2
  59.4 1.1 shard_map.52
  60.6 0.9 collective-permute-start.6
  61.4 6.7 %shard_map.53 = bf16[32,6,32,128]{3,2,1,0:T(8,128)(2,1)S(1)} custom-call(s32[5]{0:T(128)S(1)} %copy-done.3, s32[32,128]{1,0:T(8,128)S(1)} %fusion.index_ref, bf16[32,6,32,128]{3,2,1,0:T(8,128)(2,1)S(1)} %shard_map.47.field_ref, bf16[5,16,128,128]{3,2,1,0:T(8,128)(2,1)S(1)} %bitcast.14), custom_call_target="tpu_custom_call" | custom-call | flops 1207959552 | bytes 5767168 | tf_op jit(solution)/shard_map/pallas_call | solution.py:60
  68.2 0.0 copy-start
  68.2 1.1 copy-done
  69.3 0.0 collective-permute-done.5
  69.3 5.5 %all-to-all-start.1 = ((bf16[32,6,32,128]{3,2,1,0:T(8,128)(2,1)}), bf16[32,6,32,128]{3,2,1,0:T(8,128)(2,1)}, u32[]{:S(2)}, u32[]{:S(2)}) async-start(bf16[32,6,32,128]{3,2,1,0:T(8,128)(2,1)} %copy-done), calls=%async_computation.1 | async-start | bytes 3145728 | tf_op jit(solution)/shard_map/all_to_all | solution.py:235
  74.9 0.0 collective-permute-done.6
  74.9 1.0 pad_maximum_fusion.1.other_ref
  75.9 1.7 %shard_map.54.own_ref = bf16[64,32,128]{2,1,0:T(8,128)(2,1)S(1)} custom-call(s32[5]{0:T(128)S(1)} %copy-done.3, s32[640]{0:T(1024)S(1)} %reshape.8.index_ref, bf16[64,32,128]{2,1,0:T(8,128)(2,1)S(1)} %pad_maximum_fusion.own_ref, bf16[64,32,128]{2,1,0:T(8,128)(2,1)S(1)} %pad_maximum_fusion.1.other_ref, bf16[5,16,128,128]{3,2,1,0:T(8,128)(2,1)S(1)} %bitcast.15), custom_call_target="tpu_custom_call" | custom-call | flops 46976204800 | bytes 4194304 | tf_op jit(solution)/shard_map/pallas_call | solution.py:161
  77.6 1.8 %collective-permute-start.7 = (bf16[64,32,128]{2,1,0:T(8,128)(2,1)S(1)}, bf16[64,32,128]{2,1,0:T(8,128)(2,1)S(1)}, u32[]{:S(2)}, u32[]{:S(2)}) collective-permute-start(bf16[64,32,128]{2,1,0:T(8,128)(2,1)S(1)} %shard_map.54.own_ref), channel_id=1, source_target_pairs={{0,16},{16,0},{1,17},{17,1},{2,18},{18,2},{3,19},{19,3},{4,20},{20... | collective-permute-start | bytes 1572872 | tf_op jit(solution)/shard_map/ppermute | solution.py:239
  79.4 23.2 %collective-permute-done.7.other_ref = bf16[64,32,128]{2,1,0:T(8,128)(2,1)S(1)} collective-permute-done((bf16[64,32,128]{2,1,0:T(8,128)(2,1)S(1)}, bf16[64,32,128]{2,1,0:T(8,128)(2,1)S(1)}, u32[]{:S(2)}, u32[]{:S(2)}) %collective-permute-start.7) | collective-permute-done | bytes 524320 | tf_op jit(solution)/shard_map/ppermute | solution.py:239
  102.6 1.7 %shard_map.55.refs_0_ = bf16[64,32,128]{2,1,0:T(8,128)(2,1)S(1)} custom-call(s32[5]{0:T(128)S(1)} %copy-done.3, s32[640]{0:T(1024)S(1)} %reshape.8.index_ref, bf16[64,32,128]{2,1,0:T(8,128)(2,1)S(1)} %shard_map.54.own_ref, bf16[64,32,128]{2,1,0:T(8,128)(2,1)S(1)} %collective-permute-done.7.other_ref, bf16[5,16,128,128]{3,2,1,0:T(8,128)(2,1)S(1)} %bitcast.16), custom_call_target="tpu_custom_call" | custom-call | flops 939524096 | bytes 4194304 | tf_op jit(solution)/shard_map/pallas_call | solution.py:161
  104.3 0.9 shard_map.56.refs_0_
  105.2 8.4 %all-to-all-done.1 = bf16[32,6,32,128]{3,2,1,0:T(8,128)(2,1)} async-done(((bf16[32,6,32,128]{3,2,1,0:T(8,128)(2,1)}), bf16[32,6,32,128]{3,2,1,0:T(8,128)(2,1)}, u32[]{:S(2)}, u32[]{:S(2)}) %all-to-all-start.1) | async-done | bytes 1572896 | tf_op jit(solution)/shard_map/all_to_all | solution.py:235
  113.6 2.1 %shard_map.57 = bf16[256,32,128]{2,1,0:T(8,128)(2,1)} custom-call(bf16[256,32,128]{2,1,0:T(8,128)(2,1)} %shard_map.56.refs_0_, bf16[192,32,128]{2,1,0:T(8,128)(2,1)} %bitcast.4.refs_1_), custom_call_target="tpu_custom_call", output_to_operand_aliasing={{}: (0, {})} | custom-call | bytes 3145728 | tf_op jit(solution)/shard_map/pallas_call | solution.py:207
  (3 shorter events, 0.1 us)
Async XLA Ops:
  3.0 8.8 %copy-start.4 = (s32[256,5,2]{0,2,1:T(2,128)S(1)}, s32[256,5,2]{0,2,1:T(2,128)}, u32[]{:S(2)}) copy-start(s32[256,5,2]{0,2,1:T(2,128)} %param.6) | copy-start | bytes 30724
  3.0 47.6 %all-to-all-start = ((bf16[32,200,128]{2,1,0:T(8,128)(2,1)}), bf16[32,200,128]{2,1,0:T(8,128)(2,1)}, u32[]{:S(2)}, u32[]{:S(2)}) async-start(bf16[32,200,128]{2,1,0:T(8,128)(2,1)} %shard_map.46), calls=%async_computation | async-start | bytes 3276800 | tf_op jit(solution)/shard_map/all_to_all | solution.py:235
  11.5 3.9 %collective-permute-start = (bf16[64,32,128]{2,1,0:T(8,128)(2,1)S(1)}, bf16[64,32,128]{2,1,0:T(8,128)(2,1)}, u32[]{:S(2)}, u32[]{:S(2)}) collective-permute-start(bf16[64,32,128]{2,1,0:T(8,128)(2,1)S(1)} %slice.17.own_ref), channel_id=1, source_target_pairs={{0,1},{1,0},{2,3},{3,2},{4,5},{5,4},{6,7},{7,6},{8,9},{9,8},{10,11... | collective-permute-start | bytes 1572872 | tf_op jit(solution)/shard_map/ppermute | solution.py:239
  12.2 3.3 %copy-start.3 = (s32[5]{0:T(128)S(1)}, s32[5]{0:T(128)}, u32[]{:S(2)}) copy-start(s32[5]{0:T(128)} %order_ref.17) | copy-start | bytes 64
  18.3 13.4 %collective-permute-start.1 = (bf16[32,32,128]{2,1,0:T(8,128)(2,1)S(1)}, bf16[32,32,128]{2,1,0:T(8,128)(2,1)S(1)}, u32[]{:S(2)}, u32[]{:S(2)}) collective-permute-start(bf16[32,32,128]{2,1,0:T(8,128)(2,1)S(1)} %get-tuple-element.17.own_ref), channel_id=1, source_target_pairs={{0,2},{1,3},{2,0},{3,1},{4,6},{5,7},{6,4},{7,5},{8,10},{9,11},{10,... | collective-permute-start | bytes 786440 | tf_op jit(solution)/shard_map/ppermute | solution.py:239
  20.0 20.0 %collective-permute-start.3 = (bf16[32,32,128]{2,1,0:T(8,128)(2,1)S(1)}, bf16[32,32,128]{2,1,0:T(8,128)(2,1)S(1)}, u32[]{:S(2)}, u32[]{:S(2)}) collective-permute-start(bf16[32,32,128]{2,1,0:T(8,128)(2,1)S(1)} %get-tuple-element.18.own_ref), channel_id=1, source_target_pairs={{0,2},{1,3},{2,0},{3,1},{4,6},{5,7},{6,4},{7,5},{8,10},{9,11},{10,... | collective-permute-start | bytes 786440 | tf_op jit(solution)/shard_map/ppermute | solution.py:239
  32.8 14.5 %collective-permute-start.2 = (bf16[32,32,128]{2,1,0:T(8,128)(2,1)S(1)}, bf16[32,32,128]{2,1,0:T(8,128)(2,1)S(1)}, u32[]{:S(2)}, u32[]{:S(2)}) collective-permute-start(bf16[32,32,128]{2,1,0:T(8,128)(2,1)S(1)} %shard_map.49.own_ref), channel_id=1, source_target_pairs={{0,4},{1,5},{2,6},{3,7},{4,0},{5,1},{6,2},{7,3},{8,12},{9,13},{10,... | collective-permute-start | bytes 786440 | tf_op jit(solution)/shard_map/ppermute | solution.py:239
  41.2 16.6 %collective-permute-start.4 = (bf16[32,32,128]{2,1,0:T(8,128)(2,1)S(1)}, bf16[32,32,128]{2,1,0:T(8,128)(2,1)S(1)}, u32[]{:S(2)}, u32[]{:S(2)}) collective-permute-start(bf16[32,32,128]{2,1,0:T(8,128)(2,1)S(1)} %shard_map.51.own_ref), channel_id=1, source_target_pairs={{0,4},{1,5},{2,6},{3,7},{4,0},{5,1},{6,2},{7,3},{8,12},{9,13},{10,... | collective-permute-start | bytes 786440 | tf_op jit(solution)/shard_map/ppermute | solution.py:239
  48.5 20.8 %collective-permute-start.5 = (bf16[32,32,128]{2,1,0:T(8,128)(2,1)S(1)}, bf16[32,32,128]{2,1,0:T(8,128)(2,1)}, u32[]{:S(2)}, u32[]{:S(2)}) collective-permute-start(bf16[32,32,128]{2,1,0:T(8,128)(2,1)S(1)} %shard_map.50), channel_id=1, source_target_pairs={{0,8},{1,9},{2,10},{3,11},{4,12},{5,13},{6,14},{7,15},{8,0},{9,1},... | collective-permute-start | bytes 786440 | tf_op jit(solution)/shard_map/ppermute | solution.py:239
  57.8 0.7 copy-start.1
  58.5 0.9 copy-start.2
  60.6 14.4 %collective-permute-start.6 = (bf16[32,32,128]{2,1,0:T(8,128)(2,1)S(1)}, bf16[32,32,128]{2,1,0:T(8,128)(2,1)S(1)}, u32[]{:S(2)}, u32[]{:S(2)}) collective-permute-start(bf16[32,32,128]{2,1,0:T(8,128)(2,1)S(1)} %shard_map.52), channel_id=1, source_target_pairs={{0,8},{1,9},{2,10},{3,11},{4,12},{5,13},{6,14},{7,15},{8,0},{9,1},... | collective-permute-start | bytes 786440 | tf_op jit(solution)/shard_map/ppermute | solution.py:239
  68.2 1.1 copy-start
  69.3 44.3 %all-to-all-start.1 = ((bf16[32,6,32,128]{3,2,1,0:T(8,128)(2,1)}), bf16[32,6,32,128]{3,2,1,0:T(8,128)(2,1)}, u32[]{:S(2)}, u32[]{:S(2)}) async-start(bf16[32,6,32,128]{3,2,1,0:T(8,128)(2,1)} %copy-done), calls=%async_computation.1 | async-start | bytes 3145728 | tf_op jit(solution)/shard_map/all_to_all | solution.py:235
  77.6 25.0 %collective-permute-start.7 = (bf16[64,32,128]{2,1,0:T(8,128)(2,1)S(1)}, bf16[64,32,128]{2,1,0:T(8,128)(2,1)S(1)}, u32[]{:S(2)}, u32[]{:S(2)}) collective-permute-start(bf16[64,32,128]{2,1,0:T(8,128)(2,1)S(1)} %shard_map.54.own_ref), channel_id=1, source_target_pairs={{0,16},{16,0},{1,17},{17,1},{2,18},{18,2},{3,19},{19,3},{4,20},{20... | collective-permute-start | bytes 1572872 | tf_op jit(solution)/shard_map/ppermute | solution.py:239

commit v4 on v3

--- a/solution.py
+++ b/solution.py
@@ -15,11 +15,12 @@
 PARAMS = pltpu.CompilerParams(vmem_limit_bytes=24 * 1024 * 1024)
 
 
-def levels_kernel(some, order_ref, index_ref, field_ref, table_ref, out_ref, even, odd):
+def levels_kernel(some, sends, order_ref, index_ref, field_ref, table_ref, out_ref, even, odd, sem):
     devices, share, rhs, rank = out_ref.shape
     levels = order_ref.shape[0]
     for level in some:
-        target = out_ref if level == some[-1] else (even, odd)[(level + 1) % 2]
+        last = level == some[-1]
+        target = out_ref if last and not sends else (even, odd)[(level + 1) % 2]
         slot = order_ref[level]
 
         def load(d, j):
@@ -49,22 +50,31 @@
                 target[high, j] = product[:, rank:]
             return carry
 
-        lax.fori_loop(0, devices // 2, one_pair, 0, unroll=8)
-
-
-def apply_levels(some, payload, share, rhs, table, index, order):
+        if not (last and sends):
+            lax.fori_loop(0, devices // 2, one_pair, 0, unroll=8)
+            continue
+        pairs = devices // 2
+        for first in (0, pairs // 2):
+            lax.fori_loop(first, first + pairs // 2, one_pair, 0, unroll=8)
+            for begin in (first, pairs + first):
+                done = pl.ds(begin, pairs // 2)
+                pltpu.make_async_copy(target.at[done], out_ref.at[done], sem).start()
+        pltpu.make_async_copy(target, out_ref, sem).wait()
+
+
+def apply_levels(some, sends, payload, share, rhs, table, index, order):
     devices, rank = payload.shape[0], payload.shape[-1]
     levels = len(some)
     shape = (devices, share, rhs, rank)
     blocks = devices * share
     return pl.pallas_call(
-        functools.partial(levels_kernel, some),
+        functools.partial(levels_kernel, some, sends),
         grid_spec=pltpu.PrefetchScalarGridSpec(
             num_scalar_prefetch=2,
             grid=(),
             in_specs=[pl.BlockSpec(memory_space=pltpu.VMEM)] * 2,
-            out_specs=pl.BlockSpec(memory_space=pltpu.VMEM),
-            scratch_shapes=[pltpu.VMEM(shape, jnp.bfloat16)] * 2,
+            out_specs=pl.BlockSpec(memory_space=pltpu.HBM if sends else pltpu.VMEM),
+            scratch_shapes=[pltpu.VMEM(shape, jnp.bfloat16)] * 2 + [pltpu.SemaphoreType.DMA],
         ),
         out_shape=jax.ShapeDtypeStruct(shape, jnp.bfloat16),
         compiler_params=PARAMS,
@@ -142,7 +152,13 @@
     )(vectors, jnp.transpose(factor_index, (1, 2, 0)))
 
 
-def one_level_kernel(level, offset, order_ref, index_ref, own_ref, other_ref, table_ref, out_ref):
+def one_level_kernel(level, offset, order_ref, index_ref, own_ref, other_ref, table_ref, out_ref, *fetched):
+    if fetched:
+        held, sem = fetched
+        copy = pltpu.make_async_copy(other_ref, held, sem)
+        copy.start()
+        copy.wait()
+        other_ref = held
     levels = order_ref.shape[0]
     slot = order_ref[level]
 
@@ -156,15 +172,20 @@
     lax.fori_loop(0, own_ref.shape[0], one_block, 0, unroll=16)
 
 
-def apply_level(own, other, table, index, order, level, offset=0, weight=1):
+def apply_level(own, other, table, index, order, level, offset=0, weight=1, fetch=False):
     blocks, rhs, rank = own.shape
     return pl.pallas_call(
         functools.partial(one_level_kernel, level, offset),
         grid_spec=pltpu.PrefetchScalarGridSpec(
             num_scalar_prefetch=2,
             grid=(),
-            in_specs=[pl.BlockSpec(memory_space=pltpu.VMEM)] * 3,
+            in_specs=[
+                pl.BlockSpec(memory_space=pltpu.VMEM),
+                pl.BlockSpec(memory_space=pltpu.HBM if fetch else pltpu.VMEM),
+                pl.BlockSpec(memory_space=pltpu.VMEM),
+            ],
             out_specs=pl.BlockSpec(memory_space=pltpu.VMEM),
+            scratch_shapes=[pltpu.VMEM(own.shape, own.dtype), pltpu.SemaphoreType.DMA] if fetch else [],
         ),
         out_shape=jax.ShapeDtypeStruct(own.shape, jnp.bfloat16),
         compiler_params=PARAMS,
@@ -258,14 +279,14 @@
         second_other = partner(second, last_middle - 1)
     index = arrived[:, far_units * rhs].astype(jnp.int32)
     if units == far_units:
-        far = apply_levels(range(levels), arrived, far_units, rhs, table, index, level_order)
+        far = apply_levels(range(levels), False, arrived, far_units, rhs, table, index, level_order)
         return exchange(far).reshape(vectors.shape)
-    far = apply_levels(range(2), arrived, far_units, rhs, table, index, level_order)
+    far = apply_levels(range(2), False, arrived, far_units, rhs, table, index, level_order)
     far, near_index = lax.optimization_barrier((far, near_index))
-    second = near_level(second, last_middle - 1, second_other, offset=half)
+    second = near_level(second, last_middle - 1, second_other, offset=half, fetch=True)
     far, second = lax.optimization_barrier((far, second))
     second_other = partner(second, last_middle)
-    far = apply_levels(range(2, levels), far, far_units, rhs, table, index, level_order)
+    far = apply_levels(range(2, levels), True, far, far_units, rhs, table, index, level_order)
     far, first_other = lax.optimization_barrier((far, first_other))
     far = exchange(far).reshape(spread, rhs, rank)
     near = near_level(

time: 116 us -> 117 us (level)
  transfers between devices with their start and end apart: 10 -> 10, of which waited for: 5 -> 5; matrix products, arithmetic and copies ran while one was open for 6% -> 6% of each run, Pallas kernels for 21% -> 22%
where the time goes in v4:
time: 117 us
  waiting for transfers between devices  52 us (44%)
  Pallas kernels  30.6 us (26%)
  starting transfers between devices  24.4 us (21%)
  local copies, waits for them, and re-layouts  8.39 us (7%)
    ppermute x8, waiting for transfers between devices, partner(): lax.ppermute(array, axis, [(i, i ^ 1 << bit) for i in range(lax.axis_size...  43.6 us
    pallas_call x2, Pallas kernels, apply_levels(): pl.pallas_call(functools.partial(levels_kernel, some, sends), grid_spec=p...  13.9 us
    all_to_all x2, starting transfers between devices, exchange(): return lax.all_to_all(array, AXES, split_axis=0, concat_axis=0, tiled=True)  13 us
    ppermute x8, starting transfers between devices, partner(): lax.ppermute(array, axis, [(i, i ^ 1 << bit) for i in range(lax.axis_size...  11.5 us
    pallas_call x7, Pallas kernels, apply_level(): pl.pallas_call(functools.partial(one_level_kernel, level, offset), grid_s...  10.7 us
    all_to_all x2, waiting for transfers between devices, exchange(): return lax.all_to_all(array, AXES, split_axis=0, concat_axis=0, tiled=True)  8.39 us
    unnamed x11, local copies, waits for them, and re-layouts  6.04 us
    pallas_call x1, Pallas kernels, pack(): pl.pallas_call(functools.partial(pack_kernel, units), in_specs=[pl.BlockS...  3.01 us
  transfers between devices with their start and end apart: 10, of which 5 were waited for; matrix products, arithmetic and copies ran while one was open for 6% of the time, Pallas kernels for 22%

profile of v4, /device:TPU:0, one launch (start us, length us, event | category | flops | bytes accessed | tf_op | source)
XLA Modules:
  0.0 116.7 jit_solution(18225952938736128400)
XLA Ops:
  0.0 3.0 %shard_map.46 = bf16[32,200,128]{2,1,0:T(8,128)(2,1)} custom-call(bf16[256,32,128]{2,1,0:T(8,128)(2,1)} %vectors_ref.1, s32[5,2,256]{2,1,0:T(2,128)} %bitcast.17), custom_call_target="tpu_custom_call" | custom-call | bytes 4194304 | tf_op jit(solution)/shard_map/pallas_call | solution.py:144
  3.0 0.0 copy-start.4
  3.0 7.4 %all-to-all-start = ((bf16[32,200,128]{2,1,0:T(8,128)(2,1)}), bf16[32,200,128]{2,1,0:T(8,128)(2,1)}, u32[]{:S(2)}, u32[]{:S(2)}) async-start(bf16[32,200,128]{2,1,0:T(8,128)(2,1)} %shard_map.46), calls=%async_computation | async-start | bytes 3276800 | tf_op jit(solution)/shard_map/all_to_all | solution.py:256
  10.5 1.1 slice.17.own_ref
  11.5 0.3 collective-permute-start
  11.8 0.0 copy-done.4
  11.8 0.1 slice.16
  11.9 0.2 copy.15
  12.0 0.1 reshape.8.index_ref
  12.2 0.0 copy-start.3
  12.2 3.2 %copy.14 = bf16[5,16,128,128]{2,3,1,0:T(8,128)(2,1)S(1)} copy(bf16[5,16,128,128]{3,2,1,0:T(8,128)(2,1)} %param.5) | data formatting | bytes 5242880 | tf_op args[1]
  15.5 0.0 collective-permute-done.other_ref
  15.5 0.0 copy-done.3
  15.5 2.7 %shard_map.48 = bf16[64,32,128]{2,1,0:T(8,128)(2,1)S(1)} custom-call(s32[5]{0:T(128)S(1)} %copy-done.3, s32[640]{0:T(1024)S(1)} %reshape.8.index_ref, bf16[64,32,128]{2,1,0:T(8,128)(2,1)S(1)} %slice.17.own_ref, bf16[64,32,128]{2,1,0:T(8,128)(2,1)} %collective-permute-done.other_ref, bf16[5,16,128,128]{3,2,1,0:T(8,128)(2,1)S(1)} %bitcast.8), custom_call_target="tpu_custom_call" | custom-call | flops 939524096 | bytes 4194304 | tf_op jit(solution)/shard_map/pallas_call | solution.py:177
  18.3 1.7 %collective-permute-start.1 = (bf16[32,32,128]{2,1,0:T(8,128)(2,1)S(1)}, bf16[32,32,128]{2,1,0:T(8,128)(2,1)S(1)}, u32[]{:S(2)}, u32[]{:S(2)}) collective-permute-start(bf16[32,32,128]{2,1,0:T(8,128)(2,1)S(1)} %get-tuple-element.17.own_ref), channel_id=1, source_target_pairs={{0,2},{1,3},{2,0},{3,1},{4,6},{5,7},{6,4},{7,5},{8,10},{9,11},{10,... | collective-permute-start | bytes 786440 | tf_op jit(solution)/shard_map/ppermute | solution.py:260
  20.0 0.3 collective-permute-start.3
  20.4 11.3 %collective-permute-done.1.other_ref = bf16[32,32,128]{2,1,0:T(8,128)(2,1)S(1)} collective-permute-done((bf16[32,32,128]{2,1,0:T(8,128)(2,1)S(1)}, bf16[32,32,128]{2,1,0:T(8,128)(2,1)S(1)}, u32[]{:S(2)}, u32[]{:S(2)}) %collective-permute-start.1) | collective-permute-done | bytes 262176 | tf_op jit(solution)/shard_map/ppermute | solution.py:260
  31.7 1.1 shard_map.49.own_ref
  32.8 1.9 %collective-permute-start.2 = (bf16[32,32,128]{2,1,0:T(8,128)(2,1)S(1)}, bf16[32,32,128]{2,1,0:T(8,128)(2,1)S(1)}, u32[]{:S(2)}, u32[]{:S(2)}) collective-permute-start(bf16[32,32,128]{2,1,0:T(8,128)(2,1)S(1)} %shard_map.49.own_ref), channel_id=1, source_target_pairs={{0,4},{1,5},{2,6},{3,7},{4,0},{5,1},{6,2},{7,3},{8,12},{9,13},{10,... | collective-permute-start | bytes 786440 | tf_op jit(solution)/shard_map/ppermute | solution.py:260
  34.7 5.3 %collective-permute-done.3.other_ref = bf16[32,32,128]{2,1,0:T(8,128)(2,1)S(1)} collective-permute-done((bf16[32,32,128]{2,1,0:T(8,128)(2,1)S(1)}, bf16[32,32,128]{2,1,0:T(8,128)(2,1)S(1)}, u32[]{:S(2)}, u32[]{:S(2)}) %collective-permute-start.3) | collective-permute-done | bytes 262176 | tf_op jit(solution)/shard_map/ppermute | solution.py:260
  40.0 1.1 shard_map.51.own_ref
  41.2 2.4 %collective-permute-start.4 = (bf16[32,32,128]{2,1,0:T(8,128)(2,1)S(1)}, bf16[32,32,128]{2,1,0:T(8,128)(2,1)S(1)}, u32[]{:S(2)}, u32[]{:S(2)}) collective-permute-start(bf16[32,32,128]{2,1,0:T(8,128)(2,1)S(1)} %shard_map.51.own_ref), channel_id=1, source_target_pairs={{0,4},{1,5},{2,6},{3,7},{4,0},{5,1},{6,2},{7,3},{8,12},{9,13},{10,... | collective-permute-start | bytes 786440 | tf_op jit(solution)/shard_map/ppermute | solution.py:260
  43.6 3.7 %collective-permute-done.2.other_ref = bf16[32,32,128]{2,1,0:T(8,128)(2,1)S(1)} collective-permute-done((bf16[32,32,128]{2,1,0:T(8,128)(2,1)S(1)}, bf16[32,32,128]{2,1,0:T(8,128)(2,1)S(1)}, u32[]{:S(2)}, u32[]{:S(2)}) %collective-permute-start.2) | collective-permute-done | bytes 262176 | tf_op jit(solution)/shard_map/ppermute | solution.py:260
  47.3 1.1 shard_map.50
  48.5 2.2 %collective-permute-start.5 = (bf16[32,32,128]{2,1,0:T(8,128)(2,1)S(1)}, bf16[32,32,128]{2,1,0:T(8,128)(2,1)}, u32[]{:S(2)}, u32[]{:S(2)}) collective-permute-start(bf16[32,32,128]{2,1,0:T(8,128)(2,1)S(1)} %shard_map.50), channel_id=1, source_target_pairs={{0,8},{1,9},{2,10},{3,11},{4,12},{5,13},{6,14},{7,15},{8,0},{9,1},... | collective-permute-start | bytes 786440 | tf_op jit(solution)/shard_map/ppermute | solution.py:260
  50.7 0.0 all-to-all-done.field_ref
  50.7 0.9 slice.20
  51.5 6.2 %shard_map.47.field_ref = bf16[32,6,32,128]{3,2,1,0:T(8,128)(2,1)S(1)} custom-call(s32[5]{0:T(128)S(1)} %copy-done.3, s32[32,128]{1,0:T(8,128)S(1)} %fusion.index_ref, bf16[32,200,128]{2,1,0:T(8,128)(2,1)} %all-to-all-done.field_ref, bf16[5,16,128,128]{3,2,1,0:T(8,128)(2,1)S(1)} %bitcast.12), custom_call_target="tpu_custom_call" | custom-call | flops 805306368 | bytes 5767168 | tf_op jit(solution)/shard_map/pallas_call | solution.py:70
  57.8 0.0 collective-permute-done.4.other_ref
  57.8 0.0 copy-start.1
  57.8 0.7 copy-done.1
  58.5 0.0 copy-start.2
  58.5 0.9 copy-done.2
  59.4 1.2 shard_map.52
  60.6 0.9 collective-permute-start.6
  61.5 7.7 %shard_map.53 = bf16[32,6,32,128]{3,2,1,0:T(8,128)(2,1)S(1)} custom-call(s32[5]{0:T(128)S(1)} %copy-done.3, s32[32,128]{1,0:T(8,128)S(1)} %fusion.index_ref, bf16[32,6,32,128]{3,2,1,0:T(8,128)(2,1)S(1)} %shard_map.47.field_ref, bf16[5,16,128,128]{3,2,1,0:T(8,128)(2,1)S(1)} %bitcast.14), custom_call_target="tpu_custom_call" | custom-call | flops 1207959552 | bytes 5767168 | tf_op jit(solution)/shard_map/pallas_call | solution.py:70
  69.2 0.0 copy-start
  69.2 1.1 copy-done
  70.3 0.0 collective-permute-done.5
  70.3 5.5 %all-to-all-start.1 = ((bf16[32,6,32,128]{3,2,1,0:T(8,128)(2,1)}), bf16[32,6,32,128]{3,2,1,0:T(8,128)(2,1)}, u32[]{:S(2)}, u32[]{:S(2)}) async-start(bf16[32,6,32,128]{3,2,1,0:T(8,128)(2,1)} %copy-done), calls=%async_computation.1 | async-start | bytes 3145728 | tf_op jit(solution)/shard_map/all_to_all | solution.py:256
  75.9 0.0 collective-permute-done.6
  75.9 1.0 pad_maximum_fusion.1.other_ref
  76.9 1.7 %shard_map.54.own_ref = bf16[64,32,128]{2,1,0:T(8,128)(2,1)S(1)} custom-call(s32[5]{0:T(128)S(1)} %copy-done.3, s32[640]{0:T(1024)S(1)} %reshape.8.index_ref, bf16[64,32,128]{2,1,0:T(8,128)(2,1)S(1)} %pad_maximum_fusion.own_ref, bf16[64,32,128]{2,1,0:T(8,128)(2,1)S(1)} %pad_maximum_fusion.1.other_ref, bf16[5,16,128,128]{3,2,1,0:T(8,128)(2,1)S(1)} %bitcast.15), custom_call_target="tpu_custom_call" | custom-call | flops 46976204800 | bytes 4194304 | tf_op jit(solution)/shard_map/pallas_call | solution.py:177
  78.6 1.8 %collective-permute-start.7 = (bf16[64,32,128]{2,1,0:T(8,128)(2,1)S(1)}, bf16[64,32,128]{2,1,0:T(8,128)(2,1)S(1)}, u32[]{:S(2)}, u32[]{:S(2)}) collective-permute-start(bf16[64,32,128]{2,1,0:T(8,128)(2,1)S(1)} %shard_map.54.own_ref), channel_id=1, source_target_pairs={{0,16},{16,0},{1,17},{17,1},{2,18},{18,2},{3,19},{19,3},{4,20},{20... | collective-permute-start | bytes 1572872 | tf_op jit(solution)/shard_map/ppermute | solution.py:260
  80.4 23.2 %collective-permute-done.7.other_ref = bf16[64,32,128]{2,1,0:T(8,128)(2,1)S(1)} collective-permute-done((bf16[64,32,128]{2,1,0:T(8,128)(2,1)S(1)}, bf16[64,32,128]{2,1,0:T(8,128)(2,1)S(1)}, u32[]{:S(2)}, u32[]{:S(2)}) %collective-permute-start.7) | collective-permute-done | bytes 524320 | tf_op jit(solution)/shard_map/ppermute | solution.py:260
  103.6 1.7 %shard_map.55.refs_0_ = bf16[64,32,128]{2,1,0:T(8,128)(2,1)S(1)} custom-call(s32[5]{0:T(128)S(1)} %copy-done.3, s32[640]{0:T(1024)S(1)} %reshape.8.index_ref, bf16[64,32,128]{2,1,0:T(8,128)(2,1)S(1)} %shard_map.54.own_ref, bf16[64,32,128]{2,1,0:T(8,128)(2,1)S(1)} %collective-permute-done.7.other_ref, bf16[5,16,128,128]{3,2,1,0:T(8,128)(2,1)S(1)} %bitcast.16), custom_call_target="tpu_custom_call" | custom-call | flops 939524096 | bytes 4194304 | tf_op jit(solution)/shard_map/pallas_call | solution.py:177
  105.3 0.9 shard_map.56.refs_0_
  106.2 8.4 %all-to-all-done.1 = bf16[32,6,32,128]{3,2,1,0:T(8,128)(2,1)} async-done(((bf16[32,6,32,128]{3,2,1,0:T(8,128)(2,1)}), bf16[32,6,32,128]{3,2,1,0:T(8,128)(2,1)}, u32[]{:S(2)}, u32[]{:S(2)}) %all-to-all-start.1) | async-done | bytes 1572896 | tf_op jit(solution)/shard_map/all_to_all | solution.py:256
  114.6 2.1 %shard_map.57 = bf16[256,32,128]{2,1,0:T(8,128)(2,1)} custom-call(bf16[256,32,128]{2,1,0:T(8,128)(2,1)} %shard_map.56.refs_0_, bf16[192,32,128]{2,1,0:T(8,128)(2,1)} %bitcast.4.refs_1_), custom_call_target="tpu_custom_call", output_to_operand_aliasing={{}: (0, {})} | custom-call | bytes 3145728 | tf_op jit(solution)/shard_map/pallas_call | solution.py:228
  (3 shorter events, 0.1 us)
Async XLA Ops:
  3.0 8.8 %copy-start.4 = (s32[256,5,2]{0,2,1:T(2,128)S(1)}, s32[256,5,2]{0,2,1:T(2,128)}, u32[]{:S(2)}) copy-start(s32[256,5,2]{0,2,1:T(2,128)} %param.6) | copy-start | bytes 30724
  3.0 47.6 %all-to-all-start = ((bf16[32,200,128]{2,1,0:T(8,128)(2,1)}), bf16[32,200,128]{2,1,0:T(8,128)(2,1)}, u32[]{:S(2)}, u32[]{:S(2)}) async-start(bf16[32,200,128]{2,1,0:T(8,128)(2,1)} %shard_map.46), calls=%async_computation | async-start | bytes 3276800 | tf_op jit(solution)/shard_map/all_to_all | solution.py:256
  11.5 3.9 %collective-permute-start = (bf16[64,32,128]{2,1,0:T(8,128)(2,1)S(1)}, bf16[64,32,128]{2,1,0:T(8,128)(2,1)}, u32[]{:S(2)}, u32[]{:S(2)}) collective-permute-start(bf16[64,32,128]{2,1,0:T(8,128)(2,1)S(1)} %slice.17.own_ref), channel_id=1, source_target_pairs={{0,1},{1,0},{2,3},{3,2},{4,5},{5,4},{6,7},{7,6},{8,9},{9,8},{10,11... | collective-permute-start | bytes 1572872 | tf_op jit(solution)/shard_map/ppermute | solution.py:260
  12.2 3.3 %copy-start.3 = (s32[5]{0:T(128)S(1)}, s32[5]{0:T(128)}, u32[]{:S(2)}) copy-start(s32[5]{0:T(128)} %order_ref.17) | copy-start | bytes 64
  18.3 13.4 %collective-permute-start.1 = (bf16[32,32,128]{2,1,0:T(8,128)(2,1)S(1)}, bf16[32,32,128]{2,1,0:T(8,128)(2,1)S(1)}, u32[]{:S(2)}, u32[]{:S(2)}) collective-permute-start(bf16[32,32,128]{2,1,0:T(8,128)(2,1)S(1)} %get-tuple-element.17.own_ref), channel_id=1, source_target_pairs={{0,2},{1,3},{2,0},{3,1},{4,6},{5,7},{6,4},{7,5},{8,10},{9,11},{10,... | collective-permute-start | bytes 786440 | tf_op jit(solution)/shard_map/ppermute | solution.py:260
  20.0 20.0 %collective-permute-start.3 = (bf16[32,32,128]{2,1,0:T(8,128)(2,1)S(1)}, bf16[32,32,128]{2,1,0:T(8,128)(2,1)S(1)}, u32[]{:S(2)}, u32[]{:S(2)}) collective-permute-start(bf16[32,32,128]{2,1,0:T(8,128)(2,1)S(1)} %get-tuple-element.18.own_ref), channel_id=1, source_target_pairs={{0,2},{1,3},{2,0},{3,1},{4,6},{5,7},{6,4},{7,5},{8,10},{9,11},{10,... | collective-permute-start | bytes 786440 | tf_op jit(solution)/shard_map/ppermute | solution.py:260
  32.8 14.5 %collective-permute-start.2 = (bf16[32,32,128]{2,1,0:T(8,128)(2,1)S(1)}, bf16[32,32,128]{2,1,0:T(8,128)(2,1)S(1)}, u32[]{:S(2)}, u32[]{:S(2)}) collective-permute-start(bf16[32,32,128]{2,1,0:T(8,128)(2,1)S(1)} %shard_map.49.own_ref), channel_id=1, source_target_pairs={{0,4},{1,5},{2,6},{3,7},{4,0},{5,1},{6,2},{7,3},{8,12},{9,13},{10,... | collective-permute-start | bytes 786440 | tf_op jit(solution)/shard_map/ppermute | solution.py:260
  41.2 16.6 %collective-permute-start.4 = (bf16[32,32,128]{2,1,0:T(8,128)(2,1)S(1)}, bf16[32,32,128]{2,1,0:T(8,128)(2,1)S(1)}, u32[]{:S(2)}, u32[]{:S(2)}) collective-permute-start(bf16[32,32,128]{2,1,0:T(8,128)(2,1)S(1)} %shard_map.51.own_ref), channel_id=1, source_target_pairs={{0,4},{1,5},{2,6},{3,7},{4,0},{5,1},{6,2},{7,3},{8,12},{9,13},{10,... | collective-permute-start | bytes 786440 | tf_op jit(solution)/shard_map/ppermute | solution.py:260
  48.5 21.8 %collective-permute-start.5 = (bf16[32,32,128]{2,1,0:T(8,128)(2,1)S(1)}, bf16[32,32,128]{2,1,0:T(8,128)(2,1)}, u32[]{:S(2)}, u32[]{:S(2)}) collective-permute-start(bf16[32,32,128]{2,1,0:T(8,128)(2,1)S(1)} %shard_map.50), channel_id=1, source_target_pairs={{0,8},{1,9},{2,10},{3,11},{4,12},{5,13},{6,14},{7,15},{8,0},{9,1},... | collective-permute-start | bytes 786440 | tf_op jit(solution)/shard_map/ppermute | solution.py:260
  57.8 0.7 copy-start.1
  58.5 0.9 copy-start.2
  60.6 15.3 %collective-permute-start.6 = (bf16[32,32,128]{2,1,0:T(8,128)(2,1)S(1)}, bf16[32,32,128]{2,1,0:T(8,128)(2,1)S(1)}, u32[]{:S(2)}, u32[]{:S(2)}) collective-permute-start(bf16[32,32,128]{2,1,0:T(8,128)(2,1)S(1)} %shard_map.52), channel_id=1, source_target_pairs={{0,8},{1,9},{2,10},{3,11},{4,12},{5,13},{6,14},{7,15},{8,0},{9,1},... | collective-permute-start | bytes 786440 | tf_op jit(solution)/shard_map/ppermute | solution.py:260
  69.2 1.1 copy-start
  70.3 44.3 %all-to-all-start.1 = ((bf16[32,6,32,128]{3,2,1,0:T(8,128)(2,1)}), bf16[32,6,32,128]{3,2,1,0:T(8,128)(2,1)}, u32[]{:S(2)}, u32[]{:S(2)}) async-start(bf16[32,6,32,128]{3,2,1,0:T(8,128)(2,1)} %copy-done), calls=%async_computation.1 | async-start | bytes 3145728 | tf_op jit(solution)/shard_map/all_to_all | solution.py:256
  78.6 25.0 %collective-permute-start.7 = (bf16[64,32,128]{2,1,0:T(8,128)(2,1)S(1)}, bf16[64,32,128]{2,1,0:T(8,128)(2,1)S(1)}, u32[]{:S(2)}, u32[]{:S(2)}) collective-permute-start(bf16[64,32,128]{2,1,0:T(8,128)(2,1)S(1)} %shard_map.54.own_ref), channel_id=1, source_target_pairs={{0,16},{16,0},{1,17},{17,1},{2,18},{18,2},{3,19},{19,3},{4,20},{20... | collective-permute-start | bytes 1572872 | tf_op jit(solution)/shard_map/ppermute | solution.py:260

commit v5 on v3

--- a/solution.py
+++ b/solution.py
@@ -76,7 +76,7 @@
     )(order, index, payload, table)
 
 
-def pack_kernel(units, vectors_ref, index_ref, out_ref, held, in_sems, out_sems):
+def pack_kernel(units, vectors_ref, far_index_ref, out_ref, held, index_ref, index_sem, in_sems, out_sems):
     devices, rows, rank = out_ref.shape
     rhs = vectors_ref.shape[1]
     levels, _, blocks = index_ref.shape
@@ -92,6 +92,9 @@
     ]
     for copy in inward:
         copy.start()
+    fetch = pltpu.make_async_copy(far_index_ref, index_ref, index_sem)
+    fetch.start()
+    fetch.wait()
 
     def pick(shape, condition):
         first, second = (lax.broadcasted_iota(jnp.int32, shape, dim) for dim in (0, 1))
@@ -133,10 +136,11 @@
     parts = 8
     return pl.pallas_call(
         functools.partial(pack_kernel, units),
-        in_specs=[pl.BlockSpec(memory_space=pltpu.HBM), pl.BlockSpec(memory_space=pltpu.VMEM)],
+        in_specs=[pl.BlockSpec(memory_space=pltpu.HBM)] * 2,
         out_specs=pl.BlockSpec(memory_space=pltpu.HBM),
         out_shape=jax.ShapeDtypeStruct(shape, jnp.bfloat16),
-        scratch_shapes=[pltpu.VMEM(shape, jnp.bfloat16)] + [pltpu.SemaphoreType.DMA((parts,))] * 2,
+        scratch_shapes=[pltpu.VMEM(shape, jnp.bfloat16), pltpu.VMEM((levels, 2, blocks), jnp.int32)]
+        + [pltpu.SemaphoreType.DMA] + [pltpu.SemaphoreType.DMA((parts,))] * 2,
         compiler_params=PACK_PARAMS,
         cost_estimate=pl.CostEstimate(flops=0, bytes_accessed=4 * vectors.size, transcendentals=0),
     )(vectors, jnp.transpose(factor_index, (1, 2, 0)))
@@ -182,7 +186,7 @@
     out_ref = refs[aliased + count]
     held, in_sems, out_sem = refs[aliased + count + 1 :]
     total = held.shape[0]
-    step = math.gcd(32, *(piece.shape[0] for piece in pieces))
+    step = math.gcd(16, *(piece.shape[0] for piece in pieces))
     moves = []
     for piece, offset in zip(pieces, offsets):
         for first in range(0, piece.shape[0], step):
@@ -211,7 +215,7 @@
         out_shape=jax.ShapeDtypeStruct(shape, jnp.bfloat16),
         scratch_shapes=[
             pltpu.VMEM((total,) + shape[1:], jnp.bfloat16),
-            pltpu.SemaphoreType.DMA((total // math.gcd(32, *(p.shape[0] for p in pieces)),)),
+            pltpu.SemaphoreType.DMA((total // math.gcd(16, *(p.shape[0] for p in pieces)),)),
             pltpu.SemaphoreType.DMA,
         ],
         input_output_aliases={0: 0} if aliased else {},

time: 116 us -> 117 us (level)
  transfers between devices with their start and end apart: 10 -> 10, of which waited for: 5 -> 5; matrix products, arithmetic and copies ran while one was open for 6% -> 6% of each run, Pallas kernels for 21% -> 22%
where the time goes in v5:
time: 117 us; the launch traced here: 116 us
  waiting for transfers between devices  51.4 us (44%)
  Pallas kernels  30.5 us (26%)
  starting transfers between devices  24.4 us (21%)
  local copies, waits for them, and re-layouts  8.39 us (7%)
    ppermute x8, waiting for transfers between devices, partner(): lax.ppermute(array, axis, [(i, i ^ 1 << bit) for i in range(lax.axis_size...  43.6 us
    all_to_all x2, starting transfers between devices, exchange(): return lax.all_to_all(array, AXES, split_axis=0, concat_axis=0, tiled=True)  13 us
    pallas_call x2, Pallas kernels, apply_levels(): pl.pallas_call(functools.partial(levels_kernel, some), grid_spec=pltpu.Pr...  12.9 us
    ppermute x8, starting transfers between devices, partner(): lax.ppermute(array, axis, [(i, i ^ 1 << bit) for i in range(lax.axis_size...  11.5 us
    pallas_call x7, Pallas kernels, apply_level(): pl.pallas_call(functools.partial(one_level_kernel, level, offset), grid_s...  10.7 us
    all_to_all x2, waiting for transfers between devices, exchange(): return lax.all_to_all(array, AXES, split_axis=0, concat_axis=0, tiled=True)  7.74 us
    unnamed x11, local copies, waits for them, and re-layouts  6.04 us
    pallas_call x2, Pallas kernels, place(): pl.pallas_call(functools.partial(place_kernel, offsets, aliased), in_spec...  3.73 us
  transfers between devices with their start and end apart: 10, of which 5 were waited for; matrix products, arithmetic and copies ran while one was open for 6% of the time, Pallas kernels for 22%

profile of v5, /device:TPU:0, one launch (start us, length us, event | category | flops | bytes accessed | tf_op | source)
XLA Modules:
  0.0 115.9 jit_solution(4839582312265472002)
XLA Ops:
  0.0 3.1 %shard_map.46 = bf16[32,200,128]{2,1,0:T(8,128)(2,1)} custom-call(bf16[256,32,128]{2,1,0:T(8,128)(2,1)} %vectors_ref.1, s32[5,2,256]{2,1,0:T(2,128)} %bitcast.17), custom_call_target="tpu_custom_call" | custom-call | bytes 4194304 | tf_op jit(solution)/shard_map/pallas_call | solution.py:137
  3.1 0.0 copy-start.4
  3.2 7.4 %all-to-all-start = ((bf16[32,200,128]{2,1,0:T(8,128)(2,1)}), bf16[32,200,128]{2,1,0:T(8,128)(2,1)}, u32[]{:S(2)}, u32[]{:S(2)}) async-start(bf16[32,200,128]{2,1,0:T(8,128)(2,1)} %shard_map.46), calls=%async_computation | async-start | bytes 3276800 | tf_op jit(solution)/shard_map/all_to_all | solution.py:239
  10.6 1.1 slice.17.own_ref
  11.7 0.3 collective-permute-start
  11.9 0.0 copy-done.4
  11.9 0.1 slice.16
  12.0 0.2 copy.15
  12.2 0.1 reshape.8.index_ref
  12.3 0.0 copy-start.3
  12.3 3.2 %copy.14 = bf16[5,16,128,128]{2,3,1,0:T(8,128)(2,1)S(1)} copy(bf16[5,16,128,128]{3,2,1,0:T(8,128)(2,1)} %param.5) | data formatting | bytes 5242880 | tf_op args[1]
  15.6 0.0 collective-permute-done.other_ref
  15.6 0.0 copy-done.3
  15.6 2.7 %shard_map.48 = bf16[64,32,128]{2,1,0:T(8,128)(2,1)S(1)} custom-call(s32[5]{0:T(128)S(1)} %copy-done.3, s32[640]{0:T(1024)S(1)} %reshape.8.index_ref, bf16[64,32,128]{2,1,0:T(8,128)(2,1)S(1)} %slice.17.own_ref, bf16[64,32,128]{2,1,0:T(8,128)(2,1)} %collective-permute-done.other_ref, bf16[5,16,128,128]{3,2,1,0:T(8,128)(2,1)S(1)} %bitcast.8), custom_call_target="tpu_custom_call" | custom-call | flops 939524096 | bytes 4194304 | tf_op jit(solution)/shard_map/pallas_call | solution.py:165
  18.4 1.7 %collective-permute-start.1 = (bf16[32,32,128]{2,1,0:T(8,128)(2,1)S(1)}, bf16[32,32,128]{2,1,0:T(8,128)(2,1)S(1)}, u32[]{:S(2)}, u32[]{:S(2)}) collective-permute-start(bf16[32,32,128]{2,1,0:T(8,128)(2,1)S(1)} %get-tuple-element.17.own_ref), channel_id=1, source_target_pairs={{0,2},{1,3},{2,0},{3,1},{4,6},{5,7},{6,4},{7,5},{8,10},{9,11},{10,... | collective-permute-start | bytes 786440 | tf_op jit(solution)/shard_map/ppermute | solution.py:243
  20.1 0.3 collective-permute-start.3
  20.5 11.3 %collective-permute-done.1.other_ref = bf16[32,32,128]{2,1,0:T(8,128)(2,1)S(1)} collective-permute-done((bf16[32,32,128]{2,1,0:T(8,128)(2,1)S(1)}, bf16[32,32,128]{2,1,0:T(8,128)(2,1)S(1)}, u32[]{:S(2)}, u32[]{:S(2)}) %collective-permute-start.1) | collective-permute-done | bytes 262176 | tf_op jit(solution)/shard_map/ppermute | solution.py:243
  31.8 1.1 shard_map.49.own_ref
  33.0 1.9 %collective-permute-start.2 = (bf16[32,32,128]{2,1,0:T(8,128)(2,1)S(1)}, bf16[32,32,128]{2,1,0:T(8,128)(2,1)S(1)}, u32[]{:S(2)}, u32[]{:S(2)}) collective-permute-start(bf16[32,32,128]{2,1,0:T(8,128)(2,1)S(1)} %shard_map.49.own_ref), channel_id=1, source_target_pairs={{0,4},{1,5},{2,6},{3,7},{4,0},{5,1},{6,2},{7,3},{8,12},{9,13},{10,... | collective-permute-start | bytes 786440 | tf_op jit(solution)/shard_map/ppermute | solution.py:243
  34.9 5.3 %collective-permute-done.3.other_ref = bf16[32,32,128]{2,1,0:T(8,128)(2,1)S(1)} collective-permute-done((bf16[32,32,128]{2,1,0:T(8,128)(2,1)S(1)}, bf16[32,32,128]{2,1,0:T(8,128)(2,1)S(1)}, u32[]{:S(2)}, u32[]{:S(2)}) %collective-permute-start.3) | collective-permute-done | bytes 262176 | tf_op jit(solution)/shard_map/ppermute | solution.py:243
  40.2 1.1 shard_map.51.own_ref
  41.3 2.4 %collective-permute-start.4 = (bf16[32,32,128]{2,1,0:T(8,128)(2,1)S(1)}, bf16[32,32,128]{2,1,0:T(8,128)(2,1)S(1)}, u32[]{:S(2)}, u32[]{:S(2)}) collective-permute-start(bf16[32,32,128]{2,1,0:T(8,128)(2,1)S(1)} %shard_map.51.own_ref), channel_id=1, source_target_pairs={{0,4},{1,5},{2,6},{3,7},{4,0},{5,1},{6,2},{7,3},{8,12},{9,13},{10,... | collective-permute-start | bytes 786440 | tf_op jit(solution)/shard_map/ppermute | solution.py:243
  43.7 3.7 %collective-permute-done.2.other_ref = bf16[32,32,128]{2,1,0:T(8,128)(2,1)S(1)} collective-permute-done((bf16[32,32,128]{2,1,0:T(8,128)(2,1)S(1)}, bf16[32,32,128]{2,1,0:T(8,128)(2,1)S(1)}, u32[]{:S(2)}, u32[]{:S(2)}) %collective-permute-start.2) | collective-permute-done | bytes 262176 | tf_op jit(solution)/shard_map/ppermute | solution.py:243
  47.5 1.1 shard_map.50
  48.6 2.2 %collective-permute-start.5 = (bf16[32,32,128]{2,1,0:T(8,128)(2,1)S(1)}, bf16[32,32,128]{2,1,0:T(8,128)(2,1)}, u32[]{:S(2)}, u32[]{:S(2)}) collective-permute-start(bf16[32,32,128]{2,1,0:T(8,128)(2,1)S(1)} %shard_map.50), channel_id=1, source_target_pairs={{0,8},{1,9},{2,10},{3,11},{4,12},{5,13},{6,14},{7,15},{8,0},{9,1},... | collective-permute-start | bytes 786440 | tf_op jit(solution)/shard_map/ppermute | solution.py:243
  50.8 0.0 all-to-all-done.field_ref
  50.8 0.9 slice.20
  51.7 6.2 %shard_map.47.field_ref = bf16[32,6,32,128]{3,2,1,0:T(8,128)(2,1)S(1)} custom-call(s32[5]{0:T(128)S(1)} %copy-done.3, s32[32,128]{1,0:T(8,128)S(1)} %fusion.index_ref, bf16[32,200,128]{2,1,0:T(8,128)(2,1)} %all-to-all-done.field_ref, bf16[5,16,128,128]{3,2,1,0:T(8,128)(2,1)S(1)} %bitcast.12), custom_call_target="tpu_custom_call" | custom-call | flops 805306368 | bytes 5767168 | tf_op jit(solution)/shard_map/pallas_call | solution.py:60
  57.9 0.0 collective-permute-done.4.other_ref
  57.9 0.0 copy-start.1
  57.9 0.7 copy-done.1
  58.6 0.0 copy-start.2
  58.6 0.9 copy-done.2
  59.5 1.1 shard_map.52
  60.7 0.9 collective-permute-start.6
  61.6 6.7 %shard_map.53 = bf16[32,6,32,128]{3,2,1,0:T(8,128)(2,1)S(1)} custom-call(s32[5]{0:T(128)S(1)} %copy-done.3, s32[32,128]{1,0:T(8,128)S(1)} %fusion.index_ref, bf16[32,6,32,128]{3,2,1,0:T(8,128)(2,1)S(1)} %shard_map.47.field_ref, bf16[5,16,128,128]{3,2,1,0:T(8,128)(2,1)S(1)} %bitcast.14), custom_call_target="tpu_custom_call" | custom-call | flops 1207959552 | bytes 5767168 | tf_op jit(solution)/shard_map/pallas_call | solution.py:60
  68.3 0.0 copy-start
  68.3 1.1 copy-done
  69.4 0.0 collective-permute-done.5
  69.4 5.5 %all-to-all-start.1 = ((bf16[32,6,32,128]{3,2,1,0:T(8,128)(2,1)}), bf16[32,6,32,128]{3,2,1,0:T(8,128)(2,1)}, u32[]{:S(2)}, u32[]{:S(2)}) async-start(bf16[32,6,32,128]{3,2,1,0:T(8,128)(2,1)} %copy-done), calls=%async_computation.1 | async-start | bytes 3145728 | tf_op jit(solution)/shard_map/all_to_all | solution.py:239
  75.0 0.0 collective-permute-done.6
  75.1 1.0 pad_maximum_fusion.1.other_ref
  76.1 1.7 %shard_map.54.own_ref = bf16[64,32,128]{2,1,0:T(8,128)(2,1)S(1)} custom-call(s32[5]{0:T(128)S(1)} %copy-done.3, s32[640]{0:T(1024)S(1)} %reshape.8.index_ref, bf16[64,32,128]{2,1,0:T(8,128)(2,1)S(1)} %pad_maximum_fusion.own_ref, bf16[64,32,128]{2,1,0:T(8,128)(2,1)S(1)} %pad_maximum_fusion.1.other_ref, bf16[5,16,128,128]{3,2,1,0:T(8,128)(2,1)S(1)} %bitcast.15), custom_call_target="tpu_custom_call" | custom-call | flops 46976204800 | bytes 4194304 | tf_op jit(solution)/shard_map/pallas_call | solution.py:165
  77.8 1.8 %collective-permute-start.7 = (bf16[64,32,128]{2,1,0:T(8,128)(2,1)S(1)}, bf16[64,32,128]{2,1,0:T(8,128)(2,1)S(1)}, u32[]{:S(2)}, u32[]{:S(2)}) collective-permute-start(bf16[64,32,128]{2,1,0:T(8,128)(2,1)S(1)} %shard_map.54.own_ref), channel_id=1, source_target_pairs={{0,16},{16,0},{1,17},{17,1},{2,18},{18,2},{3,19},{19,3},{4,20},{20... | collective-permute-start | bytes 1572872 | tf_op jit(solution)/shard_map/ppermute | solution.py:243
  79.5 23.2 %collective-permute-done.7.other_ref = bf16[64,32,128]{2,1,0:T(8,128)(2,1)S(1)} collective-permute-done((bf16[64,32,128]{2,1,0:T(8,128)(2,1)S(1)}, bf16[64,32,128]{2,1,0:T(8,128)(2,1)S(1)}, u32[]{:S(2)}, u32[]{:S(2)}) %collective-permute-start.7) | collective-permute-done | bytes 524320 | tf_op jit(solution)/shard_map/ppermute | solution.py:243
  102.8 1.7 %shard_map.55.refs_0_ = bf16[64,32,128]{2,1,0:T(8,128)(2,1)S(1)} custom-call(s32[5]{0:T(128)S(1)} %copy-done.3, s32[640]{0:T(1024)S(1)} %reshape.8.index_ref, bf16[64,32,128]{2,1,0:T(8,128)(2,1)S(1)} %shard_map.54.own_ref, bf16[64,32,128]{2,1,0:T(8,128)(2,1)S(1)} %collective-permute-done.7.other_ref, bf16[5,16,128,128]{3,2,1,0:T(8,128)(2,1)S(1)} %bitcast.16), custom_call_target="tpu_custom_call" | custom-call | flops 939524096 | bytes 4194304 | tf_op jit(solution)/shard_map/pallas_call | solution.py:165
  104.5 1.5 %shard_map.56.refs_0_ = bf16[256,32,128]{2,1,0:T(8,128)(2,1)} custom-call(bf16[64,32,128]{2,1,0:T(8,128)(2,1)S(1)} %shard_map.55.refs_0_), custom_call_target="tpu_custom_call" | custom-call | bytes 1048576 | tf_op jit(solution)/shard_map/pallas_call | solution.py:211
  106.0 7.7 %all-to-all-done.1 = bf16[32,6,32,128]{3,2,1,0:T(8,128)(2,1)} async-done(((bf16[32,6,32,128]{3,2,1,0:T(8,128)(2,1)}), bf16[32,6,32,128]{3,2,1,0:T(8,128)(2,1)}, u32[]{:S(2)}, u32[]{:S(2)}) %all-to-all-start.1) | async-done | bytes 1572896 | tf_op jit(solution)/shard_map/all_to_all | solution.py:239
  113.7 2.2 %shard_map.57 = bf16[256,32,128]{2,1,0:T(8,128)(2,1)} custom-call(bf16[256,32,128]{2,1,0:T(8,128)(2,1)} %shard_map.56.refs_0_, bf16[192,32,128]{2,1,0:T(8,128)(2,1)} %bitcast.4.refs_1_), custom_call_target="tpu_custom_call", output_to_operand_aliasing={{}: (0, {})} | custom-call | bytes 3145728 | tf_op jit(solution)/shard_map/pallas_call | solution.py:211
  (3 shorter events, 0.1 us)
Async XLA Ops:
  3.1 8.8 %copy-start.4 = (s32[256,5,2]{0,2,1:T(2,128)S(1)}, s32[256,5,2]{0,2,1:T(2,128)}, u32[]{:S(2)}) copy-start(s32[256,5,2]{0,2,1:T(2,128)} %param.6) | copy-start | bytes 30724
  3.2 47.6 %all-to-all-start = ((bf16[32,200,128]{2,1,0:T(8,128)(2,1)}), bf16[32,200,128]{2,1,0:T(8,128)(2,1)}, u32[]{:S(2)}, u32[]{:S(2)}) async-start(bf16[32,200,128]{2,1,0:T(8,128)(2,1)} %shard_map.46), calls=%async_computation | async-start | bytes 3276800 | tf_op jit(solution)/shard_map/all_to_all | solution.py:239
  11.7 3.9 %collective-permute-start = (bf16[64,32,128]{2,1,0:T(8,128)(2,1)S(1)}, bf16[64,32,128]{2,1,0:T(8,128)(2,1)}, u32[]{:S(2)}, u32[]{:S(2)}) collective-permute-start(bf16[64,32,128]{2,1,0:T(8,128)(2,1)S(1)} %slice.17.own_ref), channel_id=1, source_target_pairs={{0,1},{1,0},{2,3},{3,2},{4,5},{5,4},{6,7},{7,6},{8,9},{9,8},{10,11... | collective-permute-start | bytes 1572872 | tf_op jit(solution)/shard_map/ppermute | solution.py:243
  12.3 3.3 %copy-start.3 = (s32[5]{0:T(128)S(1)}, s32[5]{0:T(128)}, u32[]{:S(2)}) copy-start(s32[5]{0:T(128)} %order_ref.17) | copy-start | bytes 64
  18.4 13.4 %collective-permute-start.1 = (bf16[32,32,128]{2,1,0:T(8,128)(2,1)S(1)}, bf16[32,32,128]{2,1,0:T(8,128)(2,1)S(1)}, u32[]{:S(2)}, u32[]{:S(2)}) collective-permute-start(bf16[32,32,128]{2,1,0:T(8,128)(2,1)S(1)} %get-tuple-element.17.own_ref), channel_id=1, source_target_pairs={{0,2},{1,3},{2,0},{3,1},{4,6},{5,7},{6,4},{7,5},{8,10},{9,11},{10,... | collective-permute-start | bytes 786440 | tf_op jit(solution)/shard_map/ppermute | solution.py:243
  20.1 20.0 %collective-permute-start.3 = (bf16[32,32,128]{2,1,0:T(8,128)(2,1)S(1)}, bf16[32,32,128]{2,1,0:T(8,128)(2,1)S(1)}, u32[]{:S(2)}, u32[]{:S(2)}) collective-permute-start(bf16[32,32,128]{2,1,0:T(8,128)(2,1)S(1)} %get-tuple-element.18.own_ref), channel_id=1, source_target_pairs={{0,2},{1,3},{2,0},{3,1},{4,6},{5,7},{6,4},{7,5},{8,10},{9,11},{10,... | collective-permute-start | bytes 786440 | tf_op jit(solution)/shard_map/ppermute | solution.py:243
  33.0 14.5 %collective-permute-start.2 = (bf16[32,32,128]{2,1,0:T(8,128)(2,1)S(1)}, bf16[32,32,128]{2,1,0:T(8,128)(2,1)S(1)}, u32[]{:S(2)}, u32[]{:S(2)}) collective-permute-start(bf16[32,32,128]{2,1,0:T(8,128)(2,1)S(1)} %shard_map.49.own_ref), channel_id=1, source_target_pairs={{0,4},{1,5},{2,6},{3,7},{4,0},{5,1},{6,2},{7,3},{8,12},{9,13},{10,... | collective-permute-start | bytes 786440 | tf_op jit(solution)/shard_map/ppermute | solution.py:243
  41.3 16.6 %collective-permute-start.4 = (bf16[32,32,128]{2,1,0:T(8,128)(2,1)S(1)}, bf16[32,32,128]{2,1,0:T(8,128)(2,1)S(1)}, u32[]{:S(2)}, u32[]{:S(2)}) collective-permute-start(bf16[32,32,128]{2,1,0:T(8,128)(2,1)S(1)} %shard_map.51.own_ref), channel_id=1, source_target_pairs={{0,4},{1,5},{2,6},{3,7},{4,0},{5,1},{6,2},{7,3},{8,12},{9,13},{10,... | collective-permute-start | bytes 786440 | tf_op jit(solution)/shard_map/ppermute | solution.py:243
  48.6 20.8 %collective-permute-start.5 = (bf16[32,32,128]{2,1,0:T(8,128)(2,1)S(1)}, bf16[32,32,128]{2,1,0:T(8,128)(2,1)}, u32[]{:S(2)}, u32[]{:S(2)}) collective-permute-start(bf16[32,32,128]{2,1,0:T(8,128)(2,1)S(1)} %shard_map.50), channel_id=1, source_target_pairs={{0,8},{1,9},{2,10},{3,11},{4,12},{5,13},{6,14},{7,15},{8,0},{9,1},... | collective-permute-start | bytes 786440 | tf_op jit(solution)/shard_map/ppermute | solution.py:243
  57.9 0.7 copy-start.1
  58.6 0.9 copy-start.2
  60.7 14.4 %collective-permute-start.6 = (bf16[32,32,128]{2,1,0:T(8,128)(2,1)S(1)}, bf16[32,32,128]{2,1,0:T(8,128)(2,1)S(1)}, u32[]{:S(2)}, u32[]{:S(2)}) collective-permute-start(bf16[32,32,128]{2,1,0:T(8,128)(2,1)S(1)} %shard_map.52), channel_id=1, source_target_pairs={{0,8},{1,9},{2,10},{3,11},{4,12},{5,13},{6,14},{7,15},{8,0},{9,1},... | collective-permute-start | bytes 786440 | tf_op jit(solution)/shard_map/ppermute | solution.py:243
  68.3 1.1 copy-start
  69.4 44.3 %all-to-all-start.1 = ((bf16[32,6,32,128]{3,2,1,0:T(8,128)(2,1)}), bf16[32,6,32,128]{3,2,1,0:T(8,128)(2,1)}, u32[]{:S(2)}, u32[]{:S(2)}) async-start(bf16[32,6,32,128]{3,2,1,0:T(8,128)(2,1)} %copy-done), calls=%async_computation.1 | async-start | bytes 3145728 | tf_op jit(solution)/shard_map/all_to_all | solution.py:239
  77.8 25.0 %collective-permute-start.7 = (bf16[64,32,128]{2,1,0:T(8,128)(2,1)S(1)}, bf16[64,32,128]{2,1,0:T(8,128)(2,1)S(1)}, u32[]{:S(2)}, u32[]{:S(2)}) collective-permute-start(bf16[64,32,128]{2,1,0:T(8,128)(2,1)S(1)} %shard_map.54.own_ref), channel_id=1, source_target_pairs={{0,16},{16,0},{1,17},{17,1},{2,18},{18,2},{3,19},{19,3},{4,20},{20... | collective-permute-start | bytes 1572872 | tf_op jit(solution)/shard_map/ppermute | solution.py:243

commit v6 on v3

--- a/solution.py
+++ b/solution.py
@@ -256,16 +256,14 @@
             second = near_level(second, level, offset=half)
         first_other = partner(first, last_middle)
         second_other = partner(second, last_middle - 1)
+    if units > far_units:
+        second = near_level(second, last_middle - 1, second_other, offset=half)
+        arrived, second = lax.optimization_barrier((arrived, second))
+        second_other = partner(second, last_middle)
     index = arrived[:, far_units * rhs].astype(jnp.int32)
+    far = apply_levels(range(levels), arrived, far_units, rhs, table, index, level_order)
     if units == far_units:
-        far = apply_levels(range(levels), arrived, far_units, rhs, table, index, level_order)
         return exchange(far).reshape(vectors.shape)
-    far = apply_levels(range(2), arrived, far_units, rhs, table, index, level_order)
-    far, near_index = lax.optimization_barrier((far, near_index))
-    second = near_level(second, last_middle - 1, second_other, offset=half)
-    far, second = lax.optimization_barrier((far, second))
-    second_other = partner(second, last_middle)
-    far = apply_levels(range(2, levels), far, far_units, rhs, table, index, level_order)
     far, first_other = lax.optimization_barrier((far, first_other))
     far = exchange(far).reshape(spread, rhs, rank)
     near = near_level(

time: 116 us -> 118 us (1.017)
  waiting for transfers between devices: 52 us -> 57.4 us
  local copies, waits for them, and re-layouts: 8.39 us -> 5.88 us
  starting transfers between devices: 24.4 us -> 23 us
    ppermute x8, waiting for transfers between devices: 43.6 us -> 49.1 us  [partner(): lax.ppermute(array, axis, [(i, i ^ 1 << bit) for i in range(lax.axis_size...]
    unnamed x11 -> x7, local copies, waits for them, and re-layouts: 6.04 us -> 4.39 us
    pallas_call x2 -> x1, Pallas kernels: 12.9 us -> 12.1 us  [apply_levels(): pl.pallas_call(functools.partial(levels_kernel, some), grid_spec=pltpu.Pr...]
  transfers between devices with their start and end apart: 10 -> 10, of which waited for: 5 -> 6; matrix products, arithmetic and copies ran while one was open for 6% -> 6% of each run, Pallas kernels for 21% -> 20%
where the time goes in v6:
time: 118 us; the launch traced here: 117 us
  waiting for transfers between devices  57.4 us (49%)
  Pallas kernels  28.8 us (24%)
  starting transfers between devices  23 us (19%)
  local copies, waits for them, and re-layouts  5.88 us (5%)
  other arithmetic  1.9 us (2%)
    ppermute x8, waiting for transfers between devices, partner(): lax.ppermute(array, axis, [(i, i ^ 1 << bit) for i in range(lax.axis_size...  49.1 us
    all_to_all x2, starting transfers between devices, exchange(): return lax.all_to_all(array, AXES, split_axis=0, concat_axis=0, tiled=True)  12.3 us
    pallas_call x1, Pallas kernels, apply_levels(): pl.pallas_call(functools.partial(levels_kernel, some), grid_spec=pltpu.Pr...  12.1 us
    pallas_call x7, Pallas kernels, apply_level(): pl.pallas_call(functools.partial(one_level_kernel, level, offset), grid_s...  10.7 us
    ppermute x8, starting transfers between devices, partner(): lax.ppermute(array, axis, [(i, i ^ 1 << bit) for i in range(lax.axis_size...  10.7 us
    all_to_all x2, waiting for transfers between devices, exchange(): return lax.all_to_all(array, AXES, split_axis=0, concat_axis=0, tiled=True)  8.37 us
    unnamed x7, local copies, waits for them, and re-layouts  4.39 us
    pallas_call x1, Pallas kernels, pack(): pl.pallas_call(functools.partial(pack_kernel, units), in_specs=[pl.BlockS...  3.01 us
  transfers between devices with their start and end apart: 10, of which 6 were waited for; matrix products, arithmetic and copies ran while one was open for 6% of the time, Pallas kernels for 20%

profile of v6, /device:TPU:0, one launch (start us, length us, event | category | flops | bytes accessed | tf_op | source)
XLA Modules:
  0.0 117.2 jit_solution(15446444105351613508)
XLA Ops:
  0.0 3.0 %shard_map.49 = bf16[32,200,128]{2,1,0:T(8,128)(2,1)} custom-call(bf16[256,32,128]{2,1,0:T(8,128)(2,1)} %vectors_ref.1, s32[5,2,256]{2,1,0:T(2,128)} %bitcast.13), custom_call_target="tpu_custom_call" | custom-call | bytes 4194304 | tf_op jit(solution)/shard_map/pallas_call | solution.py:134
  3.0 0.0 copy-start.2
  3.0 7.4 %all-to-all-start = ((bf16[32,200,128]{2,1,0:T(8,128)(2,1)}), bf16[32,200,128]{2,1,0:T(8,128)(2,1)}, u32[]{:S(2)}, u32[]{:S(2)}) async-start(bf16[32,200,128]{2,1,0:T(8,128)(2,1)} %shard_map.49), calls=%async_computation | async-start | bytes 3276800 | tf_op jit(solution)/shard_map/all_to_all | solution.py:235
  10.5 1.1 slice.16.own_ref
  11.5 0.3 collective-permute-start
  11.8 0.0 copy-done.2
  11.8 0.1 slice.15
  11.9 0.0 copy-start.1
  11.9 3.3 %copy.8 = bf16[5,16,128,128]{2,3,1,0:T(8,128)(2,1)S(1)} copy(bf16[5,16,128,128]{3,2,1,0:T(8,128)(2,1)} %param.5) | data formatting | bytes 5242880 | tf_op args[1]
  15.1 0.2 copy.7
  15.3 0.1 reshape.8.index_ref
  15.4 0.0 collective-permute-done.other_ref
  15.5 0.0 copy-done.1
  15.5 2.7 %shard_map.46 = bf16[64,32,128]{2,1,0:T(8,128)(2,1)S(1)} custom-call(s32[5]{0:T(128)S(1)} %copy-done.1, s32[640]{0:T(1024)S(1)} %reshape.8.index_ref, bf16[64,32,128]{2,1,0:T(8,128)(2,1)S(1)} %slice.16.own_ref, bf16[64,32,128]{2,1,0:T(8,128)(2,1)} %collective-permute-done.other_ref, bf16[5,16,128,128]{3,2,1,0:T(8,128)(2,1)S(1)} %bitcast.4), custom_call_target="tpu_custom_call" | custom-call | flops 939524096 | bytes 4194304 | tf_op jit(solution)/shard_map/pallas_call | solution.py:161
  18.3 1.7 %collective-permute-start.1 = (bf16[32,32,128]{2,1,0:T(8,128)(2,1)S(1)}, bf16[32,32,128]{2,1,0:T(8,128)(2,1)S(1)}, u32[]{:S(2)}, u32[]{:S(2)}) collective-permute-start(bf16[32,32,128]{2,1,0:T(8,128)(2,1)S(1)} %get-tuple-element.13.own_ref), channel_id=1, source_target_pairs={{0,2},{1,3},{2,0},{3,1},{4,6},{5,7},{6,4},{7,5},{8,10},{9,11},{10,... | collective-permute-start | bytes 786440 | tf_op jit(solution)/shard_map/ppermute | solution.py:239
  20.0 0.3 collective-permute-start.3
  20.4 11.3 %collective-permute-done.1.other_ref = bf16[32,32,128]{2,1,0:T(8,128)(2,1)S(1)} collective-permute-done((bf16[32,32,128]{2,1,0:T(8,128)(2,1)S(1)}, bf16[32,32,128]{2,1,0:T(8,128)(2,1)S(1)}, u32[]{:S(2)}, u32[]{:S(2)}) %collective-permute-start.1) | collective-permute-done | bytes 262176 | tf_op jit(solution)/shard_map/ppermute | solution.py:239
  31.7 1.1 shard_map.47.own_ref
  32.9 1.9 %collective-permute-start.2 = (bf16[32,32,128]{2,1,0:T(8,128)(2,1)S(1)}, bf16[32,32,128]{2,1,0:T(8,128)(2,1)S(1)}, u32[]{:S(2)}, u32[]{:S(2)}) collective-permute-start(bf16[32,32,128]{2,1,0:T(8,128)(2,1)S(1)} %shard_map.47.own_ref), channel_id=1, source_target_pairs={{0,4},{1,5},{2,6},{3,7},{4,0},{5,1},{6,2},{7,3},{8,12},{9,13},{10,... | collective-permute-start | bytes 786440 | tf_op jit(solution)/shard_map/ppermute | solution.py:239
  34.7 5.3 %collective-permute-done.3.other_ref = bf16[32,32,128]{2,1,0:T(8,128)(2,1)S(1)} collective-permute-done((bf16[32,32,128]{2,1,0:T(8,128)(2,1)S(1)}, bf16[32,32,128]{2,1,0:T(8,128)(2,1)S(1)}, u32[]{:S(2)}, u32[]{:S(2)}) %collective-permute-start.3) | collective-permute-done | bytes 262176 | tf_op jit(solution)/shard_map/ppermute | solution.py:239
  40.0 1.1 shard_map.50.own_ref
  41.2 2.4 %collective-permute-start.4 = (bf16[32,32,128]{2,1,0:T(8,128)(2,1)S(1)}, bf16[32,32,128]{2,1,0:T(8,128)(2,1)S(1)}, u32[]{:S(2)}, u32[]{:S(2)}) collective-permute-start(bf16[32,32,128]{2,1,0:T(8,128)(2,1)S(1)} %shard_map.50.own_ref), channel_id=1, source_target_pairs={{0,4},{1,5},{2,6},{3,7},{4,0},{5,1},{6,2},{7,3},{8,12},{9,13},{10,... | collective-permute-start | bytes 786440 | tf_op jit(solution)/shard_map/ppermute | solution.py:239
  43.6 3.7 %collective-permute-done.2.other_ref = bf16[32,32,128]{2,1,0:T(8,128)(2,1)S(1)} collective-permute-done((bf16[32,32,128]{2,1,0:T(8,128)(2,1)S(1)}, bf16[32,32,128]{2,1,0:T(8,128)(2,1)S(1)}, u32[]{:S(2)}, u32[]{:S(2)}) %collective-permute-start.2) | collective-permute-done | bytes 262176 | tf_op jit(solution)/shard_map/ppermute | solution.py:239
  47.3 1.1 shard_map.48
  48.5 2.2 %collective-permute-start.5 = (bf16[32,32,128]{2,1,0:T(8,128)(2,1)S(1)}, bf16[32,32,128]{2,1,0:T(8,128)(2,1)S(1)}, u32[]{:S(2)}, u32[]{:S(2)}) collective-permute-start(bf16[32,32,128]{2,1,0:T(8,128)(2,1)S(1)} %shard_map.48), channel_id=1, source_target_pairs={{0,8},{1,9},{2,10},{3,11},{4,12},{5,13},{6,14},{7,15},{8,0},{9,1},... | collective-permute-start | bytes 786440 | tf_op jit(solution)/shard_map/ppermute | solution.py:239
  50.7 5.5 %collective-permute-done.4.other_ref = bf16[32,32,128]{2,1,0:T(8,128)(2,1)S(1)} collective-permute-done((bf16[32,32,128]{2,1,0:T(8,128)(2,1)S(1)}, bf16[32,32,128]{2,1,0:T(8,128)(2,1)S(1)}, u32[]{:S(2)}, u32[]{:S(2)}) %collective-permute-start.4) | collective-permute-done | bytes 262176 | tf_op jit(solution)/shard_map/ppermute | solution.py:239
  56.2 1.1 shard_map.51
  57.3 0.0 all-to-all-done.field_ref
  57.3 0.9 slice_convert_fusion
  58.2 0.1 collective-permute-start.6
  58.3 12.1 %shard_map.52 = bf16[32,6,32,128]{3,2,1,0:T(8,128)(2,1)S(1)} custom-call(s32[5]{0:T(128)S(1)} %copy-done.1, s32[32,128]{1,0:T(8,128)S(1)} %bitcast.12, bf16[32,200,128]{2,1,0:T(8,128)(2,1)} %all-to-all-done.field_ref, bf16[5,16,128,128]{3,2,1,0:T(8,128)(2,1)S(1)} %bitcast.9), custom_call_target="tpu_custom_call" | custom-call | flops 2013265920 | bytes 5767168 | tf_op jit(solution)/shard_map/pallas_call | solution.py:60
  70.3 0.0 copy-start
  70.4 1.1 copy-done
  71.5 0.0 collective-permute-done.5
  71.5 4.9 %all-to-all-start.1 = ((bf16[32,6,32,128]{3,2,1,0:T(8,128)(2,1)}), bf16[32,6,32,128]{3,2,1,0:T(8,128)(2,1)}, u32[]{:S(2)}, u32[]{:S(2)}) async-start(bf16[32,6,32,128]{3,2,1,0:T(8,128)(2,1)} %copy-done), calls=%async_computation.1 | async-start | bytes 3145728 | tf_op jit(solution)/shard_map/all_to_all | solution.py:235
  76.4 0.0 collective-permute-done.6
  76.4 1.0 pad_maximum_fusion.1.other_ref
  77.4 1.7 %shard_map.53.own_ref = bf16[64,32,128]{2,1,0:T(8,128)(2,1)S(1)} custom-call(s32[5]{0:T(128)S(1)} %copy-done.1, s32[640]{0:T(1024)S(1)} %reshape.8.index_ref, bf16[64,32,128]{2,1,0:T(8,128)(2,1)S(1)} %pad_maximum_fusion.own_ref, bf16[64,32,128]{2,1,0:T(8,128)(2,1)S(1)} %pad_maximum_fusion.1.other_ref, bf16[5,16,128,128]{3,2,1,0:T(8,128)(2,1)S(1)} %bitcast.10), custom_call_target="tpu_custom_call" | custom-call | flops 46976204800 | bytes 4194304 | tf_op jit(solution)/shard_map/pallas_call | solution.py:161
  79.2 1.8 %collective-permute-start.7 = (bf16[64,32,128]{2,1,0:T(8,128)(2,1)S(1)}, bf16[64,32,128]{2,1,0:T(8,128)(2,1)S(1)}, u32[]{:S(2)}, u32[]{:S(2)}) collective-permute-start(bf16[64,32,128]{2,1,0:T(8,128)(2,1)S(1)} %shard_map.53.own_ref), channel_id=1, source_target_pairs={{0,16},{16,0},{1,17},{17,1},{2,18},{18,2},{3,19},{19,3},{4,20},{20... | collective-permute-start | bytes 1572872 | tf_op jit(solution)/shard_map/ppermute | solution.py:239
  80.9 23.2 %collective-permute-done.7.other_ref = bf16[64,32,128]{2,1,0:T(8,128)(2,1)S(1)} collective-permute-done((bf16[64,32,128]{2,1,0:T(8,128)(2,1)S(1)}, bf16[64,32,128]{2,1,0:T(8,128)(2,1)S(1)}, u32[]{:S(2)}, u32[]{:S(2)}) %collective-permute-start.7) | collective-permute-done | bytes 524320 | tf_op jit(solution)/shard_map/ppermute | solution.py:239
  104.2 1.7 %shard_map.54.refs_0_ = bf16[64,32,128]{2,1,0:T(8,128)(2,1)S(1)} custom-call(s32[5]{0:T(128)S(1)} %copy-done.1, s32[640]{0:T(1024)S(1)} %reshape.8.index_ref, bf16[64,32,128]{2,1,0:T(8,128)(2,1)S(1)} %shard_map.53.own_ref, bf16[64,32,128]{2,1,0:T(8,128)(2,1)S(1)} %collective-permute-done.7.other_ref, bf16[5,16,128,128]{3,2,1,0:T(8,128)(2,1)S(1)} %bitcast.11), custom_call_target="tpu_custom_call" | custom-call | flops 939524096 | bytes 4194304 | tf_op jit(solution)/shard_map/pallas_call | solution.py:161
  105.9 0.9 shard_map.55.refs_0_
  106.7 8.4 %all-to-all-done.1 = bf16[32,6,32,128]{3,2,1,0:T(8,128)(2,1)} async-done(((bf16[32,6,32,128]{3,2,1,0:T(8,128)(2,1)}), bf16[32,6,32,128]{3,2,1,0:T(8,128)(2,1)}, u32[]{:S(2)}, u32[]{:S(2)}) %all-to-all-start.1) | async-done | bytes 1572896 | tf_op jit(solution)/shard_map/all_to_all | solution.py:235
  115.1 2.1 %shard_map.56 = bf16[256,32,128]{2,1,0:T(8,128)(2,1)} custom-call(bf16[256,32,128]{2,1,0:T(8,128)(2,1)} %shard_map.55.refs_0_, bf16[192,32,128]{2,1,0:T(8,128)(2,1)} %bitcast.3.refs_1_), custom_call_target="tpu_custom_call", output_to_operand_aliasing={{}: (0, {})} | custom-call | bytes 3145728 | tf_op jit(solution)/shard_map/pallas_call | solution.py:207
  (2 shorter events, 0.1 us)
Async XLA Ops:
  3.0 8.8 %copy-start.2 = (s32[256,5,2]{0,2,1:T(2,128)S(1)}, s32[256,5,2]{0,2,1:T(2,128)}, u32[]{:S(2)}) copy-start(s32[256,5,2]{0,2,1:T(2,128)} %param.6) | copy-start | bytes 30724
  3.0 54.3 %all-to-all-start = ((bf16[32,200,128]{2,1,0:T(8,128)(2,1)}), bf16[32,200,128]{2,1,0:T(8,128)(2,1)}, u32[]{:S(2)}, u32[]{:S(2)}) async-start(bf16[32,200,128]{2,1,0:T(8,128)(2,1)} %shard_map.49), calls=%async_computation | async-start | bytes 3276800 | tf_op jit(solution)/shard_map/all_to_all | solution.py:235
  11.5 3.9 %collective-permute-start = (bf16[64,32,128]{2,1,0:T(8,128)(2,1)S(1)}, bf16[64,32,128]{2,1,0:T(8,128)(2,1)}, u32[]{:S(2)}, u32[]{:S(2)}) collective-permute-start(bf16[64,32,128]{2,1,0:T(8,128)(2,1)S(1)} %slice.16.own_ref), channel_id=1, source_target_pairs={{0,1},{1,0},{2,3},{3,2},{4,5},{5,4},{6,7},{7,6},{8,9},{9,8},{10,11... | collective-permute-start | bytes 1572872 | tf_op jit(solution)/shard_map/ppermute | solution.py:239
  11.9 3.6 %copy-start.1 = (s32[5]{0:T(128)S(1)}, s32[5]{0:T(128)}, u32[]{:S(2)}) copy-start(s32[5]{0:T(128)} %order_ref.15) | copy-start | bytes 64
  18.3 13.4 %collective-permute-start.1 = (bf16[32,32,128]{2,1,0:T(8,128)(2,1)S(1)}, bf16[32,32,128]{2,1,0:T(8,128)(2,1)S(1)}, u32[]{:S(2)}, u32[]{:S(2)}) collective-permute-start(bf16[32,32,128]{2,1,0:T(8,128)(2,1)S(1)} %get-tuple-element.13.own_ref), channel_id=1, source_target_pairs={{0,2},{1,3},{2,0},{3,1},{4,6},{5,7},{6,4},{7,5},{8,10},{9,11},{10,... | collective-permute-start | bytes 786440 | tf_op jit(solution)/shard_map/ppermute | solution.py:239
  20.0 20.0 %collective-permute-start.3 = (bf16[32,32,128]{2,1,0:T(8,128)(2,1)S(1)}, bf16[32,32,128]{2,1,0:T(8,128)(2,1)S(1)}, u32[]{:S(2)}, u32[]{:S(2)}) collective-permute-start(bf16[32,32,128]{2,1,0:T(8,128)(2,1)S(1)} %get-tuple-element.14.own_ref), channel_id=1, source_target_pairs={{0,2},{1,3},{2,0},{3,1},{4,6},{5,7},{6,4},{7,5},{8,10},{9,11},{10,... | collective-permute-start | bytes 786440 | tf_op jit(solution)/shard_map/ppermute | solution.py:239
  32.9 14.5 %collective-permute-start.2 = (bf16[32,32,128]{2,1,0:T(8,128)(2,1)S(1)}, bf16[32,32,128]{2,1,0:T(8,128)(2,1)S(1)}, u32[]{:S(2)}, u32[]{:S(2)}) collective-permute-start(bf16[32,32,128]{2,1,0:T(8,128)(2,1)S(1)} %shard_map.47.own_ref), channel_id=1, source_target_pairs={{0,4},{1,5},{2,6},{3,7},{4,0},{5,1},{6,2},{7,3},{8,12},{9,13},{10,... | collective-permute-start | bytes 786440 | tf_op jit(solution)/shard_map/ppermute | solution.py:239
  41.2 15.0 %collective-permute-start.4 = (bf16[32,32,128]{2,1,0:T(8,128)(2,1)S(1)}, bf16[32,32,128]{2,1,0:T(8,128)(2,1)S(1)}, u32[]{:S(2)}, u32[]{:S(2)}) collective-permute-start(bf16[32,32,128]{2,1,0:T(8,128)(2,1)S(1)} %shard_map.50.own_ref), channel_id=1, source_target_pairs={{0,4},{1,5},{2,6},{3,7},{4,0},{5,1},{6,2},{7,3},{8,12},{9,13},{10,... | collective-permute-start | bytes 786440 | tf_op jit(solution)/shard_map/ppermute | solution.py:239
  48.5 23.0 %collective-permute-start.5 = (bf16[32,32,128]{2,1,0:T(8,128)(2,1)S(1)}, bf16[32,32,128]{2,1,0:T(8,128)(2,1)S(1)}, u32[]{:S(2)}, u32[]{:S(2)}) collective-permute-start(bf16[32,32,128]{2,1,0:T(8,128)(2,1)S(1)} %shard_map.48), channel_id=1, source_target_pairs={{0,8},{1,9},{2,10},{3,11},{4,12},{5,13},{6,14},{7,15},{8,0},{9,1},... | collective-permute-start | bytes 786440 | tf_op jit(solution)/shard_map/ppermute | solution.py:239
  58.2 18.3 %collective-permute-start.6 = (bf16[32,32,128]{2,1,0:T(8,128)(2,1)S(1)}, bf16[32,32,128]{2,1,0:T(8,128)(2,1)}, u32[]{:S(2)}, u32[]{:S(2)}) collective-permute-start(bf16[32,32,128]{2,1,0:T(8,128)(2,1)S(1)} %shard_map.51), channel_id=1, source_target_pairs={{0,8},{1,9},{2,10},{3,11},{4,12},{5,13},{6,14},{7,15},{8,0},{9,1},... | collective-permute-start | bytes 786440 | tf_op jit(solution)/shard_map/ppermute | solution.py:239
  70.3 1.1 copy-start
  71.5 43.6 %all-to-all-start.1 = ((bf16[32,6,32,128]{3,2,1,0:T(8,128)(2,1)}), bf16[32,6,32,128]{3,2,1,0:T(8,128)(2,1)}, u32[]{:S(2)}, u32[]{:S(2)}) async-start(bf16[32,6,32,128]{3,2,1,0:T(8,128)(2,1)} %copy-done), calls=%async_computation.1 | async-start | bytes 3145728 | tf_op jit(solution)/shard_map/all_to_all | solution.py:235
  79.2 25.0 %collective-permute-start.7 = (bf16[64,32,128]{2,1,0:T(8,128)(2,1)S(1)}, bf16[64,32,128]{2,1,0:T(8,128)(2,1)S(1)}, u32[]{:S(2)}, u32[]{:S(2)}) collective-permute-start(bf16[64,32,128]{2,1,0:T(8,128)(2,1)S(1)} %shard_map.53.own_ref), channel_id=1, source_target_pairs={{0,16},{16,0},{1,17},{17,1},{2,18},{18,2},{3,19},{19,3},{4,20},{20... | collective-permute-start | bytes 1572872 | tf_op jit(solution)/shard_map/ppermute | solution.py:239

commit v7 on v3

--- a/solution.py
+++ b/solution.py
@@ -142,24 +142,27 @@
     )(vectors, jnp.transpose(factor_index, (1, 2, 0)))
 
 
-def one_level_kernel(level, offset, order_ref, index_ref, own_ref, other_ref, table_ref, out_ref):
+def one_level_kernel(level, offset, given, order_ref, index_ref, own_ref, other_ref, table_ref, out_ref):
     levels = order_ref.shape[0]
     slot = order_ref[level]
 
     def one_block(b, carry):
         at = ((offset + b) * levels + slot) * 2
         both = jnp.concatenate([own_ref[b], other_ref[b]], axis=1)
-        coupling = jnp.concatenate([table_ref[slot, index_ref[at]], table_ref[slot, index_ref[at + 1]]], axis=0)
-        out_ref[b] = jnp.dot(both, coupling, preferred_element_type=jnp.float32).astype(jnp.bfloat16)
+        pair = [table_ref[slot, index_ref[at]], table_ref[slot, index_ref[at + 1]]]
+        coupling = jnp.concatenate(pair, axis=1 if given else 0)
+        out_ref[b] = lax.dot_general(
+            both, coupling, (((1,), (1 if given else 0,)), ((), ())), preferred_element_type=jnp.float32
+        ).astype(jnp.bfloat16)
         return carry
 
     lax.fori_loop(0, own_ref.shape[0], one_block, 0, unroll=16)
 
 
-def apply_level(own, other, table, index, order, level, offset=0, weight=1):
+def apply_level(own, other, table, index, order, level, offset=0, weight=1, given=False):
     blocks, rhs, rank = own.shape
     return pl.pallas_call(
-        functools.partial(one_level_kernel, level, offset),
+        functools.partial(one_level_kernel, level, offset, given),
         grid_spec=pltpu.PrefetchScalarGridSpec(
             num_scalar_prefetch=2,
             grid=(),
@@ -248,7 +251,8 @@
     last_middle = middle_bits - 1
     if units > far_units:
         near_index = factor_index[spread:].reshape(-1)
-        near = near_level(vectors[spread:], 0)
+        near = vectors[spread:]
+        near = apply_level(near, partner(near, 0), coupling_table, near_index, level_order, 0, given=True)
         first, second = near[:half], near[half:]
         for level in range(1, last_middle):
             first = near_level(first, level)

time: 116 us -> 116 us (level)
  starting transfers between devices: 24.4 us -> 22.8 us
    ppermute x8, starting transfers between devices: 11.5 us -> 10.1 us  [partner(): lax.ppermute(array, axis, [(i, i ^ 1 << bit) for i in range(lax.axis_size...]
    unnamed x11 -> x13, local copies, waits for them, and re-layouts: 6.04 us -> 6.03 us
  transfers between devices with their start and end apart: 10 -> 10, of which waited for: 5 -> 8; matrix products, arithmetic and copies ran while one was open for 6% -> 6% of each run, Pallas kernels for 21% -> 22%
where the time goes in v7:
time: 116 us; the launch traced here: 115 us
  waiting for transfers between devices  52.8 us (46%)
  Pallas kernels  30.2 us (26%)
  starting transfers between devices  22.8 us (20%)
  local copies, waits for them, and re-layouts  8.38 us (7%)
    ppermute x8, waiting for transfers between devices, partner(): lax.ppermute(array, axis, [(i, i ^ 1 << bit) for i in range(lax.axis_size...  44.3 us
    pallas_call x2, Pallas kernels, apply_levels(): pl.pallas_call(functools.partial(levels_kernel, some), grid_spec=pltpu.Pr...  12.8 us
    all_to_all x2, starting transfers between devices, exchange(): return lax.all_to_all(array, AXES, split_axis=0, concat_axis=0, tiled=True)  12.7 us
    pallas_call x7, Pallas kernels, apply_level(): pl.pallas_call(functools.partial(one_level_kernel, level, offset, given),...  11.3 us
    ppermute x8, starting transfers between devices, partner(): lax.ppermute(array, axis, [(i, i ^ 1 << bit) for i in range(lax.axis_size...  10.1 us
    all_to_all x2, waiting for transfers between devices, exchange(): return lax.all_to_all(array, AXES, split_axis=0, concat_axis=0, tiled=True)  8.52 us
    unnamed x13, local copies, waits for them, and re-layouts  6.03 us
    pallas_call x1, Pallas kernels, pack(): pl.pallas_call(functools.partial(pack_kernel, units), in_specs=[pl.BlockS...  3.01 us
  transfers between devices with their start and end apart: 10, of which 8 were waited for; matrix products, arithmetic and copies ran while one was open for 6% of the time, Pallas kernels for 22%

profile of v7, /device:TPU:0, one launch (start us, length us, event | category | flops | bytes accessed | tf_op | source)
XLA Modules:
  0.0 115.4 jit_solution(13042458986092578258)
XLA Ops:
  0.0 3.0 %shard_map.46 = bf16[32,200,128]{2,1,0:T(8,128)(2,1)} custom-call(bf16[256,32,128]{2,1,0:T(8,128)(2,1)} %vectors_ref.1, s32[5,2,256]{2,1,0:T(2,128)} %bitcast.16), custom_call_target="tpu_custom_call" | custom-call | bytes 4194304 | tf_op jit(solution)/shard_map/pallas_call | solution.py:134
  3.0 0.0 copy-start.5
  3.0 0.0 copy-start
  3.0 0.0 copy-start.4
  3.1 7.4 %all-to-all-start = ((bf16[32,200,128]{2,1,0:T(8,128)(2,1)}), bf16[32,200,128]{2,1,0:T(8,128)(2,1)}, u32[]{:S(2)}, u32[]{:S(2)}) async-start(bf16[32,200,128]{2,1,0:T(8,128)(2,1)} %shard_map.46), calls=%async_computation | async-start | bytes 3276800 | tf_op jit(solution)/shard_map/all_to_all | solution.py:238
  10.5 1.1 slice.17.own_ref
  11.6 0.3 collective-permute-start
  11.8 0.0 copy-done.5
  11.8 0.1 slice.16
  11.9 0.2 copy.15
  12.1 0.1 reshape.8.index_ref
  12.2 1.5 %collective-permute-done.other_ref = bf16[64,32,128]{2,1,0:T(8,128)(2,1)} collective-permute-done((bf16[64,32,128]{2,1,0:T(8,128)(2,1)S(1)}, bf16[64,32,128]{2,1,0:T(8,128)(2,1)}, u32[]{:S(2)}, u32[]{:S(2)}) %collective-permute-start) | collective-permute-done | bytes 524320 | tf_op jit(solution)/shard_map/ppermute | solution.py:242
  13.7 0.0 copy-done
  13.7 0.0 copy-done.4
  13.7 3.4 %shard_map.48 = bf16[64,32,128]{2,1,0:T(8,128)(2,1)S(1)} custom-call(s32[5]{0:T(128)S(1)} %copy-done.4, s32[640]{0:T(1024)S(1)} %reshape.8.index_ref, bf16[64,32,128]{2,1,0:T(8,128)(2,1)S(1)} %slice.17.own_ref, bf16[64,32,128]{2,1,0:T(8,128)(2,1)} %collective-permute-done.other_ref, bf16[5,16,128,128]{3,2,1,0:T(8,128)(2,1)S(1)} %copy-done), custom_call_target="tpu_custom_call" | custom-call | flops 939524096 | bytes 4194304 | tf_op jit(solution)/shard_map/pallas_call | solution.py:164
  17.2 1.8 %collective-permute-start.1 = (bf16[32,32,128]{2,1,0:T(8,128)(2,1)S(1)}, bf16[32,32,128]{2,1,0:T(8,128)(2,1)S(1)}, u32[]{:S(2)}, u32[]{:S(2)}) collective-permute-start(bf16[32,32,128]{2,1,0:T(8,128)(2,1)S(1)} %get-tuple-element.17.own_ref), channel_id=1, source_target_pairs={{0,2},{1,3},{2,0},{3,1},{4,6},{5,7},{6,4},{7,5},{8,10},{9,11},{10,... | collective-permute-start | bytes 786440 | tf_op jit(solution)/shard_map/ppermute | solution.py:242
  18.9 3.2 %copy.14 = bf16[5,16,128,128]{2,3,1,0:T(8,128)(2,1)S(1)} copy(bf16[5,16,128,128]{3,2,1,0:T(8,128)(2,1)} %table_ref.1) | data formatting | bytes 5242880 | tf_op args[1]
  22.2 0.4 collective-permute-start.3
  22.6 9.0 %collective-permute-done.1.other_ref = bf16[32,32,128]{2,1,0:T(8,128)(2,1)S(1)} collective-permute-done((bf16[32,32,128]{2,1,0:T(8,128)(2,1)S(1)}, bf16[32,32,128]{2,1,0:T(8,128)(2,1)S(1)}, u32[]{:S(2)}, u32[]{:S(2)}) %collective-permute-start.1) | collective-permute-done | bytes 262176 | tf_op jit(solution)/shard_map/ppermute | solution.py:242
  31.6 1.1 shard_map.49.own_ref
  32.7 1.1 collective-permute-start.2
  33.8 5.8 %collective-permute-done.3.other_ref = bf16[32,32,128]{2,1,0:T(8,128)(2,1)S(1)} collective-permute-done((bf16[32,32,128]{2,1,0:T(8,128)(2,1)S(1)}, bf16[32,32,128]{2,1,0:T(8,128)(2,1)S(1)}, u32[]{:S(2)}, u32[]{:S(2)}) %collective-permute-start.3) | collective-permute-done | bytes 262176 | tf_op jit(solution)/shard_map/ppermute | solution.py:242
  39.6 1.1 shard_map.51.own_ref
  40.8 2.3 %collective-permute-start.4 = (bf16[32,32,128]{2,1,0:T(8,128)(2,1)S(1)}, bf16[32,32,128]{2,1,0:T(8,128)(2,1)S(1)}, u32[]{:S(2)}, u32[]{:S(2)}) collective-permute-start(bf16[32,32,128]{2,1,0:T(8,128)(2,1)S(1)} %shard_map.51.own_ref), channel_id=1, source_target_pairs={{0,4},{1,5},{2,6},{3,7},{4,0},{5,1},{6,2},{7,3},{8,12},{9,13},{10,... | collective-permute-start | bytes 786440 | tf_op jit(solution)/shard_map/ppermute | solution.py:242
  43.0 4.4 %collective-permute-done.2.other_ref = bf16[32,32,128]{2,1,0:T(8,128)(2,1)S(1)} collective-permute-done((bf16[32,32,128]{2,1,0:T(8,128)(2,1)S(1)}, bf16[32,32,128]{2,1,0:T(8,128)(2,1)S(1)}, u32[]{:S(2)}, u32[]{:S(2)}) %collective-permute-start.2) | collective-permute-done | bytes 262176 | tf_op jit(solution)/shard_map/ppermute | solution.py:242
  47.4 1.1 shard_map.50
  48.6 2.0 %collective-permute-start.5 = (bf16[32,32,128]{2,1,0:T(8,128)(2,1)S(1)}, bf16[32,32,128]{2,1,0:T(8,128)(2,1)}, u32[]{:S(2)}, u32[]{:S(2)}) collective-permute-start(bf16[32,32,128]{2,1,0:T(8,128)(2,1)S(1)} %shard_map.50), channel_id=1, source_target_pairs={{0,8},{1,9},{2,10},{3,11},{4,12},{5,13},{6,14},{7,15},{8,0},{9,1},... | collective-permute-start | bytes 786440 | tf_op jit(solution)/shard_map/ppermute | solution.py:242
  50.6 0.1 all-to-all-done.field_ref
  50.7 0.9 slice.20
  51.6 6.2 %shard_map.47.field_ref = bf16[32,6,32,128]{3,2,1,0:T(8,128)(2,1)S(1)} custom-call(s32[5]{0:T(128)S(1)} %copy-done.4, s32[32,128]{1,0:T(8,128)S(1)} %fusion.index_ref, bf16[32,200,128]{2,1,0:T(8,128)(2,1)} %all-to-all-done.field_ref, bf16[5,16,128,128]{3,2,1,0:T(8,128)(2,1)S(1)} %bitcast.11), custom_call_target="tpu_custom_call" | custom-call | flops 805306368 | bytes 5767168 | tf_op jit(solution)/shard_map/pallas_call | solution.py:60
  57.8 0.0 collective-permute-done.4.other_ref
  57.8 0.0 copy-start.2
  57.8 0.7 copy-done.2
  58.5 0.0 copy-start.3
  58.5 0.9 copy-done.3
  59.4 1.1 shard_map.52
  60.6 0.9 collective-permute-start.6
  61.5 6.7 %shard_map.53 = bf16[32,6,32,128]{3,2,1,0:T(8,128)(2,1)S(1)} custom-call(s32[5]{0:T(128)S(1)} %copy-done.4, s32[32,128]{1,0:T(8,128)S(1)} %fusion.index_ref, bf16[32,6,32,128]{3,2,1,0:T(8,128)(2,1)S(1)} %shard_map.47.field_ref, bf16[5,16,128,128]{3,2,1,0:T(8,128)(2,1)S(1)} %bitcast.13), custom_call_target="tpu_custom_call" | custom-call | flops 1207959552 | bytes 5767168 | tf_op jit(solution)/shard_map/pallas_call | solution.py:60
  68.2 0.0 copy-start.1
  68.2 1.1 copy-done.1
  69.3 0.0 collective-permute-done.5
  69.3 5.3 %all-to-all-start.1 = ((bf16[32,6,32,128]{3,2,1,0:T(8,128)(2,1)}), bf16[32,6,32,128]{3,2,1,0:T(8,128)(2,1)}, u32[]{:S(2)}, u32[]{:S(2)}) async-start(bf16[32,6,32,128]{3,2,1,0:T(8,128)(2,1)} %copy-done.1), calls=%async_computation.1 | async-start | bytes 3145728 | tf_op jit(solution)/shard_map/all_to_all | solution.py:238
  74.6 0.3 collective-permute-done.6
  75.0 1.0 pad_maximum_fusion.1.other_ref
  76.0 1.7 %shard_map.54.own_ref = bf16[64,32,128]{2,1,0:T(8,128)(2,1)S(1)} custom-call(s32[5]{0:T(128)S(1)} %copy-done.4, s32[640]{0:T(1024)S(1)} %reshape.8.index_ref, bf16[64,32,128]{2,1,0:T(8,128)(2,1)S(1)} %pad_maximum_fusion.own_ref, bf16[64,32,128]{2,1,0:T(8,128)(2,1)S(1)} %pad_maximum_fusion.1.other_ref, bf16[5,16,128,128]{3,2,1,0:T(8,128)(2,1)S(1)} %bitcast.14), custom_call_target="tpu_custom_call" | custom-call | flops 46976204800 | bytes 4194304 | tf_op jit(solution)/shard_map/pallas_call | solution.py:164
  77.7 1.4 %collective-permute-start.7 = (bf16[64,32,128]{2,1,0:T(8,128)(2,1)S(1)}, bf16[64,32,128]{2,1,0:T(8,128)(2,1)S(1)}, u32[]{:S(2)}, u32[]{:S(2)}) collective-permute-start(bf16[64,32,128]{2,1,0:T(8,128)(2,1)S(1)} %shard_map.54.own_ref), channel_id=1, source_target_pairs={{0,16},{16,0},{1,17},{17,1},{2,18},{18,2},{3,19},{19,3},{4,20},{20... | collective-permute-start | bytes 1572872 | tf_op jit(solution)/shard_map/ppermute | solution.py:242
  79.1 23.2 %collective-permute-done.7.other_ref = bf16[64,32,128]{2,1,0:T(8,128)(2,1)S(1)} collective-permute-done((bf16[64,32,128]{2,1,0:T(8,128)(2,1)S(1)}, bf16[64,32,128]{2,1,0:T(8,128)(2,1)S(1)}, u32[]{:S(2)}, u32[]{:S(2)}) %collective-permute-start.7) | collective-permute-done | bytes 524320 | tf_op jit(solution)/shard_map/ppermute | solution.py:242
  102.3 1.7 %shard_map.55.refs_0_ = bf16[64,32,128]{2,1,0:T(8,128)(2,1)S(1)} custom-call(s32[5]{0:T(128)S(1)} %copy-done.4, s32[640]{0:T(1024)S(1)} %reshape.8.index_ref, bf16[64,32,128]{2,1,0:T(8,128)(2,1)S(1)} %shard_map.54.own_ref, bf16[64,32,128]{2,1,0:T(8,128)(2,1)S(1)} %collective-permute-done.7.other_ref, bf16[5,16,128,128]{3,2,1,0:T(8,128)(2,1)S(1)} %bitcast.15), custom_call_target="tpu_custom_call" | custom-call | flops 939524096 | bytes 4194304 | tf_op jit(solution)/shard_map/pallas_call | solution.py:164
  104.0 0.9 shard_map.56.refs_0_
  104.9 8.4 %all-to-all-done.1 = bf16[32,6,32,128]{3,2,1,0:T(8,128)(2,1)} async-done(((bf16[32,6,32,128]{3,2,1,0:T(8,128)(2,1)}), bf16[32,6,32,128]{3,2,1,0:T(8,128)(2,1)}, u32[]{:S(2)}, u32[]{:S(2)}) %all-to-all-start.1) | async-done | bytes 1572896 | tf_op jit(solution)/shard_map/all_to_all | solution.py:238
  113.3 2.1 %shard_map.57 = bf16[256,32,128]{2,1,0:T(8,128)(2,1)} custom-call(bf16[256,32,128]{2,1,0:T(8,128)(2,1)} %shard_map.56.refs_0_, bf16[192,32,128]{2,1,0:T(8,128)(2,1)} %bitcast.4.refs_1_), custom_call_target="tpu_custom_call", output_to_operand_aliasing={{}: (0, {})} | custom-call | bytes 3145728 | tf_op jit(solution)/shard_map/pallas_call | solution.py:210
  (3 shorter events, 0.1 us)
Async XLA Ops:
  3.0 8.8 %copy-start.5 = (s32[256,5,2]{0,2,1:T(2,128)S(1)}, s32[256,5,2]{0,2,1:T(2,128)}, u32[]{:S(2)}) copy-start(s32[256,5,2]{0,2,1:T(2,128)} %param.6) | copy-start | bytes 30724
  3.0 10.6 %copy-start = (bf16[5,16,128,128]{3,2,1,0:T(8,128)(2,1)S(1)}, bf16[5,16,128,128]{3,2,1,0:T(8,128)(2,1)}, u32[]{:S(2)}) copy-start(bf16[5,16,128,128]{3,2,1,0:T(8,128)(2,1)} %table_ref.1) | copy-start | bytes 7864324
  3.0 10.6 %copy-start.4 = (s32[5]{0:T(128)S(1)}, s32[5]{0:T(128)}, u32[]{:S(2)}) copy-start(s32[5]{0:T(128)} %order_ref.17) | copy-start | bytes 64
  3.1 47.7 %all-to-all-start = ((bf16[32,200,128]{2,1,0:T(8,128)(2,1)}), bf16[32,200,128]{2,1,0:T(8,128)(2,1)}, u32[]{:S(2)}, u32[]{:S(2)}) async-start(bf16[32,200,128]{2,1,0:T(8,128)(2,1)} %shard_map.46), calls=%async_computation | async-start | bytes 3276800 | tf_op jit(solution)/shard_map/all_to_all | solution.py:238
  11.6 2.1 %collective-permute-start = (bf16[64,32,128]{2,1,0:T(8,128)(2,1)S(1)}, bf16[64,32,128]{2,1,0:T(8,128)(2,1)}, u32[]{:S(2)}, u32[]{:S(2)}) collective-permute-start(bf16[64,32,128]{2,1,0:T(8,128)(2,1)S(1)} %slice.17.own_ref), channel_id=1, source_target_pairs={{0,1},{1,0},{2,3},{3,2},{4,5},{5,4},{6,7},{7,6},{8,9},{9,8},{10,11... | collective-permute-start | bytes 1572872 | tf_op jit(solution)/shard_map/ppermute | solution.py:242
  17.2 14.4 %collective-permute-start.1 = (bf16[32,32,128]{2,1,0:T(8,128)(2,1)S(1)}, bf16[32,32,128]{2,1,0:T(8,128)(2,1)S(1)}, u32[]{:S(2)}, u32[]{:S(2)}) collective-permute-start(bf16[32,32,128]{2,1,0:T(8,128)(2,1)S(1)} %get-tuple-element.17.own_ref), channel_id=1, source_target_pairs={{0,2},{1,3},{2,0},{3,1},{4,6},{5,7},{6,4},{7,5},{8,10},{9,11},{10,... | collective-permute-start | bytes 786440 | tf_op jit(solution)/shard_map/ppermute | solution.py:242
  22.2 17.4 %collective-permute-start.3 = (bf16[32,32,128]{2,1,0:T(8,128)(2,1)S(1)}, bf16[32,32,128]{2,1,0:T(8,128)(2,1)S(1)}, u32[]{:S(2)}, u32[]{:S(2)}) collective-permute-start(bf16[32,32,128]{2,1,0:T(8,128)(2,1)S(1)} %get-tuple-element.18.own_ref), channel_id=1, source_target_pairs={{0,2},{1,3},{2,0},{3,1},{4,6},{5,7},{6,4},{7,5},{8,10},{9,11},{10,... | collective-permute-start | bytes 786440 | tf_op jit(solution)/shard_map/ppermute | solution.py:242
  32.7 14.7 %collective-permute-start.2 = (bf16[32,32,128]{2,1,0:T(8,128)(2,1)S(1)}, bf16[32,32,128]{2,1,0:T(8,128)(2,1)S(1)}, u32[]{:S(2)}, u32[]{:S(2)}) collective-permute-start(bf16[32,32,128]{2,1,0:T(8,128)(2,1)S(1)} %shard_map.49.own_ref), channel_id=1, source_target_pairs={{0,4},{1,5},{2,6},{3,7},{4,0},{5,1},{6,2},{7,3},{8,12},{9,13},{10,... | collective-permute-start | bytes 786440 | tf_op jit(solution)/shard_map/ppermute | solution.py:242
  40.8 17.0 %collective-permute-start.4 = (bf16[32,32,128]{2,1,0:T(8,128)(2,1)S(1)}, bf16[32,32,128]{2,1,0:T(8,128)(2,1)S(1)}, u32[]{:S(2)}, u32[]{:S(2)}) collective-permute-start(bf16[32,32,128]{2,1,0:T(8,128)(2,1)S(1)} %shard_map.51.own_ref), channel_id=1, source_target_pairs={{0,4},{1,5},{2,6},{3,7},{4,0},{5,1},{6,2},{7,3},{8,12},{9,13},{10,... | collective-permute-start | bytes 786440 | tf_op jit(solution)/shard_map/ppermute | solution.py:242
  48.6 20.7 %collective-permute-start.5 = (bf16[32,32,128]{2,1,0:T(8,128)(2,1)S(1)}, bf16[32,32,128]{2,1,0:T(8,128)(2,1)}, u32[]{:S(2)}, u32[]{:S(2)}) collective-permute-start(bf16[32,32,128]{2,1,0:T(8,128)(2,1)S(1)} %shard_map.50), channel_id=1, source_target_pairs={{0,8},{1,9},{2,10},{3,11},{4,12},{5,13},{6,14},{7,15},{8,0},{9,1},... | collective-permute-start | bytes 786440 | tf_op jit(solution)/shard_map/ppermute | solution.py:242
  57.8 0.7 copy-start.2
  58.5 0.9 copy-start.3
  60.6 14.4 %collective-permute-start.6 = (bf16[32,32,128]{2,1,0:T(8,128)(2,1)S(1)}, bf16[32,32,128]{2,1,0:T(8,128)(2,1)S(1)}, u32[]{:S(2)}, u32[]{:S(2)}) collective-permute-start(bf16[32,32,128]{2,1,0:T(8,128)(2,1)S(1)} %shard_map.52), channel_id=1, source_target_pairs={{0,8},{1,9},{2,10},{3,11},{4,12},{5,13},{6,14},{7,15},{8,0},{9,1},... | collective-permute-start | bytes 786440 | tf_op jit(solution)/shard_map/ppermute | solution.py:242
  68.2 1.1 copy-start.1
  69.3 44.0 %all-to-all-start.1 = ((bf16[32,6,32,128]{3,2,1,0:T(8,128)(2,1)}), bf16[32,6,32,128]{3,2,1,0:T(8,128)(2,1)}, u32[]{:S(2)}, u32[]{:S(2)}) async-start(bf16[32,6,32,128]{3,2,1,0:T(8,128)(2,1)} %copy-done.1), calls=%async_computation.1 | async-start | bytes 3145728 | tf_op jit(solution)/shard_map/all_to_all | solution.py:238
  77.7 24.7 %collective-permute-start.7 = (bf16[64,32,128]{2,1,0:T(8,128)(2,1)S(1)}, bf16[64,32,128]{2,1,0:T(8,128)(2,1)S(1)}, u32[]{:S(2)}, u32[]{:S(2)}) collective-permute-start(bf16[64,32,128]{2,1,0:T(8,128)(2,1)S(1)} %shard_map.54.own_ref), channel_id=1, source_target_pairs={{0,16},{16,0},{1,17},{17,1},{2,18},{18,2},{3,19},{19,3},{4,20},{20... | collective-permute-start | bytes 1572872 | tf_op jit(solution)/shard_map/ppermute | solution.py:242
